TPU v7x, 128 devices: a whole 4x4x4 slice. The times are simulated.
128 devices in a mesh: ctx: 32 (over y_lo, x, z), fsdp: 4 (over y_hi, core).
Axes of the slice: x: 4, y: 4 (y_hi: 2, y_lo: 2; y = y_hi * 2 + y_lo), z: 4, core: 2. Of those that a mesh axis runs over, the one named last changes fastest.
Arguments:
- tokens: bfloat16 [4, 6144, 896], P('fsdp', 'ctx'), may hold values from -6 to 6
- block_order: int32 [64], replicated, may hold values from 0 to 63, each once
- query_weight: bfloat16 [896, 896], P('fsdp'), may hold values from -0.1875 to 0.1875
- key_weight: bfloat16 [896, 128], P('fsdp'), may hold values from -0.1875 to 0.1875
- value_weight: bfloat16 [896, 128], P('fsdp'), may hold values from -0.1875 to 0.1875
- output_weight: bfloat16 [896, 896], P('fsdp'), may hold values from -0.5 to 0.5
- gate_weight: bfloat16 [896, 4864], P('fsdp'), may hold values from -0.1875 to 0.1875
- up_weight: bfloat16 [896, 4864], P('fsdp'), may hold values from -0.1875 to 0.1875
- down_weight: bfloat16 [4864, 896], P('fsdp'), may hold values from -0.078125 to 0.078125
- query_bias: bfloat16 [896], P('fsdp'), may hold values from -3 to 3
- key_bias: bfloat16 [128], P('fsdp'), may hold values from -3 to 3
- value_bias: bfloat16 [128], P('fsdp'), may hold values from -3 to 3
- attention_gain: bfloat16 [896], P('fsdp'), may hold values from 0.099609375 to 1.8984375
- hidden_gain: bfloat16 [896], P('fsdp'), may hold values from 0.099609375 to 1.8984375
- cotangent: bfloat16 [4, 6144, 896], P('fsdp', 'ctx'), may hold values from -6 to 6
Outputs:
- output: bfloat16 [4, 6144, 896], P('fsdp', 'ctx')
- token_grad: float32 [4, 6144, 896], P('fsdp', 'ctx')
- query_weight_grad: float32 [896, 896], P('fsdp')
- key_weight_grad: float32 [896, 128], P('fsdp')
- value_weight_grad: float32 [896, 128], P('fsdp')
- output_weight_grad: float32 [896, 896], P('fsdp')
- gate_weight_grad: float32 [896, 4864], P('fsdp')
- up_weight_grad: float32 [896, 4864], P('fsdp')
- down_weight_grad: float32 [4864, 896], P('fsdp')
- query_bias_grad: float32 [896], P('fsdp')
- key_bias_grad: float32 [128], P('fsdp')
- value_bias_grad: float32 [128], P('fsdp')
- attention_gain_grad: float32 [896], P('fsdp')
- hidden_gain_grad: float32 [896], P('fsdp')
Inputs may be any that keep to these rules, and one draw needn't show every extreme that they name: `block_order`: a permutation; index ctx device i holds layout blocks 2i and 2i + 1 of 96 tokens each.
All inputs are finite; a program needn't handle non-finite values.
Results may differ from a plain program's by a relative error of at most 0.02.
Values may be sent and summed in bfloat16 or wider, within the bound.
A program may use at most 256 MiB of HBM per device.

v0:
```python
import math

import jax
import jax.numpy as jnp
from jax import lax
from jax.sharding import PartitionSpec as P

H = 14
KVH = 2
HD = 64


EPSILON = 1e-06
THETA = 1000000.0
MASKED = -1e30


def product(left, right):
    return jnp.dot(left, right, preferred_element_type=jnp.float32)


def by_transpose(left, right):
    return lax.dot_general(
        left, right, (((1,), (1,)), ((), ())), preferred_element_type=jnp.float32
    )


def over_rows(left, right):
    return lax.dot_general(
        left, right, (((0,), (0,)), ((), ())), preferred_element_type=jnp.float32
    )


def rotary(values, positions, direction):
    half_width = HD // 2
    frequency = jnp.exp(jnp.arange(half_width, dtype=jnp.float32) * (-2.0 * math.log(THETA) / HD))
    angles = positions.astype(jnp.float32)[:, None] * frequency[None, :]
    cosine = jnp.cos(angles)[:, None, :]
    sine_table = direction * jnp.sin(angles)[:, None, :]
    front_half = values[..., :half_width]
    back_half = values[..., half_width:]
    return jnp.concatenate(
        [
            front_half * cosine - back_half * sine_table,
            back_half * cosine + front_half * sine_table,
        ],
        axis=-1,
    )


def layout_positions(block_order, seq_count, block_len):
    layout_rows = jnp.arange(seq_count, dtype=jnp.int32)
    block_ids = jnp.arange(block_order.shape[0], dtype=jnp.int32)
    block_start = jnp.sum(
        jnp.where(
            (layout_rows // block_len)[:, None] == block_ids[None, :], block_order[None, :], 0
        ),
        axis=1,
    )
    return block_start * block_len + layout_rows % block_len


def masked_scores(query_part, key_part, key_pos, own_pos, score_scale):
    scores = (
        jnp.einsum("tgd,sd->gts", query_part, key_part, preferred_element_type=jnp.float32)
        * score_scale
    )
    allowed = (key_pos[None, :] <= own_pos[:, None])[None]
    return jnp.where(allowed, scores, MASKED)


def key_split(all_keys, all_values, positions):
    seq_total = all_keys.shape[0]
    span = min(512, seq_total)
    count = seq_total // span
    return (
        all_keys.reshape(count, span, KVH, HD),
        all_values.reshape(count, span, KVH, HD),
        positions.reshape(count, span),
        span,
    )


def attention_forward(query_rot, all_keys, all_values, positions, own_pos, score_scale):
    local_rows = query_rot.shape[0]
    groups = H // KVH
    grouped = query_rot.reshape(local_rows, KVH, groups, HD)
    key_blocks, value_blocks, pos_blocks, span = key_split(all_keys, all_values, positions)
    mixed_list = []
    lse_list = []
    for head_group in range(KVH):
        query_part = grouped[:, head_group]

        def stats(carry, block):
            run_max, run_total = carry
            key_block, pos_block = block
            scores = masked_scores(query_part, key_block, pos_block, own_pos, score_scale)
            new_max = jnp.maximum(run_max, jnp.max(scores, axis=-1, keepdims=True))
            run_total = run_total * jnp.exp(run_max - new_max) + jnp.sum(
                jnp.exp(scores - new_max), axis=-1, keepdims=True
            )
            return ((new_max, run_total), None)

        start = (
            jnp.full((groups, local_rows, 1), MASKED, jnp.float32),
            jnp.zeros((groups, local_rows, 1), jnp.float32),
        )
        (row_max, row_total), _ = lax.scan(stats, start, (key_blocks[:, :, head_group], pos_blocks))
        lse = row_max + jnp.log(row_total)

        def mix(total, block):
            key_block, value_block, pos_block = block
            scores = masked_scores(query_part, key_block, pos_block, own_pos, score_scale)
            weights = jnp.exp(scores - lse).astype(jnp.bfloat16)
            return (
                total
                + jnp.einsum(
                    "gts,sd->tgd", weights, value_block, preferred_element_type=jnp.float32
                ),
                None,
            )

        mixed, _ = lax.scan(
            mix,
            jnp.zeros((local_rows, groups, HD), jnp.float32),
            (key_blocks[:, :, head_group], value_blocks[:, :, head_group], pos_blocks),
        )
        mixed_list.append(mixed)
        lse_list.append(lse)
    return (jnp.stack(mixed_list, axis=1).reshape(local_rows, H * HD), lse_list)


def attention_backward(
    query_rot, all_keys, all_values, grad_attended, lse_list, positions, own_pos, score_scale
):
    local_rows = query_rot.shape[0]
    groups = H // KVH
    seq_total = all_keys.shape[0]
    grouped = query_rot.reshape(local_rows, KVH, groups, HD)
    grad_grouped = grad_attended.reshape(local_rows, KVH, groups, HD)
    key_blocks, value_blocks, pos_blocks, span = key_split(all_keys, all_values, positions)
    query_list = []
    key_list = []
    value_list = []
    for head_group in range(KVH):
        query_part = grouped[:, head_group]
        grad_part = grad_grouped[:, head_group]
        lse = lse_list[head_group]

        def inner(total, block):
            key_block, value_block, pos_block = block
            scores = masked_scores(query_part, key_block, pos_block, own_pos, score_scale)
            probabilities = jnp.exp(scores - lse)
            grad_probs = jnp.einsum(
                "tgd,sd->gts", grad_part, value_block, preferred_element_type=jnp.float32
            )
            return (total + jnp.sum(probabilities * grad_probs, axis=-1, keepdims=True), None)

        blocks = (key_blocks[:, :, head_group], value_blocks[:, :, head_group], pos_blocks)
        row_inner, _ = lax.scan(inner, jnp.zeros((groups, local_rows, 1), jnp.float32), blocks)

        def grads(total, block):
            key_block, value_block, pos_block = block
            scores = masked_scores(query_part, key_block, pos_block, own_pos, score_scale)
            probabilities = jnp.exp(scores - lse)
            grad_probs = jnp.einsum(
                "tgd,sd->gts", grad_part, value_block, preferred_element_type=jnp.float32
            )
            grad_scores = (probabilities * (grad_probs - row_inner)).astype(jnp.bfloat16)
            total = (
                total
                + jnp.einsum(
                    "gts,sd->tgd", grad_scores, key_block, preferred_element_type=jnp.float32
                )
                * score_scale
            )
            key_part = (
                jnp.einsum(
                    "gts,tgd->sd", grad_scores, query_part, preferred_element_type=jnp.float32
                )
                * score_scale
            )
            value_part = jnp.einsum(
                "gts,tgd->sd",
                probabilities.astype(jnp.bfloat16),
                grad_part,
                preferred_element_type=jnp.float32,
            )
            return (total, (key_part, value_part))

        grad_query, (key_parts, value_parts) = lax.scan(
            grads, jnp.zeros((local_rows, groups, HD), jnp.float32), blocks
        )
        query_list.append(grad_query)
        key_list.append(key_parts.reshape(seq_total, HD))
        value_list.append(value_parts.reshape(seq_total, HD))
    grad_query_rot = jnp.stack(query_list, axis=1).reshape(local_rows, H, HD)
    grad_key_parts = jnp.stack(key_list, axis=1).reshape(-1, KVH * HD)
    grad_value_parts = jnp.stack(value_list, axis=1).reshape(-1, KVH * HD)
    return (grad_query_rot, grad_key_parts, grad_value_parts)


def body(
    tokens,
    block_order,
    query_weight,
    key_weight,
    value_weight,
    output_weight,
    gate_weight,
    up_weight,
    down_weight,
    query_bias,
    key_bias,
    value_bias,
    attention_gain,
    hidden_gain,
    cotangent,
):
    local_rows = tokens.shape[1]
    seq_total = local_rows * lax.axis_size("ctx")
    score_scale = 1.0 / math.sqrt(HD)
    positions = layout_positions(block_order, seq_total, local_rows // 2)
    own_pos = lax.dynamic_slice_in_dim(positions, lax.axis_index("ctx") * local_rows, local_rows)
    attention_set = (
        lax.all_gather(query_weight, "fsdp", axis=0, tiled=True),
        lax.all_gather(key_weight, "fsdp", axis=0, tiled=True),
        lax.all_gather(value_weight, "fsdp", axis=0, tiled=True),
        lax.all_gather(output_weight, "fsdp", axis=0, tiled=True),
        lax.all_gather(query_bias, "fsdp", axis=0, tiled=True),
        lax.all_gather(key_bias, "fsdp", axis=0, tiled=True),
        lax.all_gather(value_bias, "fsdp", axis=0, tiled=True),
        lax.all_gather(attention_gain, "fsdp", axis=0, tiled=True),
    )
    hidden_set = (
        lax.all_gather(gate_weight, "fsdp", axis=0, tiled=True),
        lax.all_gather(up_weight, "fsdp", axis=0, tiled=True),
        lax.all_gather(down_weight, "fsdp", axis=0, tiled=True),
        lax.all_gather(hidden_gain, "fsdp", axis=0, tiled=True),
    )
    inputs = tokens[0].astype(jnp.float32)
    first_scale = lax.rsqrt(jnp.mean(inputs * inputs, axis=-1, keepdims=True) + EPSILON)
    first_gain = attention_set[7].astype(jnp.float32)
    normed = (inputs * first_scale * first_gain).astype(jnp.bfloat16)
    queries = product(normed, attention_set[0]) + attention_set[4].astype(jnp.float32)
    key_pre = product(normed, attention_set[1]) + attention_set[5].astype(jnp.float32)
    value_pre = product(normed, attention_set[2]) + attention_set[6].astype(jnp.float32)
    query_rot = rotary(queries.reshape(local_rows, H, HD), own_pos, 1.0).astype(jnp.bfloat16)
    key_rot = (
        rotary(key_pre.reshape(local_rows, KVH, HD), own_pos, 1.0)
        .astype(jnp.bfloat16)
        .reshape(local_rows, KVH * HD)
    )
    value_low = value_pre.astype(jnp.bfloat16)
    all_keys, all_values = (
        lax.all_gather(key_rot, "ctx", axis=0, tiled=True),
        lax.all_gather(value_low, "ctx", axis=0, tiled=True),
    )
    attended, lse_list = attention_forward(
        query_rot, all_keys, all_values, positions, own_pos, score_scale
    )
    attended = attended.astype(jnp.bfloat16)
    middle = inputs + product(attended, attention_set[3])
    second_scale = lax.rsqrt(jnp.mean(middle * middle, axis=-1, keepdims=True) + EPSILON)
    second_gain = hidden_set[3].astype(jnp.float32)
    normed_two = (middle * second_scale * second_gain).astype(jnp.bfloat16)
    gate_pre = product(normed_two, hidden_set[0])
    upward = product(normed_two, hidden_set[1])
    gate_sigmoid = jax.nn.sigmoid(gate_pre)
    swish = gate_pre * gate_sigmoid
    hidden = (swish * upward).astype(jnp.bfloat16)
    output = middle + product(hidden, hidden_set[2])
    attention_set = (
        lax.all_gather(query_weight, "fsdp", axis=0, tiled=True),
        lax.all_gather(key_weight, "fsdp", axis=0, tiled=True),
        lax.all_gather(value_weight, "fsdp", axis=0, tiled=True),
        lax.all_gather(output_weight, "fsdp", axis=0, tiled=True),
        lax.all_gather(query_bias, "fsdp", axis=0, tiled=True),
        lax.all_gather(key_bias, "fsdp", axis=0, tiled=True),
        lax.all_gather(value_bias, "fsdp", axis=0, tiled=True),
        lax.all_gather(attention_gain, "fsdp", axis=0, tiled=True),
    )
    hidden_set = (
        lax.all_gather(gate_weight, "fsdp", axis=0, tiled=True),
        lax.all_gather(up_weight, "fsdp", axis=0, tiled=True),
        lax.all_gather(down_weight, "fsdp", axis=0, tiled=True),
        lax.all_gather(hidden_gain, "fsdp", axis=0, tiled=True),
    )
    all_keys, all_values = (
        lax.all_gather(key_rot, "ctx", axis=0, tiled=True),
        lax.all_gather(value_low, "ctx", axis=0, tiled=True),
    )
    grad_out = cotangent[0].astype(jnp.float32)
    grad_low = grad_out.astype(jnp.bfloat16)
    grad_hidden = by_transpose(grad_low, hidden_set[2])
    grad_gate = (
        grad_hidden * upward * gate_sigmoid * (1.0 + gate_pre * (1.0 - gate_sigmoid))
    ).astype(jnp.bfloat16)
    grad_up = (grad_hidden * swish).astype(jnp.bfloat16)
    grad_two = by_transpose(grad_gate, hidden_set[0]) + by_transpose(grad_up, hidden_set[1])
    hidden_gain_part = jnp.sum(grad_two * middle * second_scale, axis=0)
    weighted_two = grad_two * second_gain
    grad_middle = (
        grad_out
        + second_scale * weighted_two
        - middle
        * (second_scale * second_scale * second_scale)
        * jnp.mean(weighted_two * middle, axis=-1, keepdims=True)
    )
    grad_attn = grad_middle.astype(jnp.bfloat16)
    grad_attended = by_transpose(grad_attn, attention_set[3]).astype(jnp.bfloat16)
    grad_query_rot, grad_key_parts, grad_value_parts = attention_backward(
        query_rot, all_keys, all_values, grad_attended, lse_list, positions, own_pos, score_scale
    )
    grad_key_rot, grad_value_sum = (
        lax.psum_scatter(grad_key_parts, "ctx", scatter_dimension=0, tiled=True),
        lax.psum_scatter(grad_value_parts, "ctx", scatter_dimension=0, tiled=True),
    )
    grad_queries = (
        rotary(grad_query_rot, own_pos, -1.0).astype(jnp.bfloat16).reshape(local_rows, H * HD)
    )
    grad_keys = (
        rotary(grad_key_rot.reshape(local_rows, KVH, HD), own_pos, -1.0)
        .astype(jnp.bfloat16)
        .reshape(local_rows, KVH * HD)
    )
    grad_values = grad_value_sum.astype(jnp.bfloat16)
    grad_normed = (
        by_transpose(grad_queries, attention_set[0])
        + by_transpose(grad_keys, attention_set[1])
        + by_transpose(grad_values, attention_set[2])
    )
    attention_gain_part = jnp.sum(grad_normed * inputs * first_scale, axis=0)
    weighted_one = grad_normed * first_gain
    grad_inputs = (
        grad_middle
        + first_scale * weighted_one
        - inputs
        * (first_scale * first_scale * first_scale)
        * jnp.mean(weighted_one * inputs, axis=-1, keepdims=True)
    )
    partials = (
        over_rows(normed, grad_queries),
        over_rows(normed, grad_keys),
        over_rows(normed, grad_values),
        over_rows(attended, grad_attn),
        over_rows(normed_two, grad_gate),
        over_rows(normed_two, grad_up),
        over_rows(hidden, grad_low),
        jnp.sum(grad_queries.astype(jnp.float32), axis=0),
        jnp.sum(grad_keys.astype(jnp.float32), axis=0),
        jnp.sum(grad_values.astype(jnp.float32), axis=0),
        attention_gain_part,
        hidden_gain_part,
    )
    shares = (
        lax.psum_scatter(partials[0], "fsdp", scatter_dimension=0, tiled=True),
        lax.psum_scatter(partials[1], "fsdp", scatter_dimension=0, tiled=True),
        lax.psum_scatter(partials[2], "fsdp", scatter_dimension=0, tiled=True),
        lax.psum_scatter(partials[3], "fsdp", scatter_dimension=0, tiled=True),
        lax.psum_scatter(partials[4], "fsdp", scatter_dimension=0, tiled=True),
        lax.psum_scatter(partials[5], "fsdp", scatter_dimension=0, tiled=True),
        lax.psum_scatter(partials[6], "fsdp", scatter_dimension=0, tiled=True),
        lax.psum_scatter(partials[7], "fsdp", scatter_dimension=0, tiled=True),
        lax.psum_scatter(partials[8], "fsdp", scatter_dimension=0, tiled=True),
        lax.psum_scatter(partials[9], "fsdp", scatter_dimension=0, tiled=True),
        lax.psum_scatter(partials[10], "fsdp", scatter_dimension=0, tiled=True),
        lax.psum_scatter(partials[11], "fsdp", scatter_dimension=0, tiled=True),
    )
    totals = lax.psum(
        (
            shares[0],
            shares[1],
            shares[2],
            shares[3],
            shares[4],
            shares[5],
            shares[6],
            shares[7],
            shares[8],
            shares[9],
            shares[10],
            shares[11],
        ),
        "ctx",
    )
    return (
        output.astype(jnp.bfloat16)[None],
        grad_inputs[None],
        totals[0],
        totals[1],
        totals[2],
        totals[3],
        totals[4],
        totals[5],
        totals[6],
        totals[7],
        totals[8],
        totals[9],
        totals[10],
        totals[11],
    )


def solution(mesh):
    placed = (
        P("fsdp", "ctx", None),
        P(),
        P("fsdp", None),
        P("fsdp", None),
        P("fsdp", None),
        P("fsdp", None),
        P("fsdp", None),
        P("fsdp", None),
        P("fsdp", None),
        P("fsdp"),
        P("fsdp"),
        P("fsdp"),
        P("fsdp"),
        P("fsdp"),
        P("fsdp", "ctx", None),
    )
    return jax.shard_map(
        body,
        mesh=mesh,
        in_specs=placed,
        out_specs=(
            P("fsdp", "ctx", None),
            P("fsdp", "ctx", None),
            P("fsdp", None),
            P("fsdp", None),
            P("fsdp", None),
            P("fsdp", None),
            P("fsdp", None),
            P("fsdp", None),
            P("fsdp", None),
            P("fsdp"),
            P("fsdp"),
            P("fsdp"),
            P("fsdp"),
            P("fsdp"),
        ),
        check_vma=False,
    )
```

profile of v0, /device:TPU:8, one launch (start us, length us, event | category | flops | bytes accessed | tf_op | source)
XLA Modules:
  0.0 2466.6 jit_solution(3748625617935260480)
XLA Ops:
  54.6 137.8 %all-gather.10.cloned.1.call-done = bf16[6144,128]{1,0:T(8,128)(2,1)} async-done(((bf16[192,128]{1,0:T(8,128)(2,1)}), bf16[6144,128]{1,0:T(8,128)(2,1)}) %all-gather.10.cloned.1.call-update) | async-done | bytes 1572880 | tf_op jit(solution)/shard_map/all_gather | solution.py:256
  200.3 49.2 %while.100 = (s32[]{:T(128)}, f32[7,192,1]{1,0,2:T(8,128)S(1)}, f32[7,192,1]{1,0,2:T(8,128)S(1)}, s32[12,512]{1,0:T(8,128)}, s32[192]{0:T(256)}, /*index=5*/bf16...) while((s32[]{:T(128)}, f32[7,192,1]{1,0,2:T(8,128)S(1)}, ...), condition=%wide.region_5.6_spmd.clone, body=%wide.region_2.5_spmd.clone.sunk | while | flops 93002304 | bytes 6114924 | solution.py:108
  249.6 97.7 %all-gather.8.cloned.1.call-done = bf16[6144,128]{1,0:T(8,128)(2,1)} async-done(((bf16[192,128]{1,0:T(8,128)(2,1)}), bf16[6144,128]{1,0:T(8,128)(2,1)}) %all-gather.8.cloned.1.call-update) | async-done | bytes 1572880 | tf_op jit(solution)/shard_map/all_gather | solution.py:257
  356.5 49.3 %while.102 = (s32[]{:T(128)}, f32[7,192,1]{1,0,2:T(8,128)S(1)}, f32[7,192,1]{1,0,2:T(8,128)S(1)}, s32[12,512]{1,0:T(8,128)}, s32[192]{0:T(256)}, /*index=5*/bf16...) while((s32[]{:T(128)}, f32[7,192,1]{1,0,2:T(8,128)S(1)}, ...), condition=%wide.region_11.12_spmd.clone, body=%wide.region_8.11_spmd.clone.sunk | while | flops 93002304 | bytes 6114924 | solution.py:108
  405.9 55.9 %while.101 = (s32[]{:T(128)}, f32[192,7,64]{0,2,1:T(8,128)}, bf16[12,512,64]{1,2,0:T(8,128)(2,1)}, s32[12,512]{1,0:T(8,128)}, s32[192]{0:T(256)}, /*index=5*/bf1...) while((s32[]{:T(128)}, f32[192,7,64]{0,2,1:T(8,128)}, ...), condition=%wide.region_7.8_spmd.clone, body=%wide.region_6.7_spmd.clone.sunk | while | flops 179183616 | bytes 1315955 | solution.py:123
  463.3 44.1 %while.103 = (s32[]{:T(128)}, f32[192,7,64]{0,2,1:T(8,128)S(1)}, bf16[12,512,64]{1,2,0:T(8,128)(2,1)S(1)}, s32[12,512]{1,0:T(8,128)}, s32[192]{0:T(256)}, /*inde...) while((s32[]{:T(128)}, f32[192,7,64]{0,2,1:T(8,128)S(1)}, ...), condition=%wide.region_13.14_spmd.clone, body=%wide.region_12.13_spmd.clone.sunk | while | flops 179183616 | bytes 1376115 | solution.py:123
  527.2 41.0 %all-gather.20.cloned.1.call-done = bf16[4864,896]{1,0:T(8,128)(2,1)} async-done(((bf16[1216,896]{1,0:T(8,128)(2,1)}), bf16[4864,896]{1,0:T(8,128)(2,1)}) %all-gather.20.cloned.1.call-update) | async-done | bytes 8716304 | tf_op jit(solution)/shard_map/all_gather | solution.py:238
  594.9 62.3 %while.104 = (s32[]{:T(128)}, f32[7,192,1]{1,2,0:T(1,128)S(1)}, s32[12,512]{1,0:T(8,128)}, s32[192]{0:T(256)}, bf16[12,512,64]{1,2,0:T(8,128)(2,1)}, /*index=5*/...) while((s32[]{:T(128)}, f32[7,192,1]{1,2,0:T(1,128)S(1)}, ...), condition=%wide.region_18.19_spmd.clone, body=%wide.region_16.18_spmd.clone.sunk | while | flops 179701056 | bytes 6269051 | solution.py:160
  660.5 209.5 %while.105 = (s32[]{:T(128)}, f32[192,7,64]{0,2,1:T(8,128)S(1)}, f32[12,512,64]{1,0,2:T(8,128)}, f32[12,512,64]{1,0,2:T(8,128)}, bf16[12,512,64]{1,2,0:T(8,128)(...) while((s32[]{:T(128)}, f32[192,7,64]{0,2,1:T(8,128)S(1)}, ...), condition=%wide.region_20.21_spmd.clone, body=%wide.region_19.20_spmd.clone.sunk | while | flops 447672320 | bytes 26656952 | solution.py:191
  870.0 61.2 %while.106 = (s32[]{:T(128)}, f32[7,192,1]{1,2,0:T(1,128)S(1)}, s32[12,512]{1,0:T(8,128)}, s32[192]{0:T(256)}, bf16[12,512,64]{1,2,0:T(8,128)(2,1)}, /*index=5*/...) while((s32[]{:T(128)}, f32[7,192,1]{1,2,0:T(1,128)S(1)}, ...), condition=%wide.region_23.24_spmd.clone, body=%wide.region_21.23_spmd.clone.sunk | while | flops 179701056 | bytes 6899863 | solution.py:160
  934.4 207.8 %while.107 = (s32[]{:T(128)}, f32[192,7,64]{0,2,1:T(8,128)S(1)}, f32[12,512,64]{1,0,2:T(8,128)}, f32[12,512,64]{1,0,2:T(8,128)}, bf16[12,512,64]{1,2,0:T(8,128)(...) while((s32[]{:T(128)}, f32[192,7,64]{0,2,1:T(8,128)S(1)}, ...), condition=%wide.region_25.26_spmd.clone, body=%wide.region_24.25_spmd.clone.sunk | while | flops 447672320 | bytes 27287764 | solution.py:191
  1174.5 146.2 %reduce-scatter.28.cloned.1.call-done = f32[192,128]{1,0:T(8,128)} async-done(((f32[6144,128]{1,0:T(8,128)}), f32[192,128]{1,0:T(8,128)}) %reduce-scatter.28.cloned.1.call-update) | async-done | bytes 98320
  1323.2 162.7 %reduce-scatter.30.cloned.1.call-done = f32[192,128]{1,0:T(8,128)} async-done(((f32[6144,128]{1,0:T(8,128)}), f32[192,128]{1,0:T(8,128)}) %reduce-scatter.30.cloned.1.call-update) | async-done | bytes 98320
  1488.1 11.4 fusion.185
  1519.3 11.4 reduce-scatter.14.cloned.1.call-done
  1530.7 48.2 %reduce-scatter.20.cloned.1.call-done = f32[224,896]{1,0:T(8,128)} async-done(((f32[896,896]{1,0:T(8,128)}), f32[224,896]{1,0:T(8,128)}) %reduce-scatter.20.cloned.1.call-update) | async-done | bytes 802832 | tf_op jit(solution)/shard_map/reduce_scatter | solution.py:360
  1578.8 30.6 %reduce-scatter.16.cloned.1.call-done = f32[224,128]{1,0:T(8,128)} async-done(((f32[896,128]{1,0:T(8,128)}), f32[224,128]{1,0:T(8,128)}) %reduce-scatter.16.cloned.1.call-update) | async-done | bytes 114704 | tf_op jit(solution)/shard_map/reduce_scatter | solution.py:358
  1609.4 30.7 %reduce-scatter.18.cloned.1.call-done = f32[224,128]{1,0:T(8,128)} async-done(((f32[896,128]{1,0:T(8,128)}), f32[224,128]{1,0:T(8,128)}) %reduce-scatter.18.cloned.1.call-update) | async-done | bytes 114704 | tf_op jit(solution)/shard_map/reduce_scatter | solution.py:359
  1640.2 139.0 %reduce-scatter.22.cloned.1.call-done = f32[224,4864]{1,0:T(8,128)} async-done(((f32[896,4864]{1,0:T(8,128)}), f32[224,4864]{1,0:T(8,128)}) %reduce-scatter.22.cloned.1.call-update) | async-done | bytes 4358160 | tf_op jit(solution)/shard_map/reduce_scatter | solution.py:361
  1779.2 139.2 %reduce-scatter.24.cloned.1.call-done = f32[224,4864]{1,0:T(8,128)} async-done(((f32[896,4864]{1,0:T(8,128)}), f32[224,4864]{1,0:T(8,128)}) %reduce-scatter.24.cloned.1.call-update) | async-done | bytes 4358160 | tf_op jit(solution)/shard_map/reduce_scatter | solution.py:362
  1918.4 139.0 %reduce-scatter.26.cloned.1.call-done = f32[1216,896]{1,0:T(8,128)} async-done(((f32[4864,896]{1,0:T(8,128)}), f32[1216,896]{1,0:T(8,128)}) %reduce-scatter.26.cloned.1.call-update) | async-done | bytes 4358160 | tf_op jit(solution)/shard_map/reduce_scatter | solution.py:363
  2069.3 14.5 all-reduce.12
  2084.2 84.1 %all-reduce.10 = (f32[224]{0:T(256)}, f32[32]{0:T(128)}, f32[32]{0:T(128)}, f32[224]{0:T(256)}, f32[224]{0:T(256)}) all-reduce(f32[224]{0:T(256)S(1)} %dynamic-slice.6, f32[32]{0:T(128)S(1)} %dynamic-slice.8, f32[32]{0:T(128)S(1)} %dynamic-slice.10, f32[224]{0:T(256)S(1)} %dynamic-slice.12, ...), channel_id=1, replica_groups=mesh['ctx'=32,'fsdp'=4] {'ctx'}, use_global_device_ids=true, to_apply=%region_45.46 | all-reduce | flops 736 | bytes 5888 | tf_op jit(solution)/shard_map/psum | solution.py:370
  2170.4 272.4 %all-reduce.16.cloned.1.call-done = (f32[224,896]{1,0:T(8,128)}, f32[224,128]{1,0:T(8,128)}, f32[224,128]{1,0:T(8,128)}, f32[224,896]{1,0:T(8,128)}, f32[224,486...) async-done(((f32[224,896]{1,0:T(8,128)}, f32[224,128]{1,0:T(8,128)}, f32[224,128]{1,0:T(8,128)}, f32[224,896]{1,0:T(8,128)}, f32[224,4864]{1,0:T(8,128)}, ...) | async-done | bytes 14909456 | tf_op jit(solution)/shard_map/psum | solution.py:370
  (983 shorter events, 937.6 us)
Async XLA Ops:
  7.2 44.8 %all-gather.12.cloned.1.call-start = ((), (), s32[]{:S(2)}) async-start(), calls=%async_computation.11 | async-start | bytes 2007040 | tf_op jit(solution)/shard_map/all_gather | solution.py:226
  7.9 184.5 %all-gather.10.cloned.1.call-start = ((), (), s32[]{:S(2)}) async-start(), calls=%async_computation.10 | async-start | bytes 1622016 | tf_op jit(solution)/shard_map/all_gather | solution.py:256
  39.3 308.0 %all-gather.8.cloned.1.call-start = ((), (), s32[]{:S(2)}) async-start(), calls=%async_computation.9 | async-start | bytes 1622016 | tf_op jit(solution)/shard_map/all_gather | solution.py:257
  47.6 460.9 %all-gather.14.cloned.1.call-start = ((), (), s32[]{:S(2)}) async-start(), calls=%async_computation.12 | async-start | bytes 2007040 | tf_op jit(solution)/shard_map/all_gather | solution.py:229
  48.1 462.8 %all-gather.16.cloned.1.call-start = ((), (), s32[]{:S(2)}) async-start(), calls=%async_computation.13 | async-start | bytes 10895360 | tf_op jit(solution)/shard_map/all_gather | solution.py:236
  48.7 470.3 %all-gather.18.cloned.1.call-start = ((), (), s32[]{:S(2)}) async-start(), calls=%async_computation.14 | async-start | bytes 10895360 | tf_op jit(solution)/shard_map/all_gather | solution.py:237
  49.3 518.9 %all-gather.20.cloned.1.call-start = ((), (), s32[]{:S(2)}) async-start(), calls=%async_computation.15 | async-start | bytes 10895360 | tf_op jit(solution)/shard_map/all_gather | solution.py:238
  50.1 1270.7 %reduce-scatter.28.cloned.1.call-start = ((), (), s32[]{:S(2)}) async-start(), calls=%async_computation.23 | async-start | bytes 3244032
  405.9 55.9 %copy-start.15 = (bf16[12,512,64]{1,0,2:T(8,128)(2,1)S(1)}, bf16[12,512,64]{1,0,2:T(8,128)(2,1)}, u32[]{:S(2)}) copy-start(bf16[12,512,64]{1,0,2:T(8,128)(2,1)} %get-tuple-element.1092) | copy-start | bytes 2359300
  405.9 57.4 %copy-start.36 = (f32[192,7,64]{0,2,1:T(8,128)S(1)}, f32[192,7,64]{0,2,1:T(8,128)}, u32[]{:S(2)}) copy-start(f32[192,7,64]{0,2,1:T(8,128)} %custom-call.5) | copy-start | bytes 1032196
  510.8 79.1 %copy-start.9 = (f32[192,896]{1,0:T(8,128)}, f32[192,896]{1,0:T(8,128)S(1)}, u32[]{:S(2)}) copy-start(f32[192,896]{1,0:T(8,128)S(1)} %get-tuple-element.1115) | copy-start | bytes 2064388
  519.0 49.2 %copy-start.23 = (bf16[1,192,896]{2,1,0:T(8,128)(2,1)S(1)}, bf16[1,192,896]{2,1,0:T(8,128)(2,1)}, u32[]{:S(2)}) copy-start(bf16[1,192,896]{2,1,0:T(8,128)(2,1)} %param.45) | copy-start | bytes 1032196
  660.5 209.5 %copy-start.40 = (f32[7,192,1]{1,2,0:T(1,128)S(1)}, f32[7,192,1]{1,2,0:T(1,128)}, u32[]{:S(2)}) copy-start(f32[7,192,1]{1,2,0:T(1,128)} %custom-call.8) | copy-start | bytes 16132
  1155.4 330.4 %reduce-scatter.30.cloned.1.call-start = ((), (), s32[]{:S(2)}) async-start(), calls=%async_computation.24 | async-start | bytes 3244032
  1168.4 362.2 %reduce-scatter.14.cloned.1.call-start = ((), (), s32[]{:S(2)}) async-start(), calls=%async_computation.16 | async-start | bytes 4014080 | tf_op jit(solution)/shard_map/reduce_scatter | solution.py:357
  1172.1 406.8 %reduce-scatter.20.cloned.1.call-start = ((), (), s32[]{:S(2)}) async-start(), calls=%async_computation.19 | async-start | bytes 4014080 | tf_op jit(solution)/shard_map/reduce_scatter | solution.py:360
  1174.5 434.9 %reduce-scatter.16.cloned.1.call-start = ((), (), s32[]{:S(2)}) async-start(), calls=%async_computation.17 | async-start | bytes 573440 | tf_op jit(solution)/shard_map/reduce_scatter | solution.py:358
  1321.9 177.6 %copy-start.34 = (bf16[192,2,64]{0,2,1:T(8,128)(2,1)}, bf16[192,2,64]{0,2,1:T(8,128)(2,1)S(1)}, u32[]{:S(2)}) copy-start(bf16[192,2,64]{0,2,1:T(8,128)(2,1)S(1)} %get-tuple-element.1077) | copy-start | bytes 147460
  1323.1 317.1 %reduce-scatter.18.cloned.1.call-start = ((), (), s32[]{:S(2)}) async-start(), calls=%async_computation.18 | async-start | bytes 573440 | tf_op jit(solution)/shard_map/reduce_scatter | solution.py:359
  1488.1 291.1 %reduce-scatter.22.cloned.1.call-start = ((), (), s32[]{:S(2)}) async-start(), calls=%async_computation.20 | async-start | bytes 21790720 | tf_op jit(solution)/shard_map/reduce_scatter | solution.py:361
  1499.5 418.9 %reduce-scatter.24.cloned.1.call-start = ((), (), s32[]{:S(2)}) async-start(), calls=%async_computation.21 | async-start | bytes 21790720 | tf_op jit(solution)/shard_map/reduce_scatter | solution.py:362
  1509.7 547.7 %reduce-scatter.26.cloned.1.call-start = ((), (), s32[]{:S(2)}) async-start(), calls=%async_computation.22 | async-start | bytes 21790720 | tf_op jit(solution)/shard_map/reduce_scatter | solution.py:363
  1519.1 923.8 %all-reduce.16.cloned.1.call-start = ((), (), s32[]{:S(2)}) async-start(), calls=%async_computation.25 | async-start | bytes 29818880 | tf_op jit(solution)/shard_map/psum | solution.py:370
  2066.4 101.9 %copy-start.50 = (f32[192]{0:T(256)S(1)}, f32[192]{0:T(256)}, u32[]{:S(2)}) copy-start(f32[192]{0:T(256)} %get-tuple-element.1108) | copy-start | bytes 2308
  (90 other events, 487.9 us)
Sparse Core Ops, SparseCore 0:
  9.7 26.5 all-gather.11
  39.4 152.9 all-gather.9
  194.6 152.6 all-gather.7
  348.8 23.6 all-gather.13
  374.0 63.6 all-gather.15
  439.2 63.5 all-gather.17
  504.5 63.6 all-gather.19
  1155.6 165.1 reduce-scatter.27
  1323.9 161.9 reduce-scatter.29
  1488.9 41.6 reduce-scatter.13
  1534.1 44.6 reduce-scatter.19
  1581.9 27.4 reduce-scatter.15
  1612.6 27.4 reduce-scatter.17
  1642.8 136.3 reduce-scatter.21
  1782.0 136.3 reduce-scatter.23
  1921.0 136.3 reduce-scatter.25
  2060.7 382.0 all-reduce.15
where the time goes:
time: 2490 us; the launch traced here: 2470 us
  waiting for transfers between devices  1400 us (56%)
  matrix products  469 us (19%)
  local copies, waits for them, and re-layouts  334 us (13%)
  blocking collectives  124 us (5%)
  other arithmetic  116 us (5%)
    unnamed x19, waiting for transfers between devices  312 us
    psum x1, waiting for transfers between devices, body(): lax.psum((shares[0], shares[1], shares[2], shares[3], shares[4], shares[5...  272 us
    dynamic_update_slice x96, local copies, waits for them, and re-layouts, attention_backward(): lax.scan(grads, jnp.zeros((local_rows, groups, HD), jnp.float32), blocks)  187 us
    reduce_scatter x1, waiting for transfers between devices, body(): lax.psum_scatter(partials[5], 'fsdp', scatter_dimension=0, tiled=True)  139 us
    reduce_scatter x1, waiting for transfers between devices, body(): lax.psum_scatter(partials[6], 'fsdp', scatter_dimension=0, tiled=True)  139 us
    reduce_scatter x1, waiting for transfers between devices, body(): lax.psum_scatter(partials[4], 'fsdp', scatter_dimension=0, tiled=True)  139 us
    all_gather x1, waiting for transfers between devices, body(): lax.all_gather(key_rot, 'ctx', axis=0, tiled=True)  138 us
    dot_general x72, matrix products, masked_scores(): jnp.einsum('tgd,sd->gts', query_part, key_part, preferred_element_type=jn...  108 us
  transfers between devices with their start and end apart: 17, of which 13 were waited for; matrix products, arithmetic and copies ran while one was open for 13% of the time, Pallas kernels for 0%

commit v1 on v0

v1 whole, which is shorter than its diff:
```python
import functools
import math

import jax
import jax.numpy as jnp
from jax import lax
from jax.experimental import pallas as pl
from jax.experimental.pallas import tpu as pltpu
from jax.sharding import PartitionSpec as P

H = 14
KVH = 2
GROUP = H // KVH
HD = 64
ROWS = 192
BLK = 96
LANES = 1408
SLAB = 1536
SLABS = 4
OWN = 256

EPSILON = 1e-06
THETA = 1000000.0
MASKED = -1e30

BF = jnp.bfloat16
F32 = jnp.float32
VMEM = pl.BlockSpec(memory_space=pltpu.VMEM)
NT = (((1,), (1,)), ((), ()))
TN = (((0,), (0,)), ((), ()))


def dot(left, right):
    return jnp.dot(left, right, preferred_element_type=F32)


def dot_nt(left, right):
    return lax.dot_general(left, right, NT, preferred_element_type=F32)


def dot_tn(left, right):
    return lax.dot_general(left, right, TN, preferred_element_type=F32)


def thirds(value):
    high = value.astype(BF).astype(F32)
    rest = value - high
    middle = rest.astype(BF).astype(F32)
    low = (rest - middle).astype(BF).astype(F32)
    return high, middle, low


MESH = pl.DeviceIdType.MESH
ANY = pl.BlockSpec(memory_space=pl.ANY)
WINDOW = 1280
UNITS = 1216
SHARD = 224
WIDTH = 896
MIB = 2**20


def place():
    ctx, f = lax.axis_index("ctx"), lax.axis_index("fsdp")
    return lax.div(ctx, 16), lax.rem(lax.div(ctx, 4), 4), lax.rem(ctx, 4), lax.div(f, 2), lax.rem(f, 2)


def at(yl, x, z, yh, c):
    return ((yl * 4 + x) * 4 + z, yh * 2 + c)


def turn(index, by):
    return lax.rem(index + by, 4)


def greet(devices):
    barrier = pltpu.get_barrier_semaphore()
    for device in devices:
        pl.semaphore_signal(barrier, inc=1, device_id=device, device_id_type=MESH)
    pl.semaphore_wait(barrier, len(devices))


class Links:
    def __init__(self, send, recv):
        self.send, self.recv, self.used = send, recv, 0

    def reserve(self, count):
        first = self.used
        self.used += count
        return first

    def copy(self, src, dst, device, slot):
        return pltpu.make_async_remote_copy(
            src_ref=src,
            dst_ref=dst,
            send_sem=self.send.at[slot],
            recv_sem=self.recv.at[slot],
            device_id=device,
            device_id_type=MESH,
        )

    def push(self, src, dst, device):
        copy = self.copy(src, dst, device, self.reserve(1))
        copy.start()
        return copy


def lanes_below(shape, bound):
    return lax.broadcasted_iota(jnp.int32, shape, 1) < bound


def swap64(value):
    return pltpu.roll(value, 64, axis=1)


def turn_pairs(value, cosine, sine):
    lane = lax.broadcasted_iota(jnp.int32, value.shape, 1)
    other = jnp.where(
        lax.rem(lane, 64) < 32, pltpu.roll(value, 96, axis=1), pltpu.roll(value, 32, axis=1)
    )
    return value * cosine + other * sine


def key_extra(rows):
    count = rows.shape[0]
    return jnp.broadcast_to(rows[:, None, :], (count, BLK, 128)).reshape(count * BLK, 128).astype(BF)


def own_extra():
    lane = lax.broadcasted_iota(jnp.int32, (OWN, 128), 1)
    return jnp.where((lane >= 2) & (lane < 5), 1.0, 0.0).astype(BF)


def window_start(f):
    return pl.multiple_of(lax.div(19 * f, 2) * 128, 128)


def front_kernel(
    tokens_ref,
    wq_ref,
    wk_ref,
    wv_ref,
    small_ref,
    cos_ref,
    sin_ref,
    extra_ref,
    kpos_ref,
    qpos_ref,
    wo_ref,
    gate_ref,
    up_ref,
    cot_ref,
    attended_ref,
    ot_ref,
    lse_ref,
    q_ref,
    kv_ref,
    normed_ref,
    wq_all,
    wk_all,
    wv_all,
    small_all,
    wo_all,
    gate_all,
    up_all,
    cot_all,
    own,
    acc,
    top,
    natural,
    send,
    recv,
    local,
):
    yl, x, z, yh, c = place()
    f = yh * 2 + c
    f_cross = (1 - yh) * 2 + c
    f_sib = yh * 2 + 1 - c
    f_far = (1 - yh) * 2 + 1 - c
    sib = at(yl, x, z, yh, 1 - c)
    cross = at(1 - yl, x, z, 1 - yh, c)
    far = at(1 - yl, x, z, 1 - yh, 1 - c)
    mate = at(1 - yl, x, z, yh, c)
    on_x = [at(yl, turn(x, d), z, yh, c) for d in (1, 2, 3)]
    on_z = [at(yl, x, turn(z, d), yh, c) for d in (1, 2, 3)]
    links = Links(send, recv)
    greet([sib, cross, far, mate] + on_x + on_z)

    def gather_start(pairs):
        return [
            (links.push(mine, whole.at[f], sib), links.push(mine, whole.at[f], cross), whole)
            for mine, whole in pairs
        ]

    def gather_relay(started):
        relays = []
        for _, over, whole in started:
            over.wait_recv()
            relays.append(links.push(whole.at[f_cross], whole.at[f_cross], sib))
        return relays

    def gather_end(started, relays):
        for beside, over, _ in started:
            beside.wait()
            over.wait_send()
        for relay in relays:
            relay.wait()

    first = gather_start(
        [(wq_ref, wq_all), (wk_ref, wk_all), (wv_ref, wv_all), (small_ref, small_all)]
    )
    keep = []
    for n, (mine, whole) in enumerate(
        [(wo_ref, wo_all.at[f]), (cot_ref, cot_all.at[f])]
        + [
            (ref.at[:, pl.ds(window_start(f), WINDOW)], whole.at[f])
            for ref, whole in ((gate_ref, gate_all), (up_ref, up_all))
        ]
    ):
        copy = pltpu.make_async_copy(mine, whole, local.at[n])
        copy.start()
        keep.append(copy)
    wq_all[f] = wq_ref[...]
    wk_all[f] = wk_ref[...]
    wv_all[f] = wv_ref[...]
    small_all[f] = small_ref[...]
    inputs = tokens_ref[...].astype(F32)
    scale = lax.rsqrt(jnp.mean(inputs * inputs, axis=-1, keepdims=True) + EPSILON)
    relays = gather_relay(first)
    second = gather_start([(wo_ref, wo_all), (cot_ref, cot_all)])
    spread = []
    for ref, whole in ((gate_ref, gate_all), (up_ref, up_all)):
        for device, index in ((cross, f_cross), (far, f_far), (sib, f_sib)):
            part = ref.at[:, pl.ds(window_start(index), WINDOW)]
            spread.append(links.push(part, whole.at[f], device))
    gather_end(first, relays)

    def vector(row, count):
        return jnp.concatenate([small_all[n, row : row + 1, 0:count] for n in range(4)], axis=1)

    normed = (inputs * scale * vector(1, SHARD)).astype(BF)
    normed_ref[...] = normed
    cosine, sine = cos_ref[...], sin_ref[...]
    low = lanes_below((ROWS, 128), 64)

    queries = dot(normed, wq_all[...].reshape(WIDTH, WIDTH)) + vector(0, SHARD)
    keys = dot(normed, wk_all[...].reshape(WIDTH, 128)) + vector(3, 32)
    values = dot(normed, wv_all[...].reshape(WIDTH, 128)) + vector(4, 32)
    keys = turn_pairs(keys, cosine, sine).astype(BF).astype(F32)
    values = values.astype(BF).astype(F32)
    own[...] = jnp.zeros(own.shape, BF)
    own[0, 0:ROWS] = jnp.where(low, keys, swap64(values)).astype(BF)
    own[1, 0:ROWS] = jnp.where(low, swap64(keys), values).astype(BF)

    slab_of = (x, z)
    spot = [
        pl.ds(pl.multiple_of((z * 2 + yl) * ROWS, ROWS), ROWS),
        pl.ds(pl.multiple_of((x * 2 + yl) * ROWS, ROWS), ROWS),
    ]
    pair = [
        pl.ds(pl.multiple_of(z * 2 * ROWS, 2 * ROWS), 2 * ROWS),
        pl.ds(pl.multiple_of(x * 2 * ROWS, 2 * ROWS), 2 * ROWS),
    ]
    mates = [
        links.push(own.at[g, 0:ROWS], kv_ref.at[g, slab_of[g], spot[g]], mate) for g in range(KVH)
    ]
    for g in range(KVH):
        kv_ref[g, slab_of[g], spot[g], :] = own[g, 0:ROWS]

    for tile in range(H // 2):
        part = turn_pairs(queries[:, tile * 128 : tile * 128 + 128], cosine, sine)
        part = part.astype(BF).astype(F32) * (1.0 / math.sqrt(HD))
        for half in range(2):
            head = tile * 2 + half
            j = head % GROUP
            mine = part if half == 0 else swap64(part)
            q_ref[head // GROUP, j * ROWS : (j + 1) * ROWS, 0:128] = jnp.where(
                low, mine, 0.0
            ).astype(BF)
    row = lax.broadcasted_iota(jnp.int32, (LANES, 128), 0)
    lane = lax.broadcasted_iota(jnp.int32, (LANES, 128), 1)
    block = lax.rem(lax.div(row, BLK), 2)
    hot = jnp.where((block == lane) & (row < GROUP * ROWS), 1.0, 0.0).astype(BF)
    for g in range(KVH):
        q_ref[g, :, 128:256] = hot
        q_ref[g, GROUP * ROWS :, 0:128] = jnp.zeros((LANES - GROUP * ROWS, 128), BF)

    def mix(g, keys, scores):
        old = top[g, 0:1]
        new = jnp.maximum(old, jnp.max(scores, axis=0, keepdims=True))
        weights = jnp.exp(scores - new).astype(BF)
        acc[g] = acc[g] * jnp.exp(old - new) + dot(keys.T[64:136], weights)
        top[g, 0:1] = new

    top[...] = jnp.full(top.shape, MASKED, F32)
    acc[...] = jnp.zeros(acc.shape, F32)
    for copy in mates:
        copy.wait()
    pairs = [
        links.push(kv_ref.at[0, x, pair[0]], kv_ref.at[0, x, pair[0]], device) for device in on_z
    ] + [links.push(kv_ref.at[1, z, pair[1]], kv_ref.at[1, z, pair[1]], device) for device in on_x]
    mask = jnp.where(kpos_ref[:, 0:1] <= qpos_ref[0:1], 0.0, MASKED)
    for g in range(KVH):
        keys = jnp.concatenate([own[g], own_extra()], axis=1)
        mix(g, keys, dot_nt(keys, q_ref[g]) + mask)
    for copy in pairs:
        copy.wait()
    base = links.reserve(6)

    def slab_copy(g, d, slab):
        device = (
            ((yl * 4 + jnp.where(g == 0, turn(x, d), x)) * 4 + jnp.where(g == 0, z, turn(z, d))),
            f,
        )
        return links.copy(kv_ref.at[g, slab], kv_ref.at[g, slab], device, base + g * 3 + d - 1)

    slabs = [slab_copy(g, d, slab_of[g]) for d in (1, 3, 2) for g in range(KVH)]
    for copy in slabs:
        copy.start()
    relays = []

    def step(i, _):
        g, n = lax.rem(i, 2), lax.div(i, 2)
        d = jnp.where(n == 2, 3, jnp.where(n == 3, 2, n))
        slab = turn(jnp.where(g == 0, x, z), d)

        @pl.when(n > 0)
        def _():
            slab_copy(g, 4 - d, slab).wait_recv()

        rows = extra_ref[g, pl.ds(pl.multiple_of(slab * 16, 16), 16), :]
        keys = jnp.concatenate([kv_ref[g, slab], key_extra(rows)], axis=1)
        mix(g, keys, dot_nt(keys, q_ref[g]))
        return 0

    lax.fori_loop(0, 8, step, 0)
    for copy in slabs:
        copy.wait_send()
    relays = gather_relay(second)

    for g in range(KVH):
        total = acc[g, 66:67]
        out = acc[g, 0:64] / total
        ot_ref[g] = out
        lse_ref[g] = jnp.broadcast_to(top[g, 0:1] + jnp.log(total), (8, LANES))
        natural[g] = jnp.concatenate([out, jnp.zeros((64, LANES), F32)], axis=0).T
    for tile in range(H // 2):
        even, odd = tile * 2, tile * 2 + 1
        left = natural[even // GROUP, (even % GROUP) * ROWS : (even % GROUP + 1) * ROWS]
        right = natural[odd // GROUP, (odd % GROUP) * ROWS : (odd % GROUP + 1) * ROWS]
        attended_ref[:, tile * 128 : tile * 128 + 128] = jnp.where(
            low, left, swap64(right)
        ).astype(BF)
    for copy in spread:
        copy.wait()
    gather_end(second, relays)
    for copy in keep:
        copy.wait()


def front(tokens, wq, wk, wv, small, cosine, sine, extra, kpos, qpos, wo, gate, up, cot):
    shape = jax.ShapeDtypeStruct
    return pl.pallas_call(
        front_kernel,
        out_shape=[
            shape((ROWS, WIDTH), BF),
            shape((KVH, HD, LANES), F32),
            shape((KVH, 8, LANES), F32),
            shape((KVH, LANES, 256), BF),
            shape((KVH, SLABS, SLAB, 128), BF),
            shape((ROWS, WIDTH), BF),
            shape((4, SHARD, WIDTH), BF),
            shape((4, SHARD, 128), BF),
            shape((4, SHARD, 128), BF),
            shape((4, 8, 256), F32),
            shape((4, SHARD, WIDTH), BF),
            shape((4, SHARD, WINDOW), BF),
            shape((4, SHARD, WINDOW), BF),
            shape((4, ROWS, WIDTH), BF),
        ],
        in_specs=[VMEM] * 10 + [ANY] * 4,
        out_specs=[VMEM] * 10 + [ANY] * 4,
        scratch_shapes=[
            pltpu.VMEM((KVH, OWN, 128), BF),
            pltpu.VMEM((KVH, 72, LANES), F32),
            pltpu.VMEM((KVH, 8, LANES), F32),
            pltpu.VMEM((KVH, LANES, 128), F32),
            pltpu.SemaphoreType.DMA((48,)),
            pltpu.SemaphoreType.DMA((48,)),
            pltpu.SemaphoreType.DMA((4,)),
        ],
        compiler_params=pltpu.CompilerParams(
            vmem_limit_bytes=58 * MIB, collective_id=0, has_side_effects=True
        ),
        name="front",
    )(tokens, wq, wk, wv, small, cosine, sine, extra, kpos, qpos, wo, gate, up, cot)


UNIT = 106
HALF = 53
CHUNK = 768


def widen(ref, index):
    return ref[index].astype(F32)


def back_kernel(
    q_ref,
    do_ref,
    ot_ref,
    lse_ref,
    kv_ref,
    extra_ref,
    kpos_ref,
    qpos_ref,
    grads_ref,
    dkv_ref,
    dq_ref,
    sum_ref,
    qx,
    dox,
    own,
    own_grad,
    parts,
    parts_in,
    pairs,
    pairs_in,
    single,
    single_in,
    side_a,
    side_b,
    in_a,
    in_b,
    late_a,
    late_b,
    whole,
    whole_in,
    send,
    recv,
    local,
):
    yl, x, z, yh, c = place()
    f = yh * 2 + c
    mate = at(1 - yl, x, z, yh, c)
    on_x = [at(yl, turn(x, d), z, yh, c) for d in (1, 2, 3)]
    on_z = [at(yl, x, turn(z, d), yh, c) for d in (1, 2, 3)]
    links = Links(send, recv)
    greet([mate] + on_x + on_z)

    first = []
    for n in range(3):
        first.append(
            links.push(grads_ref.at[turn(x, n + 1), :, 0:HALF], in_a.at[n], on_x[n])
        )
        first.append(
            links.push(grads_ref.at[:, turn(z, n + 1), HALF:UNIT], in_b.at[n], on_z[n])
        )
    keep = [
        pltpu.make_async_copy(grads_ref.at[x, :, 0:HALF], side_a, local.at[0]),
        pltpu.make_async_copy(grads_ref.at[:, z, HALF:UNIT], side_b, local.at[1]),
    ]
    for copy in keep:
        copy.start()

    row = lax.broadcasted_iota(jnp.int32, (128, LANES), 0)
    for g in range(KVH):
        lse = thirds(lse_ref[g, 0:1])
        inner = jnp.sum(do_ref[g].astype(F32).T[64:128] * ot_ref[g], axis=0, keepdims=True)
        inner = thirds(inner)
        extra_q = jnp.zeros((128, LANES), F32)
        extra_d = jnp.zeros((128, LANES), F32)
        for n in range(3):
            extra_q = jnp.where(row == 2 + n, -lse[n], extra_q)
            extra_d = jnp.where(row == 2 + n, -inner[n], extra_d)
        qx[g, :, 0:128] = q_ref[g, :, 0:128]
        qx[g, :, 128:256] = (q_ref[g, :, 128:256].astype(F32) + extra_q.T).astype(BF)
        dox[g, :, 0:128] = do_ref[g]
        dox[g, :, 128:256] = extra_d.T.astype(BF)

    def piece(g, keys, mask):
        scores = dot_nt(keys, qx[g])
        if mask is not None:
            scores = scores + mask
        probs = jnp.exp(scores)
        grad = (probs * dot_nt(keys, dox[g])).astype(BF)
        both = dot(grad, qx[g, :, 0:128]) + dot(probs.astype(BF), dox[g, :, 0:128])
        return both, dot(keys[:, 0:128].T[0:64], grad)

    mask = jnp.where(kpos_ref[:, 0:1] <= qpos_ref[0:1], 0.0, MASKED)
    spots = (
        pl.ds(pl.multiple_of((z * 2 + yl) * ROWS, ROWS), ROWS),
        pl.ds(pl.multiple_of((x * 2 + yl) * ROWS, ROWS), ROWS),
    )
    slab_of = (x, z)
    for g in range(KVH):
        own[...] = jnp.zeros(own.shape, BF)
        own[0:ROWS] = kv_ref[g, slab_of[g], spots[g], :]
        both, dq = piece(g, jnp.concatenate([own[...], own_extra()], axis=1), mask)
        own_grad[g] = both[0:ROWS]
        dq_ref[g] = dq
    count = SLAB // CHUNK
    base = links.reserve(6)

    def part_copy(g, d, slab):
        device = (
            ((yl * 4 + jnp.where(g == 0, slab, x)) * 4 + jnp.where(g == 0, z, slab)),
            f,
        )
        n = g * 3 + d - 1
        return links.copy(parts.at[g, slab], parts_in.at[g, d - 1], device, base + n)

    def step(i, _):
        g = lax.div(i, SLABS * count)
        d = lax.rem(lax.rem(lax.div(i, count), SLABS) + 1, 4)
        part = lax.rem(i, count)
        slab = turn(jnp.where(g == 0, x, z), d)
        start = pl.multiple_of(part * CHUNK, CHUNK)
        rows = extra_ref[g, pl.ds(pl.multiple_of(slab * 16 + part * 8, 8), 8), :]
        keys = jnp.concatenate([kv_ref[g, slab, pl.ds(start, CHUNK), :], key_extra(rows)], axis=1)
        both, dq = piece(g, keys, None)
        parts[g, slab, pl.ds(start, CHUNK), :] = both.astype(BF)
        dq_ref[g] += dq

        @pl.when((part == count - 1) & (d > 0))
        def _():
            part_copy(g, d, slab).start()

        return 0

    pair_copies = []

    def pair_start(g):
        slab = slab_of[g]
        for d in (1, 2, 3):
            part_copy(g, d, turn(slab, d)).wait()
        for n in range(4):
            rows = slice(n * 2 * ROWS, (n + 1) * 2 * ROWS)
            total = parts[g, slab, rows, :].astype(F32)
            for m in range(3):
                total = total + parts_in[g, m, rows, :].astype(F32)
            pairs[g, n] = total.astype(BF)
        other = (z, x)[g]
        devices = (on_z, on_x)[g]
        return [
            links.push(pairs.at[g, turn(other, n + 1)], pairs_in.at[g, n], devices[n])
            for n in range(3)
        ]

    def single_start(g, copies):
        for copy in copies:
            copy.wait()
        total = pairs[g, (z, x)[g]].astype(F32)
        for m in range(3):
            total = total + pairs_in[g, m].astype(F32)
        single[g, 0] = total[0:ROWS]
        single[g, 1] = total[ROWS:]
        low = jnp.where(yl == 0, total[ROWS:], total[0:ROWS])
        single_low = low.astype(BF)
        single_in[g, 0] = single_low
        return links.push(single_in.at[g, 0], single_in.at[g, 1], mate)

    def single_end(g, copy):
        copy.wait()
        dkv_ref[g] = single[g, yl] + single_in[g, 1].astype(F32) + own_grad[g]

    def second_start():
        for copy in keep + first:
            copy.wait()

        def add(n, _):
            a = side_a[n].astype(F32)
            b = side_b[n].astype(F32)
            for m in range(3):
                a = a + in_a[m, n].astype(F32)
                b = b + in_b[m, n].astype(F32)
            side_a[n] = a.astype(BF)
            side_b[n] = b.astype(BF)
            return 0

        lax.fori_loop(0, 4, add, 0)
        copies = []
        for n in range(3):
            copies.append(links.push(side_a.at[turn(z, n + 1)], late_a.at[n], on_z[n]))
            copies.append(links.push(side_b.at[turn(x, n + 1)], late_b.at[n], on_x[n]))
        return copies

    def third_start(copies):
        for copy in copies:
            copy.wait()
        a = side_a[z].astype(F32)
        b = side_b[x].astype(F32)
        for m in range(3):
            a = a + late_a[m].astype(F32)
            b = b + late_b[m].astype(F32)
        whole[0:HALF] = a.astype(BF)
        whole[HALF:UNIT] = b.astype(BF)
        return links.push(whole, whole_in, mate)

    steps = SLABS * count
    lax.fori_loop(0, steps, step, 0)
    pair_copies = pair_start(0)
    lax.fori_loop(steps, 2 * steps, step, 0)
    single_copy = single_start(0, pair_copies)
    second = second_start()
    pair_copies = pair_start(1)
    single_end(0, single_copy)
    third = third_start(second)
    single_copy = single_start(1, pair_copies)
    single_end(1, single_copy)
    third.wait()
    sum_ref[...] = (whole[...].astype(F32) + whole_in[...].astype(F32)).astype(BF)


def back(q, do, ot, lse, kv, extra, kpos, qpos, grads):
    shape = jax.ShapeDtypeStruct
    return pl.pallas_call(
        back_kernel,
        out_shape=[
            shape((KVH, ROWS, 128), F32),
            shape((KVH, HD, LANES), F32),
            shape((UNIT, 16, 128), BF),
        ],
        in_specs=[VMEM] * 8 + [ANY],
        out_specs=[VMEM] * 3,
        scratch_shapes=[
            pltpu.VMEM((KVH, LANES, 256), BF),
            pltpu.VMEM((KVH, LANES, 256), BF),
            pltpu.VMEM((OWN, 128), BF),
            pltpu.VMEM((KVH, ROWS, 128), F32),
            pltpu.VMEM((KVH, SLABS, SLAB, 128), BF),
            pltpu.VMEM((KVH, 3, SLAB, 128), BF),
            pltpu.VMEM((KVH, 4, 2 * ROWS, 128), BF),
            pltpu.VMEM((KVH, 3, 2 * ROWS, 128), BF),
            pltpu.VMEM((KVH, 2, ROWS, 128), F32),
            pltpu.VMEM((KVH, 2, ROWS, 128), BF),
            pltpu.VMEM((4, HALF, 16, 128), BF),
            pltpu.VMEM((4, HALF, 16, 128), BF),
            pltpu.VMEM((3, 4, HALF, 16, 128), BF),
            pltpu.VMEM((3, 4, HALF, 16, 128), BF),
            pltpu.VMEM((3, HALF, 16, 128), BF),
            pltpu.VMEM((3, HALF, 16, 128), BF),
            pltpu.VMEM((UNIT, 16, 128), BF),
            pltpu.VMEM((UNIT, 16, 128), BF),
            pltpu.SemaphoreType.DMA((48,)),
            pltpu.SemaphoreType.DMA((48,)),
            pltpu.SemaphoreType.DMA((2,)),
        ],
        compiler_params=pltpu.CompilerParams(
            vmem_limit_bytes=62 * MIB, collective_id=1, has_side_effects=True
        ),
        name="back",
    )(q, do, ot, lse, kv, extra, kpos, qpos, grads)


def last_kernel(
    sum_ref,
    dq_ref,
    dkv_ref,
    cos_ref,
    sin_ref,
    normed_ref,
    attended_ref,
    grad_attn_ref,
    grad_middle_ref,
    tokens_ref,
    wq_all,
    wk_all,
    wv_all,
    small_all,
    hidden_gain_ref,
    token_grad_ref,
    late_ref,
    thin_ref,
    whole_ref,
    natural,
    table,
    table_in,
    lines,
    lines_in,
    cols,
    cols_in,
    ends,
    ends_in,
    thin,
    send,
    recv,
    local,
):
    yl, x, z, yh, c = place()
    f = yh * 2 + c
    f_cross = (1 - yh) * 2 + c
    f_sib = yh * 2 + 1 - c
    f_far = (1 - yh) * 2 + 1 - c
    sib = at(yl, x, z, yh, 1 - c)
    cross = at(1 - yl, x, z, 1 - yh, c)
    far = at(1 - yl, x, z, 1 - yh, 1 - c)
    mate = at(1 - yl, x, z, yh, c)
    on_x = [at(yl, turn(x, d), z, yh, c) for d in (1, 2, 3)]
    on_z = [at(yl, x, turn(z, d), yh, c) for d in (1, 2, 3)]
    links = Links(send, recv)
    greet([sib, cross, far, mate] + on_x + on_z)

    shared = []
    for device, index in ((sib, f_sib), (cross, f_cross), (far, f_far)):
        shared.append(
            links.push(
                sum_ref.at[pl.ds(18 * index, 18)], whole_ref.at[x, z, pl.ds(18 * f, 18)], device
            )
        )
    keep = [
        pltpu.make_async_copy(
            sum_ref.at[pl.ds(18 * f, 18)], whole_ref.at[x, z, pl.ds(18 * f, 18)], local.at[0]
        ),
        pltpu.make_async_copy(
            sum_ref.at[72:UNIT], whole_ref.at[x, z, 72:UNIT], local.at[1]
        ),
    ]
    for copy in keep:
        copy.start()

    def assemble(tile):
        even, odd = tile * 2, tile * 2 + 1
        left = natural[even // GROUP, (even % GROUP) * ROWS : (even % GROUP + 1) * ROWS]
        right = natural[odd // GROUP, (odd % GROUP) * ROWS : (odd % GROUP + 1) * ROWS]
        return jnp.where(low, left, swap64(right))

    low = lanes_below((ROWS, 128), 64)
    cosine, sine = cos_ref[...], -sin_ref[...]
    for g in range(KVH):
        natural[g] = jnp.concatenate([dq_ref[g], jnp.zeros((64, LANES), F32)], axis=0).T
    grad_queries = jnp.concatenate(
        [
            turn_pairs(assemble(tile) * (1.0 / math.sqrt(HD)), cosine, sine)
            for tile in range(H // 2)
        ],
        axis=1,
    ).astype(BF)
    grad_keys = turn_pairs(jnp.where(low, dkv_ref[0], swap64(dkv_ref[1])), cosine, sine).astype(BF)
    grad_values = jnp.where(low, swap64(dkv_ref[0]), dkv_ref[1]).astype(BF)

    normed, attended = normed_ref[...], attended_ref[...]
    column = 0
    for left, right in (
        (normed, grad_queries),
        (normed, grad_keys),
        (normed, grad_values),
        (attended, grad_attn_ref[...]),
    ):
        product = dot_tn(left, right).astype(BF)
        for n in range(right.shape[1] // 128):
            table[column] = product[:, n * 128 : n * 128 + 128].reshape(4, SHARD, 128)
            column += 1
    beside = [
        links.push(table.at[:, 2 * n + 1 - c], table_in.at[n], sib) for n in range(2)
    ]

    inputs = tokens_ref[...].astype(F32)
    scale = lax.rsqrt(jnp.mean(inputs * inputs, axis=-1, keepdims=True) + EPSILON)

    def vector(row, count):
        return jnp.concatenate([small_all[n, row : row + 1, 0:count] for n in range(4)], axis=1)

    grad_normed = (
        dot_nt(grad_queries, wq_all[...].reshape(WIDTH, WIDTH))
        + dot_nt(grad_keys, wk_all[...].reshape(WIDTH, 128))
        + dot_nt(grad_values, wv_all[...].reshape(WIDTH, 128))
    )
    weighted = grad_normed * vector(1, SHARD)
    token_grad_ref[...] = (
        grad_middle_ref[...]
        + scale * weighted
        - inputs * (scale * scale * scale) * jnp.mean(weighted * inputs, axis=-1, keepdims=True)
    )
    thin[0, c] = jnp.concatenate(
        [
            jnp.sum(grad_queries.astype(F32), axis=0, keepdims=True),
            jnp.sum(grad_normed * inputs * scale, axis=0, keepdims=True),
            hidden_gain_ref[0:1],
            jnp.concatenate(
                [
                    jnp.sum(grad_keys.astype(F32), axis=0, keepdims=True),
                    jnp.sum(grad_values.astype(F32), axis=0, keepdims=True),
                    jnp.zeros((1, WIDTH - 256), F32),
                ],
                axis=1,
            ),
            jnp.zeros((4, WIDTH), F32),
        ],
        axis=0,
    )

    def thin_push(level, index, device):
        return links.push(thin.at[level, index], thin.at[level, index], device)

    thin_copies = [thin_push(0, c, sib)]

    for copy in keep + shared:
        copy.wait()
    spread = []
    for n in range(3):
        spread.append(
            links.push(whole_ref.at[x, z, 0:HALF], whole_ref.at[x, z, 0:HALF], on_z[n])
        )
        spread.append(
            links.push(whole_ref.at[x, z, HALF:UNIT], whole_ref.at[x, z, HALF:UNIT], on_x[n])
        )

    for copy in beside + thin_copies:
        copy.wait()

    def add_beside(n, _):
        for m in range(2):
            total = table[n, 2 * m + c].astype(F32) + table_in[m, n].astype(F32)
            lines[m, n] = total.astype(BF)
        return 0

    lax.fori_loop(0, 16, add_beside, 0)
    thin[1, x] = thin[0, 0] + thin[0, 1]
    along = []
    for n in range(3):
        xt, zt = turn(x, n + 1), turn(z, n + 1)
        along.append(links.push(lines.at[0, pl.ds(xt * 4, 4)], lines_in.at[0, n], on_x[n]))
        for m in range(4):
            along.append(
                links.push(lines.at[1, m * 4 + zt], lines_in.at[1, n, m], on_z[n])
            )
        along.append(thin_push(1, x, on_x[n]))
    for copy in along:
        copy.wait()
    for m in range(4):
        a = lines[0, x * 4 + m].astype(F32)
        b = lines[1, m * 4 + z].astype(F32)
        for n in range(3):
            a = a + lines_in[0, n, m].astype(F32)
            b = b + lines_in[1, n, m].astype(F32)
        cols[0, m] = a.astype(BF)
        cols[1, m] = b.astype(BF)
    thin[2, z] = (thin[1, 0] + thin[1, 1]) + (thin[1, 2] + thin[1, 3])
    along = []
    for n in range(3):
        along.append(links.push(cols.at[0, turn(z, n + 1)], cols_in.at[0, n], on_z[n]))
        along.append(links.push(cols.at[1, turn(x, n + 1)], cols_in.at[1, n], on_x[n]))
        along.append(thin_push(2, z, on_z[n]))
    for copy in along:
        copy.wait()
    a = cols[0, z].astype(F32)
    b = cols[1, x].astype(F32)
    for n in range(3):
        a = a + cols_in[0, n].astype(F32)
        b = b + cols_in[1, n].astype(F32)
    ends[0] = a.astype(BF)
    ends[1] = b.astype(BF)
    thin[3, yh] = (thin[2, 0] + thin[2, 1]) + (thin[2, 2] + thin[2, 3])
    along = [links.push(ends.at[1 - yh], ends_in.at[0], cross), thin_push(3, yh, cross)]
    for copy in along:
        copy.wait()
    ends[2] = (ends[yh].astype(F32) + ends_in[0].astype(F32)).astype(BF)
    thin[4, yl] = thin[3, 0] + thin[3, 1]
    along = [links.push(ends.at[2], ends_in.at[1], mate), thin_push(4, yl, mate)]
    for copy in along:
        copy.wait()
    late_ref[x, z] = (ends[2].astype(F32) + ends_in[1].astype(F32)).astype(BF)
    thin_ref[...] = thin[4, 0] + thin[4, 1]

    for copy in spread:
        copy.wait()
    cut = SHARD // 2
    last = []
    for n in range(3):
        last.append(links.push(late_ref.at[x, z, 0:cut], late_ref.at[x, z, 0:cut], on_z[n]))
        last.append(links.push(late_ref.at[x, z, cut:], late_ref.at[x, z, cut:], on_x[n]))
    spread = []
    for n in range(3):
        spread.append(links.push(whole_ref.at[x, :, 0:HALF], whole_ref.at[x, :, 0:HALF], on_x[n]))
        spread.append(
            links.push(whole_ref.at[:, z, HALF:UNIT], whole_ref.at[:, z, HALF:UNIT], on_z[n])
        )
    for copy in last:
        copy.wait()
    last = []
    for n in range(3):
        last.append(links.push(late_ref.at[x, :, 0:cut], late_ref.at[x, :, 0:cut], on_x[n]))
        last.append(links.push(late_ref.at[:, z, cut:], late_ref.at[:, z, cut:], on_z[n]))
    for copy in last + spread:
        copy.wait()


def last_call(*operands):
    shape = jax.ShapeDtypeStruct
    return pl.pallas_call(
        last_kernel,
        out_shape=[
            shape((ROWS, WIDTH), F32),
            shape((4, 4, SHARD, 128), BF),
            shape((8, WIDTH), F32),
            shape((4, 4, UNIT, 16, 128), BF),
        ],
        in_specs=[VMEM] * 15,
        out_specs=[VMEM] * 3 + [ANY],
        scratch_shapes=[
            pltpu.VMEM((KVH, LANES, 128), F32),
            pltpu.VMEM((16, 4, SHARD, 128), BF),
            pltpu.VMEM((2, 16, SHARD, 128), BF),
            pltpu.VMEM((2, 16, SHARD, 128), BF),
            pltpu.VMEM((2, 3, 4, SHARD, 128), BF),
            pltpu.VMEM((2, 4, SHARD, 128), BF),
            pltpu.VMEM((2, 3, SHARD, 128), BF),
            pltpu.VMEM((3, SHARD, 128), BF),
            pltpu.VMEM((2, SHARD, 128), BF),
            pltpu.VMEM((5, 4, 8, WIDTH), F32),
            pltpu.SemaphoreType.DMA((72,)),
            pltpu.SemaphoreType.DMA((72,)),
            pltpu.SemaphoreType.DMA((2,)),
        ],
        compiler_params=pltpu.CompilerParams(
            vmem_limit_bytes=58 * MIB, collective_id=2, has_side_effects=True
        ),
        name="last",
    )(*operands)


def tables(block_order, ctx):
    own_blocks = lax.dynamic_slice_in_dim(block_order, ctx * 2, 2)
    own_pos = (own_blocks[:, None] * BLK + jnp.arange(BLK, dtype=jnp.int32)[None, :]).reshape(ROWS)
    own_pos = own_pos.astype(F32)
    frequency = jnp.exp(jnp.arange(HD // 2, dtype=F32) * (-2.0 * math.log(THETA) / HD))
    angles = own_pos[:, None] * frequency[None, :]
    cosine, sine = jnp.cos(angles), jnp.sin(angles)
    cosine = jnp.concatenate([cosine] * 4, axis=1)
    sine = jnp.concatenate([-sine, sine] * 2, axis=1)
    slots = jnp.arange(64, dtype=jnp.int32)
    shown = (block_order[:, None] < own_blocks[None, :]) & (slots // 2 != ctx)[:, None]
    lane = jnp.arange(128)[None, :]
    bias = jnp.where(shown, 0.0, MASKED)
    extra = jnp.where(lane == 0, bias[:, 0:1], jnp.where(lane == 1, bias[:, 1:2], 0.0))
    extra = jnp.where((lane >= 2) & (lane < 5), 1.0, extra).astype(F32).reshape(2, 4, 4, 2, 128)
    extra = jnp.stack(
        [
            extra.transpose(1, 2, 0, 3, 4).reshape(64, 128),
            extra.transpose(2, 1, 0, 3, 4).reshape(64, 128),
        ]
    )
    kpos = jnp.pad(own_pos, (0, OWN - ROWS), constant_values=1e9)
    kpos = jnp.broadcast_to(kpos[:, None], (OWN, 128))
    qpos = jnp.pad(jnp.tile(own_pos, GROUP), (0, LANES - GROUP * ROWS), constant_values=5e8)
    qpos = jnp.broadcast_to(qpos[None, :], (8, LANES))
    return cosine, sine, extra, kpos, qpos


def by_head(rows):
    split = rows.reshape(ROWS, KVH, GROUP, HD).transpose(1, 2, 0, 3)
    return jnp.pad(split.reshape(KVH, GROUP * ROWS, HD), ((0, 0), (0, LANES - GROUP * ROWS), (0, 0)))


def body(
    tokens,
    block_order,
    query_weight,
    key_weight,
    value_weight,
    output_weight,
    gate_weight,
    up_weight,
    down_weight,
    query_bias,
    key_bias,
    value_bias,
    attention_gain,
    hidden_gain,
    cotangent,
):
    ctx, f = lax.axis_index("ctx"), lax.axis_index("fsdp")
    cosine, sine, extra, kpos, qpos = tables(block_order, ctx)

    def line(vector):
        return jnp.pad(vector.astype(F32), (0, 256 - vector.shape[0]))

    small = jnp.stack(
        [line(v) for v in (query_bias, attention_gain, hidden_gain, key_bias, value_bias)]
        + [jnp.zeros((256,), F32)] * 3
    )
    (
        attended,
        ot,
        lse,
        q,
        kv,
        normed,
        wq_all,
        wk_all,
        wv_all,
        small_all,
        wo_all,
        gate_all,
        up_all,
        cot_all,
    ) = front(
        tokens[0],
        query_weight,
        key_weight,
        value_weight,
        small,
        cosine,
        sine,
        extra,
        kpos,
        qpos,
        output_weight,
        gate_weight,
        up_weight,
        cotangent[0],
    )
    out_weight = wo_all.reshape(WIDTH, WIDTH)
    gate_cols = gate_all.reshape(WIDTH, WINDOW)
    up_cols = up_all.reshape(WIDTH, WINDOW)
    shift = 64 * (f % 2)
    down_rows = lax.dynamic_update_slice_in_dim(
        jnp.zeros((WINDOW, WIDTH), BF), down_weight, shift, axis=0
    )
    inputs = tokens[0].astype(F32)
    second_gain = small_all[:, 2, :SHARD].reshape(WIDTH)
    middle = inputs + dot(attended, out_weight)
    second_scale = lax.rsqrt(jnp.mean(middle * middle, axis=-1, keepdims=True) + EPSILON)
    normed_two = (middle * second_scale * second_gain).astype(BF)
    grad_out = cotangent[0].astype(F32)
    grad_all = lax.all_gather(cotangent[0], "fsdp", axis=0, tiled=True)
    normed_all = lax.all_gather(normed_two, "fsdp", axis=0, tiled=True)
    gate_pre = dot(normed_all, gate_cols)
    upward = dot(normed_all, up_cols)
    sigmoid = jax.nn.sigmoid(gate_pre)
    swish = gate_pre * sigmoid
    hidden = (swish * upward).astype(BF)
    out_part = dot(hidden, down_rows)
    output = middle + lax.psum_scatter(
        out_part.astype(BF), "fsdp", scatter_dimension=0, tiled=True
    ).astype(F32)
    grad_hidden = dot_nt(grad_all, down_rows)
    grad_gate = (grad_hidden * upward * sigmoid * (1.0 + gate_pre * (1.0 - sigmoid))).astype(BF)
    grad_up = (grad_hidden * swish).astype(BF)
    two_part = dot_nt(grad_gate, gate_cols) + dot_nt(grad_up, up_cols)
    grad_two = lax.psum_scatter(
        two_part.astype(BF), "fsdp", scatter_dimension=0, tiled=True
    ).astype(F32)
    gate_up_grad = dot_tn(normed_all, jnp.concatenate([grad_gate, grad_up], axis=1)).astype(BF)
    down_grad = lax.dynamic_slice_in_dim(dot_tn(hidden, grad_all), shift, UNITS).astype(BF)
    grads = gate_up_grad.reshape(4, 14, 16, 20, 128).transpose(0, 1, 3, 2, 4).reshape(4, 280, 16, 128)
    grads = jnp.pad(grads, ((0, 0), (0, 8), (0, 0), (0, 0))).reshape(4, 16, 18, 16, 128)
    grads = grads.transpose(1, 0, 2, 3, 4).reshape(16, 72, 16, 128)
    downs = down_grad.reshape(76, 16, 7, 128).transpose(0, 2, 1, 3).reshape(532, 16, 128)
    downs = jnp.pad(downs, ((0, 12), (0, 0), (0, 0))).reshape(16, 34, 16, 128)
    grads = jnp.concatenate([grads, downs], axis=1).reshape(4, 4, UNIT, 16, 128)

    hidden_gain_part = jnp.sum(grad_two * middle * second_scale, axis=0)
    weighted_two = grad_two * second_gain
    grad_middle = (
        grad_out
        + second_scale * weighted_two
        - middle
        * (second_scale * second_scale * second_scale)
        * jnp.mean(weighted_two * middle, axis=-1, keepdims=True)
    )
    grad_attn = grad_middle.astype(BF)
    grad_attended = by_head(dot_nt(grad_attn, out_weight).astype(BF))
    grad_attended = jnp.concatenate([jnp.zeros_like(grad_attended), grad_attended], axis=-1)
    dkv, dq, total = back(q, grad_attended, ot, lse, kv, extra, kpos, qpos, grads)
    token_grad, late, thin, whole = last_call(
        total,
        dq,
        dkv,
        cosine,
        sine,
        normed,
        attended,
        grad_attn,
        grad_middle,
        tokens[0],
        wq_all,
        wk_all,
        wv_all,
        small_all,
        jnp.broadcast_to(hidden_gain_part[None], (8, WIDTH)),
    )
    late = late.reshape(16, SHARD, 128).transpose(1, 0, 2).reshape(SHARD, 2048).astype(F32)
    whole = whole.reshape(16, UNIT, 16, 128)
    down_out = whole[:, 72:].reshape(544, 16, 128)[:532].reshape(76, 7, 16, 128)
    down_out = down_out.transpose(0, 2, 1, 3).reshape(UNITS, WIDTH).astype(F32)
    both = []
    for n in range(4):
        block = whole[:, 18 * n : 18 * n + 18].reshape(288, 16, 128)[:280].reshape(14, 20, 16, 128)
        block = block.transpose(0, 2, 1, 3).reshape(SHARD, 2 * WINDOW)
        start = 128 * ((19 * n) // 2)
        both.append(
            [
                jnp.pad(half, ((0, 0), (start, 4 * UNITS - WINDOW - start)))
                for half in (block[:, :WINDOW], block[:, WINDOW:])
            ]
        )
    gate_out, up_out = (
        ((both[0][n] + both[1][n]) + (both[2][n] + both[3][n])).astype(F32) for n in range(2)
    )
    wide, narrow = WIDTH, 128

    def share(row, start, count):
        part = count // 4
        return lax.dynamic_slice_in_dim(thin[row], start + f * part, part)

    return (
        output.astype(BF)[None],
        token_grad[None],
        late[:, :wide],
        late[:, wide : wide + narrow],
        late[:, wide + narrow : wide + 2 * narrow],
        late[:, wide + 2 * narrow :],
        gate_out,
        up_out,
        down_out,
        share(0, 0, wide),
        share(3, 0, narrow),
        share(3, narrow, narrow),
        share(1, 0, wide),
        share(2, 0, wide),
    )


def solution(mesh):
    rows = P("fsdp", "ctx", None)
    matrix = P("fsdp", None)
    vector = P("fsdp")
    placed = (rows, P()) + (matrix,) * 7 + (vector,) * 5 + (rows,)
    return jax.shard_map(
        body,
        mesh=mesh,
        in_specs=placed,
        out_specs=(rows, rows) + (matrix,) * 7 + (vector,) * 5,
        check_vma=False,
    )
```

time: 2490 us -> 496 us (0.20)
  waiting for transfers between devices: 1400 us -> 57.7 us
  matrix products: 469 us -> 40.6 us
  Pallas kernels: 0 us -> 298 us
  local copies, waits for them, and re-layouts: 334 us -> 53.3 us
  blocking collectives: 124 us -> 0 us
  other arithmetic: 116 us -> 23.4 us
    reduce_scatter x7 -> x2, waiting for transfers between devices: 538 us -> 23.7 us  [the longest x1 23.7 us: body(): lax.psum_scatter(out_part.astype(BF), 'fsdp', scatter_dimension=0, tiled=...]
    dot_general x237 -> x10, matrix products: 469 us -> 40.6 us  [the longest x4 17.5 us: dot(): return jnp.dot(left, right, preferred_element_type=F32)]
    unnamed x19 -> x4, waiting for transfers between devices: 312 us -> 0.74 us
    pallas_call x0 -> x3, Pallas kernels: none -> 298 us  [the longest x1 116 us: back(): pl.pallas_call(back_kernel, out_shape=[shape((KVH, ROWS, 128), F32), shap...]
    psum x1 -> x0, waiting for transfers between devices: 272 us -> none  [body(): lax.psum((shares[0], shares[1], shares[2], shares[3], shares[4], shares[5...]
    all_gather x7 -> x2, waiting for transfers between devices: 277 us -> 33.2 us  [the longest x1 19.9 us: body(): normed_all = lax.all_gather(normed_two, 'fsdp', axis=0, tiled=True)]
    dynamic_update_slice x96 -> x1, local copies, waits for them, and re-layouts: 187 us -> 1.97 us  [body(): lax.dynamic_update_slice_in_dim(jnp.zeros((WINDOW, WIDTH), BF), down_weig...]
    psum x1 -> x0, blocking collectives: 84.1 us -> none  [body(): lax.psum((shares[0], shares[1], shares[2], shares[3], shares[4], shares[5...]
  transfers between devices with their start and end apart: 17 -> 4, of which waited for: 13 -> 3; matrix products, arithmetic and copies ran while one was open for 13% -> 12% of each run, Pallas kernels for 0% -> 0%
where the time goes in v1:
time: 496 us; the launch traced here: 489 us
  Pallas kernels  298 us (60%)
  waiting for transfers between devices  57.7 us (12%)
  local copies, waits for them, and re-layouts  53.3 us (11%)
  matrix products  40.6 us (8%)
  other arithmetic  23.4 us (5%)
  between operations  14.7 us (3%)
    pallas_call x1, Pallas kernels, back(): pl.pallas_call(back_kernel, out_shape=[shape((KVH, ROWS, 128), F32), shap...  116 us
    pallas_call x1, Pallas kernels, last_call(): pl.pallas_call(last_kernel, out_shape=[shape((ROWS, WIDTH), F32), shape((...  95.2 us
    pallas_call x1, Pallas kernels, front(): pl.pallas_call(front_kernel, out_shape=[shape((ROWS, WIDTH), BF), shape((...  87.6 us
    reduce_scatter x1, waiting for transfers between devices, body(): lax.psum_scatter(out_part.astype(BF), 'fsdp', scatter_dimension=0, tiled=...  23.7 us
    all_gather x1, waiting for transfers between devices, body(): normed_all = lax.all_gather(normed_two, 'fsdp', axis=0, tiled=True)  19.9 us
    dot_general x4, matrix products, dot(): return jnp.dot(left, right, preferred_element_type=F32)  17.5 us
    all_gather x1, waiting for transfers between devices, body(): grad_all = lax.all_gather(cotangent[0], 'fsdp', axis=0, tiled=True)  13.3 us
    dot_general x4, matrix products, dot_nt(): return lax.dot_general(left, right, NT, preferred_element_type=F32)  13.3 us
  transfers between devices with their start and end apart: 4, of which 3 were waited for; matrix products, arithmetic and copies ran while one was open for 12% of the time, Pallas kernels for 0%

profile of v1, /device:TPU:8, one launch (start us, length us, event | category | flops | bytes accessed | tf_op | source)
XLA Modules:
  0.0 488.7 jit_solution(3594797838518615569)
XLA Ops:
  17.1 87.6 %front.1 = (bf16[192,896]{1,0:T(8,128)(2,1)}, f32[2,64,1408]{2,1,0:T(8,128)}, f32[2,8,1408]{2,1,0:T(8,128)}, bf16[2,1408,256]{2,1,0:T(8,128)(2,1)}, bf16[2,4,153...) custom-call(bf16[192,896]{1,0:T(8,128)(2,1)} %bitcast.164, ...), custom_call_target="tpu_custom_call" | custom-call | tf_op jit(solution)/shard_map/front/pallas_call | solution.py:362
  105.6 2.2 multiply_reduce_fusion
  113.0 19.9 %all-gather.4.cloned.1.call-done = bf16[768,896]{1,0:T(8,128)(2,1)} async-done(((bf16[192,896]{1,0:T(8,128)(2,1)}), bf16[768,896]{1,0:T(8,128)(2,1)}) %all-gather.4.cloned.1.call-update) | async-done | bytes 1376272 | tf_op jit(solution)/shard_map/all_gather | solution.py:1027
  132.9 6.3 %fusion.35 = f32[768,1280]{1,0:T(8,128)} fusion(bf16[768,896]{1,0:T(8,128)(2,1)} %all-gather.4.cloned.1.call-done, bf16[896,1280]{1,0:T(8,128)(2,1)} %bitcast.183), kind=kOutput, calls=%fused_computation.95 | convolution fusion | flops 1761607680 | bytes 7602176 | tf_op jit(solution)/shard_map/dot_general | solution.py:34
  139.2 4.1 fusion.36
  143.4 13.3 %all-gather.6.cloned.1.call-done = bf16[1,768,896]{2,1,0:T(8,128)(2,1)} async-done(((bf16[1,192,896]{2,1,0:T(8,128)(2,1)}), bf16[1,768,896]{2,1,0:T(8,128)(2,1)}) %all-gather.6.cloned.1.call-update) | async-done | bytes 1376272 | tf_op jit(solution)/shard_map/all_gather | solution.py:1026
  156.6 7.0 %fusion.6 = (bf16[768,1280]{1,0:T(8,128)(2,1)S(1)}, bf16[768,1280]{1,0:T(8,128)(2,1)S(1)}, bf16[768,1280]{1,0:T(8,128)(2,1)}) fusion(f32[768,1280]{1,0:T(8,128)} %fusion.35, f32[768,1280]{1,0:T(8,128)} %fusion.36, bf16[1280,896]{1,0:T(8,128)(2,1)S(1)} %constant_dynamic-update-slice_fusion, bf16[1,768,896]{2,1,0:T(8,128)(2,1)} %all-gather.6.cloned.1.call-done), kind=kOutput, calls=%fused_computation.13 | convolution fusion | flops 1776353280 | bytes 17432576 | tf_op jit(solution)/shard_map/dot_general | solution.py:38
  163.7 2.2 fusion.37
  166.7 3.4 add_convert_fusion
  170.2 4.8 convolution_convert_fusion.1
  175.0 4.2 fusion.8
  180.7 4.6 reshape.381
  188.8 5.7 %convolution_convert_fusion = bf16[896,2560]{1,0:T(8,128)(2,1)} fusion(bf16[768,896]{1,0:T(8,128)(2,1)S(1)} %copy-done.11, bf16[768,1280]{1,0:T(8,128)(2,1)S(1)} %copy-done.13, bf16[768,1280]{1,0:T(8,128)(2,1)S(1)} %copy-done.15), kind=kOutput, calls=%fused_computation.1 | convolution fusion | flops 3533373440 | bytes 9895936 | tf_op jit(solution)/shard_map/dot_general | solution.py:42
  194.4 8.8 %reshape.378 = bf16[4,14,16,20,128]{4,3,2,1,0:T(8,128)(2,1)} reshape(bf16[896,2560]{1,0:T(8,128)(2,1)} %convolution_convert_fusion) | data formatting | bytes 9175040 | tf_op jit(solution)/shard_map/reshape | solution.py:1046
  203.2 3.9 copy.59
  209.1 5.1 %pad_maximum_fusion.grads_ref = bf16[4,4,106,16,128]{4,3,2,1,0:T(8,128)(2,1)} fusion(bf16[4,4,34,16,128]{4,3,2,1,0:T(8,128)(2,1)} %bitcast.138, bf16[4,4,72,16,128]{4,3,2,1,0:T(8,128)(2,1)S(1)} %bitcast.134), kind=kLoop, calls=%fused_computation | loop fusion | flops 3473408 | bytes 13893632 | tf_op jit(solution)/shard_map/concatenate | solution.py:1051
  215.8 23.7 %reduce-scatter.3.cloned.1.call-done = bf16[192,896]{1,0:T(8,128)(2,1)} async-done(((bf16[768,896]{1,0:T(8,128)(2,1)}), bf16[192,896]{1,0:T(8,128)(2,1)}) %reduce-scatter.3.cloned.1.call-update) | async-done | bytes 344080 | tf_op jit(solution)/shard_map/reduce_scatter | solution.py:1034
  239.5 2.5 fusion.25
  244.4 115.6 %back.1 = (f32[2,192,128]{2,1,0:T(8,128)}, f32[2,64,1408]{2,1,0:T(8,128)}, bf16[106,16,128]{2,1,0:T(8,128)(2,1)}) custom-call(bf16[2,1408,256]{2,1,0:T(8,128)(2,1)} %get-tuple-element.39.q_ref, bf16[2,1408,128]{2,1,0:T(8,128)(2,1)} %pad.103.do_ref, f32[2,64,1408]{2,1,0:T(8,128)} %get-tuple-element.40.ot_ref, f32[2,8,1408]{2,1,0:T(8,128)} %get-tuple-element.41.lse_ref, ...), custom_call_target="tpu_custom_call" | custom-call | tf_op jit(solution)/shard_map/back/pallas_call | solution.py:616
  360.6 95.2 %last.1 = (f32[192,896]{1,0:T(8,128)}, bf16[4,4,224,128]{3,2,1,0:T(8,128)(2,1)}, f32[8,896]{1,0:T(8,128)}, bf16[4,4,106,16,128]{4,3,2,1,0:T(8,128)(2,1)}) custom-call(bf16[106,16,128]{2,1,0:T(8,128)(2,1)} %get-tuple-element.43.sum_ref, f32[2,64,1408]{2,1,0:T(8,128)} %get-tuple-element.44.dq_ref, f32[2,192,128]{2,1,0:T(8,128)} %get-tuple-element.45.dkv_ref, ...), custom_call_target="tpu_custom_call" | custom-call | tf_op jit(solution)/shard_map/last/pallas_call | solution.py:890
  459.2 3.2 fusion.27
  470.5 3.1 copy.81
  476.2 2.3 add_convert_fusion.2
  478.5 2.3 add_convert_fusion.1
  (125 shorter events, 42.9 us)
Async XLA Ops:
  7.2 125.7 %all-gather.4.cloned.1.call-start = ((), (), s32[]{:S(2)}) async-start(), calls=%async_computation.2 | async-start | bytes 1720320 | tf_op jit(solution)/shard_map/all_gather | solution.py:1027
  17.1 88.5 %copy-start.4 = (bf16[1,192,896]{2,1,0:T(8,128)(2,1)S(1)}, bf16[1,192,896]{2,1,0:T(8,128)(2,1)}, u32[]{:S(2)}) copy-start(bf16[1,192,896]{2,1,0:T(8,128)(2,1)} %param.15) | copy-start | bytes 1032196
  107.8 0.9 copy-start
  109.5 47.1 %all-gather.6.cloned.1.call-start = ((), (), s32[]{:S(2)}) async-start(), calls=%async_computation.5 | async-start | bytes 1720320 | tf_op jit(solution)/shard_map/all_gather | solution.py:1026
  110.3 103.9 %reduce-scatter.5.cloned.1.call-start = ((), (), s32[]{:S(2)}) async-start(), calls=%async_computation.4 | async-start | bytes 1720320 | tf_op jit(solution)/shard_map/reduce_scatter | solution.py:1041
  132.9 6.3 %copy-start.7 = (bf16[4,224,1280]{2,1,0:T(8,128)(2,1)S(1)}, bf16[4,224,1280]{2,1,0:T(8,128)(2,1)}, u32[]{:S(2)}) copy-start(bf16[4,224,1280]{2,1,0:T(8,128)(2,1)} %get-tuple-element.38) | copy-start | bytes 6881284
  132.9 6.3 %copy-start.10 = (bf16[768,896]{1,0:T(8,128)(2,1)S(1)}, bf16[768,896]{1,0:T(8,128)(2,1)}, u32[]{:S(2)}) copy-start(bf16[768,896]{1,0:T(8,128)(2,1)} %all-gather.4.cloned.1.call-done) | copy-start | bytes 4128772
  156.6 7.0 %copy-start.9 = (bf16[4,224,1280]{2,1,0:T(8,128)(2,1)S(1)}, bf16[4,224,1280]{2,1,0:T(8,128)(2,1)}, u32[]{:S(2)}) copy-start(bf16[4,224,1280]{2,1,0:T(8,128)(2,1)} %get-tuple-element.37) | copy-start | bytes 6881284
  163.6 2.2 copy-start.14
  163.7 2.3 copy-start.12
  163.7 3.1 copy-start.8
  170.1 69.4 %reduce-scatter.3.cloned.1.call-start = ((), (), s32[]{:S(2)}) async-start(), calls=%async_computation.3 | async-start | bytes 1720320 | tf_op jit(solution)/shard_map/reduce_scatter | solution.py:1034
  185.3 2.2 copy-start.15
  185.7 2.0 copy-start.11
  185.7 3.0 copy-start.13
  209.1 30.4 %copy-start.3 = (bf16[1,192,896]{2,1,0:T(8,128)(2,1)S(1)}, bf16[1,192,896]{2,1,0:T(8,128)(2,1)}, u32[]{:S(2)}) copy-start(bf16[1,192,896]{2,1,0:T(8,128)(2,1)} %param.29) | copy-start | bytes 1032196
  214.2 27.8 %copy-start.1 = (bf16[4,224,896]{2,1,0:T(8,128)(2,1)S(1)}, bf16[4,224,896]{2,1,0:T(8,128)(2,1)}, u32[]{:S(2)}) copy-start(bf16[4,224,896]{2,1,0:T(8,128)(2,1)} %get-tuple-element.35) | copy-start | bytes 4816900
  242.1 2.4 copy-start.2
  470.5 3.1 copy-start.6
  478.5 2.4 copy-start.5
Sparse Core Ops, SparseCore 0:
  109.7 23.1 all-gather.3
  134.6 22.0 all-gather.5
  170.2 33.2 reduce-scatter.4
  206.2 33.2 reduce-scatter.2

commit v2 on v1

--- a/solution.py
+++ b/solution.py
@@ -102,6 +102,47 @@
         copy = self.copy(src, dst, device, self.reserve(1))
         copy.start()
         return copy
+
+
+class RingSum:
+    def __init__(self, links, me, devices, chunk, relay, landing, staged):
+        self.links, self.me, self.devices, self.chunk = links, me, devices, chunk
+        self.relay, self.landing, self.staged = relay, landing, staged
+        self.base = links.reserve(6)
+
+    def copies(self, wanted):
+        me, right, left = self.me, self.devices[0], self.devices[2]
+        across, after, before = turn(me, 2), turn(me, 1), turn(me, 3)
+        chunk, landing, staged = self.chunk, self.landing, self.staged
+        moves = (
+            (chunk(across, 0), self.relay.at[0], right),
+            (chunk(across, 1), self.relay.at[1], left),
+            (chunk(after, 1), landing.at[0, 1], right),
+            (chunk(before, 0), landing.at[1, 0], left),
+            (staged.at[0], landing.at[0, 0], right),
+            (staged.at[1], landing.at[1, 1], left),
+        )
+        return [self.links.copy(*moves[n], self.base + n) for n in wanted]
+
+    def start(self):
+        for copy in self.copies((0, 1, 2, 3)):
+            copy.start()
+
+    def merge(self):
+        for n in range(2):
+            came, on = self.copies((n, 4 + n))
+            came.wait_recv()
+            self.staged[n] = (self.staged[n].astype(F32) + self.relay[n].astype(F32)).astype(BF)
+            on.start()
+
+    def finish(self):
+        for copy in self.copies((0, 1)):
+            copy.wait_send()
+        for copy in self.copies((2, 3, 4, 5)):
+            copy.wait()
+
+    def arrived(self, half):
+        return self.landing[0, half].astype(F32) + self.landing[1, half].astype(F32)
 
 
 def lanes_below(shape, bound):
@@ -226,12 +267,19 @@
     inputs = tokens_ref[...].astype(F32)
     scale = lax.rsqrt(jnp.mean(inputs * inputs, axis=-1, keepdims=True) + EPSILON)
     relays = gather_relay(first)
-    second = gather_start([(wo_ref, wo_all), (cot_ref, cot_all)])
+    def quarter(n, start):
+        rows = pl.ds(pl.multiple_of(lax.div(n, 2) * 112, 16), 112)
+        return rows, pl.ds(pl.multiple_of(start + lax.rem(n, 2) * 640, 128), 640)
+
     spread = []
+    for ref, whole, n in ((gate_ref, gate_all, x), (up_ref, up_all, z)):
+        rows, lanes = quarter(n, 0)
+        for device, index in ((cross, f_cross), (far, f_far)):
+            part = ref.at[quarter(n, window_start(index))]
+            spread.append(links.push(part, whole.at[f, rows, lanes], device))
     for ref, whole in ((gate_ref, gate_all), (up_ref, up_all)):
-        for device, index in ((cross, f_cross), (far, f_far), (sib, f_sib)):
-            part = ref.at[:, pl.ds(window_start(index), WINDOW)]
-            spread.append(links.push(part, whole.at[f], device))
+        part = ref.at[:, pl.ds(window_start(f_sib), WINDOW)]
+        spread.append(links.push(part, whole.at[f], sib))
     gather_end(first, relays)
 
     def vector(row, count):
@@ -316,7 +364,34 @@
     slabs = [slab_copy(g, d, slab_of[g]) for d in (1, 3, 2) for g in range(KVH)]
     for copy in slabs:
         copy.start()
-    relays = []
+    again = links.reserve(12)
+
+    def quarters():
+        copies = []
+        for whole, n, devices in ((gate_all, x, on_x), (up_all, z, on_z)):
+            rows, lanes = quarter(n, 0)
+            for index in (f_cross, f_far):
+                part = whole.at[index, rows, lanes]
+                copies += [
+                    links.copy(part, part, device, again + len(copies) + m)
+                    for m, device in enumerate(devices)
+                ]
+        return copies
+
+    second = links.reserve(4)
+
+    def outer():
+        copies = []
+        for mine, whole in ((wo_ref, wo_all), (cot_ref, cot_all)):
+            for device in (sib, cross):
+                copies.append(links.copy(mine, whole.at[f], device, second + len(copies)))
+        return copies
+
+    def spread_on():
+        for copy in spread[0:4]:
+            copy.wait_recv()
+        for copy in quarters() + outer():
+            copy.start()
 
     def step(i, _):
         g, n = lax.rem(i, 2), lax.div(i, 2)
@@ -330,11 +405,14 @@
         rows = extra_ref[g, pl.ds(pl.multiple_of(slab * 16, 16), 16), :]
         keys = jnp.concatenate([kv_ref[g, slab], key_extra(rows)], axis=1)
         mix(g, keys, dot_nt(keys, q_ref[g]))
+        pl.when(i == 0)(spread_on)
         return 0
 
     lax.fori_loop(0, 8, step, 0)
     for copy in slabs:
         copy.wait_send()
+    outers = outer()
+    second = list(zip(outers[0::2], outers[1::2], (wo_all, cot_all)))
     relays = gather_relay(second)
 
     for g in range(KVH):
@@ -350,7 +428,9 @@
         attended_ref[:, tile * 128 : tile * 128 + 128] = jnp.where(
             low, left, swap64(right)
         ).astype(BF)
-    for copy in spread:
+    for copy in spread[0:4]:
+        copy.wait_send()
+    for copy in spread[4:] + quarters():
         copy.wait()
     gather_end(second, relays)
     for copy in keep:
@@ -384,8 +464,8 @@
             pltpu.VMEM((KVH, 72, LANES), F32),
             pltpu.VMEM((KVH, 8, LANES), F32),
             pltpu.VMEM((KVH, LANES, 128), F32),
-            pltpu.SemaphoreType.DMA((48,)),
-            pltpu.SemaphoreType.DMA((48,)),
+            pltpu.SemaphoreType.DMA((64,)),
+            pltpu.SemaphoreType.DMA((64,)),
             pltpu.SemaphoreType.DMA((4,)),
         ],
         compiler_params=pltpu.CompilerParams(
@@ -395,8 +475,283 @@
     )(tokens, wq, wk, wv, small, cosine, sine, extra, kpos, qpos, wo, gate, up, cot)
 
 
+def tile_stores(ref, value, first_row, first_lane, place_of):
+    for r in range(value.shape[0] // 16):
+        for n in range(value.shape[1] // 128):
+            p, k = place_of(first_row + r, first_lane + n)
+            ref[p // 4, p % 4, k] = value[r * 16 : r * 16 + 16, n * 128 : n * 128 + 128]
+
+
+def gate_place(r, n):
+    t = (r % 14) * 20 + n
+    return t // 18, 18 * (r // 14) + t % 18
+
+
+def down_place(r, n):
+    t = r * 7 + n
+    return t // 34, t % 34
+
+
+def middle_kernel(
+    attended_ref,
+    tokens_ref,
+    small_all,
+    wo_all,
+    cot_all,
+    gate_hbm,
+    up_hbm,
+    down_hbm,
+    output_ref,
+    grad_middle_ref,
+    grad_attn_ref,
+    gain_ref,
+    do_ref,
+    grads_ref,
+    sum_a_ref,
+    sum_b_ref,
+    gate_ref,
+    up_ref,
+    down_ref,
+    blocks,
+    back_gate,
+    hidden_ref,
+    down_grad,
+    two,
+    two_in,
+    out,
+    out_in,
+    downs,
+    relay,
+    landing,
+    staged,
+    send,
+    recv,
+    local,
+):
+    yl, x, z, yh, c = place()
+    f = yh * 2 + c
+    f_cross = (1 - yh) * 2 + c
+    f_sib = yh * 2 + 1 - c
+    f_far = (1 - yh) * 2 + 1 - c
+    sib = at(yl, x, z, yh, 1 - c)
+    cross = at(1 - yl, x, z, 1 - yh, c)
+    links = Links(send, recv)
+    loads = [
+        pltpu.make_async_copy(gate_hbm, gate_ref, local.at[0]),
+        pltpu.make_async_copy(up_hbm, up_ref, local.at[1]),
+        pltpu.make_async_copy(
+            down_hbm, down_ref.at[pl.ds(pl.multiple_of(64 * c, 64), UNITS)], local.at[2]
+        ),
+    ]
+    for copy in loads:
+        copy.start()
+    down_ref[pl.ds(pl.multiple_of((1 - c) * UNITS, 64), 64), :] = jnp.zeros((64, WIDTH), BF)
+    on_x = [at(yl, turn(x, d), z, yh, c) for d in (1, 2, 3)]
+    on_z = [at(yl, x, turn(z, d), yh, c) for d in (1, 2, 3)]
+    greet([sib, cross, on_x[0], on_x[2], on_z[0], on_z[2]])
+    rings = (
+        RingSum(
+            links,
+            x,
+            on_x,
+            lambda n, half: downs.at[n, 2 * half : 2 * half + 2, 0:17],
+            relay.at[0],
+            landing.at[0],
+            staged.at[0],
+        ),
+        RingSum(
+            links,
+            z,
+            on_z,
+            lambda n, half: downs.at[2 * half : 2 * half + 2, n, 17:34],
+            relay.at[1],
+            landing.at[1],
+            staged.at[1],
+        ),
+    )
+
+    gain = jnp.concatenate([small_all[n, 2:3, 0:SHARD] for n in range(4)], axis=1)
+    wo = wo_all[...].reshape(WIDTH, WIDTH)
+    middle = tokens_ref[...].astype(F32) + dot(attended_ref[...], wo)
+    scale = lax.rsqrt(jnp.mean(middle * middle, axis=-1, keepdims=True) + EPSILON)
+    grad_middle_ref[...] = middle
+    blocks[0] = (middle * scale * gain).astype(BF)
+    beside = links.push(blocks.at[0], blocks.at[1], sib)
+    over = links.push(blocks.at[0], blocks.at[2], cross)
+    order = ((f, f_sib), (f_cross, f_far))
+    for copy in loads:
+        copy.wait()
+
+    def grads_of(p):
+        return jnp.concatenate([cot_all[order[p][0]], cot_all[order[p][1]]], axis=0)
+
+    def hidden_grad(p):
+        return dot_nt(grads_of(p), down_ref[...])
+
+    def units(p, grad_hidden):
+        rows = slice(p * 2 * ROWS, (p + 1) * 2 * ROWS)
+        block = blocks[2 * p : 2 * p + 2].reshape(2 * ROWS, WIDTH)
+        gate_pre = dot(block, gate_ref[...].reshape(WIDTH, WINDOW))
+        upward = dot(block, up_ref[...].reshape(WIDTH, WINDOW))
+        sigmoid = 1.0 / (1.0 + jnp.exp(-gate_pre))
+        swish = gate_pre * sigmoid
+        hidden_ref[rows] = (swish * upward).astype(BF)
+        back_gate[rows, 0:WINDOW] = (
+            grad_hidden * upward * sigmoid * (1.0 + gate_pre * (1.0 - sigmoid))
+        ).astype(BF)
+        back_gate[rows, WINDOW:] = (grad_hidden * swish).astype(BF)
+
+    def two_part(p):
+        rows = slice(p * 2 * ROWS, (p + 1) * 2 * ROWS)
+        return dot_nt(back_gate[rows, 0:WINDOW], gate_ref[...].reshape(WIDTH, WINDOW)) + dot_nt(
+            back_gate[rows, WINDOW:], up_ref[...].reshape(WIDTH, WINDOW)
+        )
+
+    def out_part(p):
+        rows = slice(p * 2 * ROWS, (p + 1) * 2 * ROWS)
+        return dot(hidden_ref[rows], down_ref[...])
+
+    beside.wait()
+    units(0, hidden_grad(0))
+    part = two_part(0)
+    two_mine = part[0:ROWS]
+    two[0] = part[ROWS:].astype(BF)
+    two_copies = [links.push(two.at[0], two_in.at[0], sib)]
+    far_grad = hidden_grad(1)
+    over.wait()
+    relay = links.push(blocks.at[2], blocks.at[3], sib)
+    relay.wait()
+    units(1, far_grad)
+    part = two_part(1)
+    two[1] = part[ROWS:].astype(BF)
+    copy = links.push(two.at[1], two_in.at[1], sib)
+    two_cross = part[0:ROWS]
+    part = out_part(1)
+    out[1] = part[ROWS:].astype(BF)
+    copy.wait()
+    two[2] = (two_cross + two_in[1].astype(F32)).astype(BF)
+    two_copies.append(links.push(two.at[2], two_in.at[2], cross))
+    copy = links.push(out.at[1], out_in.at[1], sib)
+    out_cross = part[0:ROWS]
+    part = out_part(0)
+    out_mine = part[0:ROWS]
+    out[0] = part[ROWS:].astype(BF)
+    out_copies = [links.push(out.at[0], out_in.at[0], sib)]
+    copy.wait()
+    out[2] = (out_cross + out_in[1].astype(F32)).astype(BF)
+    out_copies.append(links.push(out.at[2], out_in.at[2], cross))
+
+    down_grad[...] = dot_tn(
+        hidden_ref[...], jnp.concatenate([grads_of(0), grads_of(1)], axis=0)
+    ).astype(BF)
+    blank = jnp.zeros((16, 128), BF)
+    product = down_grad[pl.ds(pl.multiple_of(64 * c, 64), UNITS), :]
+    tile_stores(downs, product, 0, 0, down_place)
+    for t in range(532, 544):
+        downs[3, 3, t % 34] = blank
+    for ring in rings:
+        ring.start()
+    staged[0, 0] = downs[turn(x, 1), 0:2, 0:17]
+    staged[0, 1] = downs[turn(x, 3), 2:4, 0:17]
+    staged[1, 0] = downs[0:2, turn(z, 1), 17:34]
+    staged[1, 1] = downs[2:4, turn(z, 3), 17:34]
+    block = blocks[...].reshape(4 * ROWS, WIDTH)
+    for n in range(0, 2 * WINDOW, 512):
+        product = dot_tn(block, back_gate[:, n : n + 512]).astype(BF)
+        tile_stores(grads_ref, product, 0, n // 128, gate_place)
+        if n == 1536:
+            for ring in rings:
+                ring.merge()
+    for n in range(4):
+        for t in range(280, 288):
+            grads_ref[3, 3, 18 * n + t % 18] = blank
+
+    for copy in two_copies:
+        copy.wait()
+    grad_two = two_mine + two_in[0].astype(F32) + two_in[2].astype(F32)
+    middle = grad_middle_ref[...]
+    scale = lax.rsqrt(jnp.mean(middle * middle, axis=-1, keepdims=True) + EPSILON)
+    weighted = grad_two * gain
+    grad_middle = (
+        cot_all[f].astype(F32)
+        + scale * weighted
+        - middle * (scale * scale * scale) * jnp.mean(weighted * middle, axis=-1, keepdims=True)
+    )
+    gain_ref[...] = jnp.broadcast_to(
+        jnp.sum(grad_two * middle * scale, axis=0, keepdims=True), (8, WIDTH)
+    )
+    grad_attn = grad_middle.astype(BF)
+    grad_attn_ref[...] = grad_attn
+    grad_middle_ref[...] = grad_middle
+    grad_attended = dot_nt(grad_attn, wo_all[...].reshape(WIDTH, WIDTH)).astype(BF).astype(F32)
+    low = lanes_below((ROWS, 128), 64)
+    for tile in range(H // 2):
+        part = grad_attended[:, tile * 128 : tile * 128 + 128]
+        for half in range(2):
+            head = tile * 2 + half
+            j = head % GROUP
+            mine = swap64(part) if half == 0 else part
+            do_ref[head // GROUP, j * ROWS : (j + 1) * ROWS] = jnp.where(low, 0.0, mine).astype(BF)
+    for g in range(KVH):
+        do_ref[g, GROUP * ROWS :] = jnp.zeros((LANES - GROUP * ROWS, 128), BF)
+    for copy in out_copies:
+        copy.wait()
+    total = out_mine + out_in[0].astype(F32) + out_in[2].astype(F32)
+    output_ref[...] = (middle + total).astype(BF)
+    for ring in rings:
+        ring.finish()
+    for half in range(2):
+        two_of = slice(2 * half, 2 * half + 2)
+        sum_a_ref[two_of] = (downs[x, two_of, 0:17].astype(F32) + rings[0].arrived(half)).astype(BF)
+        sum_b_ref[two_of] = (downs[two_of, z, 17:34].astype(F32) + rings[1].arrived(half)).astype(BF)
+
+
+def middle_call(*operands):
+    shape = jax.ShapeDtypeStruct
+    return pl.pallas_call(
+        middle_kernel,
+        out_shape=[
+            shape((ROWS, WIDTH), BF),
+            shape((ROWS, WIDTH), F32),
+            shape((ROWS, WIDTH), BF),
+            shape((8, WIDTH), F32),
+            shape((KVH, LANES, 128), BF),
+            shape((4, 4, 72, 16, 128), BF),
+            shape((4, 17, 16, 128), BF),
+            shape((4, 17, 16, 128), BF),
+        ],
+        in_specs=[VMEM] * 5 + [ANY] * 3,
+        out_specs=[VMEM] * 8,
+        scratch_shapes=[
+            pltpu.VMEM((4, SHARD, WINDOW), BF),
+            pltpu.VMEM((4, SHARD, WINDOW), BF),
+            pltpu.VMEM((WINDOW, WIDTH), BF),
+            pltpu.VMEM((4, ROWS, WIDTH), BF),
+            pltpu.VMEM((4 * ROWS, 2 * WINDOW), BF),
+            pltpu.VMEM((4 * ROWS, WINDOW), BF),
+            pltpu.VMEM((WINDOW, WIDTH), BF),
+            pltpu.VMEM((3, ROWS, WIDTH), BF),
+            pltpu.VMEM((3, ROWS, WIDTH), BF),
+            pltpu.VMEM((3, ROWS, WIDTH), BF),
+            pltpu.VMEM((3, ROWS, WIDTH), BF),
+            pltpu.VMEM((4, 4, 34, 16, 128), BF),
+            pltpu.VMEM((2, 2, 2, 17, 16, 128), BF),
+            pltpu.VMEM((2, 2, 2, 2, 17, 16, 128), BF),
+            pltpu.VMEM((2, 2, 2, 17, 16, 128), BF),
+            pltpu.SemaphoreType.DMA((24,)),
+            pltpu.SemaphoreType.DMA((24,)),
+            pltpu.SemaphoreType.DMA((3,)),
+        ],
+        compiler_params=pltpu.CompilerParams(
+            vmem_limit_bytes=60 * MIB, collective_id=3, has_side_effects=True
+        ),
+        name="middle",
+    )(*operands)
+
+
 UNIT = 106
 HALF = 53
+UPPER = 36
 CHUNK = 768
 
 
@@ -413,6 +768,8 @@
     extra_ref,
     kpos_ref,
     qpos_ref,
+    down_a_ref,
+    down_b_ref,
     grads_ref,
     dkv_ref,
     dq_ref,
@@ -429,8 +786,9 @@
     single_in,
     side_a,
     side_b,
-    in_a,
-    in_b,
+    relay,
+    landing,
+    staged,
     late_a,
     late_b,
     whole,
@@ -447,20 +805,44 @@
     links = Links(send, recv)
     greet([mate] + on_x + on_z)
 
-    first = []
-    for n in range(3):
-        first.append(
-            links.push(grads_ref.at[turn(x, n + 1), :, 0:HALF], in_a.at[n], on_x[n])
+    rings = (
+        RingSum(
+            links,
+            x,
+            on_x,
+            lambda n, half: grads_ref.at[n, 2 * half : 2 * half + 2, 0:UPPER],
+            relay.at[0],
+            landing.at[0],
+            staged.at[0],
+        ),
+        RingSum(
+            links,
+            z,
+            on_z,
+            lambda n, half: grads_ref.at[2 * half : 2 * half + 2, n, UPPER : 2 * UPPER],
+            relay.at[1],
+            landing.at[1],
+            staged.at[1],
+        ),
+    )
+    for ring in rings:
+        ring.start()
+
+    def keep():
+        moves = (
+            (grads_ref.at[turn(x, 1), 0:2, 0:UPPER], staged.at[0, 0]),
+            (grads_ref.at[turn(x, 3), 2:4, 0:UPPER], staged.at[0, 1]),
+            (grads_ref.at[0:2, turn(z, 1), UPPER : 2 * UPPER], staged.at[1, 0]),
+            (grads_ref.at[2:4, turn(z, 3), UPPER : 2 * UPPER], staged.at[1, 1]),
+            (grads_ref.at[x, :, 0:UPPER], side_a.at[:, 0:UPPER]),
+            (grads_ref.at[:, z, UPPER : 2 * UPPER], side_b.at[:, 0:UPPER]),
         )
-        first.append(
-            links.push(grads_ref.at[:, turn(z, n + 1), HALF:UNIT], in_b.at[n], on_z[n])
-        )
-    keep = [
-        pltpu.make_async_copy(grads_ref.at[x, :, 0:HALF], side_a, local.at[0]),
-        pltpu.make_async_copy(grads_ref.at[:, z, HALF:UNIT], side_b, local.at[1]),
-    ]
-    for copy in keep:
+        return [pltpu.make_async_copy(*move, local.at[n]) for n, move in enumerate(moves)]
+
+    for copy in keep():
         copy.start()
+    side_a[:, UPPER:HALF] = down_a_ref[...]
+    side_b[:, UPPER:HALF] = down_b_ref[...]
 
     row = lax.broadcasted_iota(jnp.int32, (128, LANES), 0)
     for g in range(KVH):
@@ -510,9 +892,9 @@
         return links.copy(parts.at[g, slab], parts_in.at[g, d - 1], device, base + n)
 
     def step(i, _):
-        g = lax.div(i, SLABS * count)
-        d = lax.rem(lax.rem(lax.div(i, count), SLABS) + 1, 4)
-        part = lax.rem(i, count)
+        n, part = lax.div(i, count), lax.rem(i, count)
+        g = lax.rem(n, 2)
+        d = lax.rem(lax.div(n, 2) + 1, 4)
         slab = turn(jnp.where(g == 0, x, z), d)
         start = pl.multiple_of(part * CHUNK, CHUNK)
         rows = extra_ref[g, pl.ds(pl.multiple_of(slab * 16 + part * 8, 8), 8), :]
@@ -525,9 +907,28 @@
         def _():
             part_copy(g, d, slab).start()
 
+        for at_step, event in events:
+            pl.when(i == at_step)(event)
         return 0
 
-    pair_copies = []
+    pair_base, single_base, second_base, third_slot = (
+        links.reserve(6),
+        links.reserve(2),
+        links.reserve(6),
+        links.reserve(1),
+    )
+
+    def pair_copies(g):
+        other, devices = (z, x)[g], (on_z, on_x)[g]
+        return [
+            links.copy(
+                pairs.at[g, turn(other, n + 1)],
+                pairs_in.at[g, n],
+                devices[n],
+                pair_base + 3 * g + n,
+            )
+            for n in range(3)
+        ]
 
     def pair_start(g):
         slab = slab_of[g]
@@ -539,53 +940,60 @@
             for m in range(3):
                 total = total + parts_in[g, m, rows, :].astype(F32)
             pairs[g, n] = total.astype(BF)
-        other = (z, x)[g]
-        devices = (on_z, on_x)[g]
-        return [
-            links.push(pairs.at[g, turn(other, n + 1)], pairs_in.at[g, n], devices[n])
-            for n in range(3)
-        ]
-
-    def single_start(g, copies):
-        for copy in copies:
+        for copy in pair_copies(g):
+            copy.start()
+
+    def single_copy(g):
+        return links.copy(single_in.at[g, 0], single_in.at[g, 1], mate, single_base + g)
+
+    def single_start(g):
+        for copy in pair_copies(g):
             copy.wait()
         total = pairs[g, (z, x)[g]].astype(F32)
         for m in range(3):
             total = total + pairs_in[g, m].astype(F32)
         single[g, 0] = total[0:ROWS]
         single[g, 1] = total[ROWS:]
-        low = jnp.where(yl == 0, total[ROWS:], total[0:ROWS])
-        single_low = low.astype(BF)
-        single_in[g, 0] = single_low
-        return links.push(single_in.at[g, 0], single_in.at[g, 1], mate)
-
-    def single_end(g, copy):
-        copy.wait()
+        single_in[g, 0] = jnp.where(yl == 0, total[ROWS:], total[0:ROWS]).astype(BF)
+        single_copy(g).start()
+
+    def single_end(g):
+        single_copy(g).wait()
         dkv_ref[g] = single[g, yl] + single_in[g, 1].astype(F32) + own_grad[g]
 
-    def second_start():
-        for copy in keep + first:
+    def merge():
+        for copy in keep():
             copy.wait()
-
-        def add(n, _):
-            a = side_a[n].astype(F32)
-            b = side_b[n].astype(F32)
-            for m in range(3):
-                a = a + in_a[m, n].astype(F32)
-                b = b + in_b[m, n].astype(F32)
-            side_a[n] = a.astype(BF)
-            side_b[n] = b.astype(BF)
-            return 0
-
-        lax.fori_loop(0, 4, add, 0)
+        for ring in rings:
+            ring.merge()
+
+    def second_copies():
         copies = []
         for n in range(3):
-            copies.append(links.push(side_a.at[turn(z, n + 1)], late_a.at[n], on_z[n]))
-            copies.append(links.push(side_b.at[turn(x, n + 1)], late_b.at[n], on_x[n]))
+            for source, target, index, device in (
+                (side_a, late_a, turn(z, n + 1), on_z[n]),
+                (side_b, late_b, turn(x, n + 1), on_x[n]),
+            ):
+                copies.append(
+                    links.copy(source.at[index], target.at[n], device, second_base + len(copies))
+                )
         return copies
 
-    def third_start(copies):
-        for copy in copies:
+    def second_start():
+        for side, ring in zip((side_a, side_b), rings):
+            ring.finish()
+            for half in range(2):
+                rows = slice(2 * half, 2 * half + 2)
+                total = side[rows, 0:UPPER].astype(F32) + ring.arrived(half)
+                side[rows, 0:UPPER] = total.astype(BF)
+        for copy in second_copies():
+            copy.start()
+
+    def third():
+        return links.copy(whole, whole_in, mate, third_slot)
+
+    def third_start():
+        for copy in second_copies():
             copy.wait()
         a = side_a[z].astype(F32)
         b = side_b[x].astype(F32)
@@ -594,24 +1002,25 @@
             b = b + late_b[m].astype(F32)
         whole[0:HALF] = a.astype(BF)
         whole[HALF:UNIT] = b.astype(BF)
-        return links.push(whole, whole_in, mate)
-
-    steps = SLABS * count
-    lax.fori_loop(0, steps, step, 0)
-    pair_copies = pair_start(0)
-    lax.fori_loop(steps, 2 * steps, step, 0)
-    single_copy = single_start(0, pair_copies)
-    second = second_start()
-    pair_copies = pair_start(1)
-    single_end(0, single_copy)
-    third = third_start(second)
-    single_copy = single_start(1, pair_copies)
-    single_end(1, single_copy)
-    third.wait()
+        third().start()
+
+    events = (
+        (3, merge),
+        (9, second_start),
+        (13, lambda: pair_start(0)),
+        (14, third_start),
+    )
+    lax.fori_loop(0, KVH * SLABS * count, step, 0)
+    pair_start(1)
+    single_start(0)
+    single_end(0)
+    single_start(1)
+    single_end(1)
+    third().wait()
     sum_ref[...] = (whole[...].astype(F32) + whole_in[...].astype(F32)).astype(BF)
 
 
-def back(q, do, ot, lse, kv, extra, kpos, qpos, grads):
+def back(q, do, ot, lse, kv, extra, kpos, qpos, down_a, down_b, grads):
     shape = jax.ShapeDtypeStruct
     return pl.pallas_call(
         back_kernel,
@@ -620,7 +1029,7 @@
             shape((KVH, HD, LANES), F32),
             shape((UNIT, 16, 128), BF),
         ],
-        in_specs=[VMEM] * 8 + [ANY],
+        in_specs=[VMEM] * 10 + [ANY],
         out_specs=[VMEM] * 3,
         scratch_shapes=[
             pltpu.VMEM((KVH, LANES, 256), BF),
@@ -635,21 +1044,22 @@
             pltpu.VMEM((KVH, 2, ROWS, 128), BF),
             pltpu.VMEM((4, HALF, 16, 128), BF),
             pltpu.VMEM((4, HALF, 16, 128), BF),
-            pltpu.VMEM((3, 4, HALF, 16, 128), BF),
-            pltpu.VMEM((3, 4, HALF, 16, 128), BF),
+            pltpu.VMEM((2, 2, 2, UPPER, 16, 128), BF),
+            pltpu.VMEM((2, 2, 2, 2, UPPER, 16, 128), BF),
+            pltpu.VMEM((2, 2, 2, UPPER, 16, 128), BF),
             pltpu.VMEM((3, HALF, 16, 128), BF),
             pltpu.VMEM((3, HALF, 16, 128), BF),
             pltpu.VMEM((UNIT, 16, 128), BF),
             pltpu.VMEM((UNIT, 16, 128), BF),
             pltpu.SemaphoreType.DMA((48,)),
             pltpu.SemaphoreType.DMA((48,)),
-            pltpu.SemaphoreType.DMA((2,)),
+            pltpu.SemaphoreType.DMA((6,)),
         ],
         compiler_params=pltpu.CompilerParams(
             vmem_limit_bytes=62 * MIB, collective_id=1, has_side_effects=True
         ),
         name="back",
-    )(q, do, ot, lse, kv, extra, kpos, qpos, grads)
+    )(q, do, ot, lse, kv, extra, kpos, qpos, down_a, down_b, grads)
 
 
 def last_kernel(
@@ -701,19 +1111,17 @@
     greet([sib, cross, far, mate] + on_x + on_z)
 
     shared = []
+
+    def spot(index):
+        return pl.ds(18 * index + 17 * lax.div(index, 2), 18)
+
     for device, index in ((sib, f_sib), (cross, f_cross), (far, f_far)):
         shared.append(
-            links.push(
-                sum_ref.at[pl.ds(18 * index, 18)], whole_ref.at[x, z, pl.ds(18 * f, 18)], device
-            )
+            links.push(sum_ref.at[spot(index)], whole_ref.at[x, z, spot(f)], device)
         )
     keep = [
-        pltpu.make_async_copy(
-            sum_ref.at[pl.ds(18 * f, 18)], whole_ref.at[x, z, pl.ds(18 * f, 18)], local.at[0]
-        ),
-        pltpu.make_async_copy(
-            sum_ref.at[72:UNIT], whole_ref.at[x, z, 72:UNIT], local.at[1]
-        ),
+        pltpu.make_async_copy(sum_ref.at[part], whole_ref.at[x, z, part], local.at[n])
+        for n, part in enumerate((spot(f), slice(UPPER, HALF), slice(HALF + UPPER, UNIT)))
     ]
     for copy in keep:
         copy.start()
@@ -737,6 +1145,17 @@
     ).astype(BF)
     grad_keys = turn_pairs(jnp.where(low, dkv_ref[0], swap64(dkv_ref[1])), cosine, sine).astype(BF)
     grad_values = jnp.where(low, swap64(dkv_ref[0]), dkv_ref[1]).astype(BF)
+
+    for copy in keep + shared:
+        copy.wait()
+    spread = []
+    for n in range(3):
+        spread.append(
+            links.push(whole_ref.at[x, z, 0:HALF], whole_ref.at[x, z, 0:HALF], on_z[n])
+        )
+        spread.append(
+            links.push(whole_ref.at[x, z, HALF:UNIT], whole_ref.at[x, z, HALF:UNIT], on_x[n])
+        )
 
     normed, attended = normed_ref[...], attended_ref[...]
     column = 0
@@ -794,17 +1213,16 @@
 
     thin_copies = [thin_push(0, c, sib)]
 
-    for copy in keep + shared:
-        copy.wait()
-    spread = []
-    for n in range(3):
-        spread.append(
-            links.push(whole_ref.at[x, z, 0:HALF], whole_ref.at[x, z, 0:HALF], on_z[n])
+    for copy in spread:
+        copy.wait()
+    rounds = []
+    for n in (0, 2):
+        rounds.append(
+            links.push(whole_ref.at[x, :, 0:HALF], whole_ref.at[x, :, 0:HALF], on_x[n])
         )
-        spread.append(
-            links.push(whole_ref.at[x, z, HALF:UNIT], whole_ref.at[x, z, HALF:UNIT], on_x[n])
+        rounds.append(
+            links.push(whole_ref.at[:, z, HALF:UNIT], whole_ref.at[:, z, HALF:UNIT], on_z[n])
         )
-
     for copy in beside + thin_copies:
         copy.wait()
 
@@ -862,26 +1280,26 @@
     late_ref[x, z] = (ends[2].astype(F32) + ends_in[1].astype(F32)).astype(BF)
     thin_ref[...] = thin[4, 0] + thin[4, 1]
 
-    for copy in spread:
-        copy.wait()
     cut = SHARD // 2
-    last = []
+    along = []
     for n in range(3):
-        last.append(links.push(late_ref.at[x, z, 0:cut], late_ref.at[x, z, 0:cut], on_z[n]))
-        last.append(links.push(late_ref.at[x, z, cut:], late_ref.at[x, z, cut:], on_x[n]))
-    spread = []
+        along.append(links.push(late_ref.at[x, z, 0:cut], late_ref.at[x, z, 0:cut], on_z[n]))
+        along.append(links.push(late_ref.at[x, z, cut:], late_ref.at[x, z, cut:], on_x[n]))
+    for copy in rounds:
+        copy.wait()
+    rounds = []
+    for half, came, n in ((0, 3, 0), (1, 1, 2)):
+        rows = slice(2 * half, 2 * half + 2)
+        a = whole_ref.at[turn(x, came), rows, 0:HALF]
+        b = whole_ref.at[rows, turn(z, came), HALF:UNIT]
+        rounds += [links.push(a, a, on_x[n]), links.push(b, b, on_z[n])]
+    for copy in along:
+        copy.wait()
+    along = []
     for n in range(3):
-        spread.append(links.push(whole_ref.at[x, :, 0:HALF], whole_ref.at[x, :, 0:HALF], on_x[n]))
-        spread.append(
-            links.push(whole_ref.at[:, z, HALF:UNIT], whole_ref.at[:, z, HALF:UNIT], on_z[n])
-        )
-    for copy in last:
-        copy.wait()
-    last = []
-    for n in range(3):
-        last.append(links.push(late_ref.at[x, :, 0:cut], late_ref.at[x, :, 0:cut], on_x[n]))
-        last.append(links.push(late_ref.at[:, z, cut:], late_ref.at[:, z, cut:], on_z[n]))
-    for copy in last + spread:
+        along.append(links.push(late_ref.at[x, :, 0:cut], late_ref.at[x, :, 0:cut], on_x[n]))
+        along.append(links.push(late_ref.at[:, z, cut:], late_ref.at[:, z, cut:], on_z[n]))
+    for copy in along + rounds:
         copy.wait()
 
 
@@ -910,13 +1328,118 @@
             pltpu.VMEM((5, 4, 8, WIDTH), F32),
             pltpu.SemaphoreType.DMA((72,)),
             pltpu.SemaphoreType.DMA((72,)),
-            pltpu.SemaphoreType.DMA((2,)),
+            pltpu.SemaphoreType.DMA((3,)),
         ],
         compiler_params=pltpu.CompilerParams(
             vmem_limit_bytes=58 * MIB, collective_id=2, has_side_effects=True
         ),
         name="last",
     )(*operands)
+
+
+def finish_kernel(
+    late_ref,
+    thin_ref,
+    whole_ref,
+    q_out,
+    k_out,
+    v_out,
+    o_out,
+    gate_out,
+    up_out,
+    down_out,
+    qb_out,
+    kb_out,
+    vb_out,
+    ag_out,
+    hg_out,
+    q_val,
+    k_val,
+    v_val,
+    o_val,
+    gate_val,
+    up_val,
+    down_val,
+    sems,
+):
+    copies = []
+
+    def leave(value, out):
+        copy = pltpu.make_async_copy(value, out, sems.at[len(copies)])
+        copy.start()
+        copies.append(copy)
+
+    def gate_tile(n, r, lane):
+        t = r * 20 + lane
+        p, k = t // 18, 18 * n + 17 * (n // 2) + t % 18
+        return whole_ref[p // 4, p % 4, k].astype(F32)
+
+    for value, out, first in ((gate_val, gate_out, 0), (up_val, up_out, 10)):
+        for r in range(14):
+            for tile in range(38):
+                parts = []
+                for n in range(4):
+                    lane = tile - (19 * n) // 2
+                    if 0 <= lane < 10:
+                        parts.append(gate_tile(n, r, first + lane))
+                total = parts[0] if len(parts) == 1 else parts[0] + parts[1]
+                value[r * 16 : r * 16 + 16, tile * 128 : tile * 128 + 128] = total
+        leave(value, out)
+    for r in range(76):
+        for tile in range(7):
+            t = r * 7 + tile
+            p, k = t // 34, t % 34
+            k = UPPER + k if k < 17 else HALF + UPPER + k - 17
+            down_val[r * 16 : r * 16 + 16, tile * 128 : tile * 128 + 128] = whole_ref[
+                p // 4, p % 4, k
+            ].astype(F32)
+    leave(down_val, down_out)
+    column = 0
+    for value, out, count in ((q_val, q_out, 7), (k_val, k_out, 1), (v_val, v_out, 1), (o_val, o_out, 7)):
+        for tile in range(count):
+            value[:, tile * 128 : tile * 128 + 128] = late_ref[column // 4, column % 4].astype(F32)
+            column += 1
+        leave(value, out)
+    f = lax.axis_index("fsdp")
+
+    def share(row, start, part):
+        total = thin_ref[row : row + 1, start : start + part]
+        for n in range(1, 4):
+            first = start + n * part
+            total = jnp.where(f == n, thin_ref[row : row + 1, first : first + part], total)
+        return total
+
+    qb_out[...] = share(0, 0, SHARD)
+    kb_out[...] = share(3, 0, 32)
+    vb_out[...] = share(3, 128, 32)
+    ag_out[...] = share(1, 0, SHARD)
+    hg_out[...] = share(2, 0, SHARD)
+    for copy in copies:
+        copy.wait()
+
+
+def finish(late, thin, whole):
+    shape = jax.ShapeDtypeStruct
+    large = [
+        (SHARD, WIDTH),
+        (SHARD, 128),
+        (SHARD, 128),
+        (SHARD, WIDTH),
+        (SHARD, 4 * UNITS),
+        (SHARD, 4 * UNITS),
+        (UNITS, WIDTH),
+    ]
+    tiny = [(1, SHARD), (1, 32), (1, 32), (1, SHARD), (1, SHARD)]
+    return pl.pallas_call(
+        finish_kernel,
+        out_shape=[shape(size, F32) for size in large + tiny],
+        in_specs=[VMEM] * 3,
+        out_specs=[ANY] * 7 + [VMEM] * 5,
+        scratch_shapes=[pltpu.VMEM(size, F32) for size in large]
+        + [pltpu.SemaphoreType.DMA((7,))],
+        compiler_params=pltpu.CompilerParams(vmem_limit_bytes=58 * MIB),
+        name="finish",
+    )(late, thin, whole)
 
 
 def tables(block_order, ctx):
@@ -947,11 +1470,6 @@
     return cosine, sine, extra, kpos, qpos
 
 
-def by_head(rows):
-    split = rows.reshape(ROWS, KVH, GROUP, HD).transpose(1, 2, 0, 3)
-    return jnp.pad(split.reshape(KVH, GROUP * ROWS, HD), ((0, 0), (0, LANES - GROUP * ROWS), (0, 0)))
-
-
 def body(
     tokens,
     block_order,
@@ -969,7 +1487,7 @@
     hidden_gain,
     cotangent,
 ):
-    ctx, f = lax.axis_index("ctx"), lax.axis_index("fsdp")
+    ctx = lax.axis_index("ctx")
     cosine, sine, extra, kpos, qpos = tables(block_order, ctx)
 
     def line(vector):
@@ -1010,59 +1528,21 @@
         up_weight,
         cotangent[0],
     )
-    out_weight = wo_all.reshape(WIDTH, WIDTH)
-    gate_cols = gate_all.reshape(WIDTH, WINDOW)
-    up_cols = up_all.reshape(WIDTH, WINDOW)
-    shift = 64 * (f % 2)
-    down_rows = lax.dynamic_update_slice_in_dim(
-        jnp.zeros((WINDOW, WIDTH), BF), down_weight, shift, axis=0
-    )
-    inputs = tokens[0].astype(F32)
-    second_gain = small_all[:, 2, :SHARD].reshape(WIDTH)
-    middle = inputs + dot(attended, out_weight)
-    second_scale = lax.rsqrt(jnp.mean(middle * middle, axis=-1, keepdims=True) + EPSILON)
-    normed_two = (middle * second_scale * second_gain).astype(BF)
-    grad_out = cotangent[0].astype(F32)
-    grad_all = lax.all_gather(cotangent[0], "fsdp", axis=0, tiled=True)
-    normed_all = lax.all_gather(normed_two, "fsdp", axis=0, tiled=True)
-    gate_pre = dot(normed_all, gate_cols)
-    upward = dot(normed_all, up_cols)
-    sigmoid = jax.nn.sigmoid(gate_pre)
-    swish = gate_pre * sigmoid
-    hidden = (swish * upward).astype(BF)
-    out_part = dot(hidden, down_rows)
-    output = middle + lax.psum_scatter(
-        out_part.astype(BF), "fsdp", scatter_dimension=0, tiled=True
-    ).astype(F32)
-    grad_hidden = dot_nt(grad_all, down_rows)
-    grad_gate = (grad_hidden * upward * sigmoid * (1.0 + gate_pre * (1.0 - sigmoid))).astype(BF)
-    grad_up = (grad_hidden * swish).astype(BF)
-    two_part = dot_nt(grad_gate, gate_cols) + dot_nt(grad_up, up_cols)
-    grad_two = lax.psum_scatter(
-        two_part.astype(BF), "fsdp", scatter_dimension=0, tiled=True
-    ).astype(F32)
-    gate_up_grad = dot_tn(normed_all, jnp.concatenate([grad_gate, grad_up], axis=1)).astype(BF)
-    down_grad = lax.dynamic_slice_in_dim(dot_tn(hidden, grad_all), shift, UNITS).astype(BF)
-    grads = gate_up_grad.reshape(4, 14, 16, 20, 128).transpose(0, 1, 3, 2, 4).reshape(4, 280, 16, 128)
-    grads = jnp.pad(grads, ((0, 0), (0, 8), (0, 0), (0, 0))).reshape(4, 16, 18, 16, 128)
-    grads = grads.transpose(1, 0, 2, 3, 4).reshape(16, 72, 16, 128)
-    downs = down_grad.reshape(76, 16, 7, 128).transpose(0, 2, 1, 3).reshape(532, 16, 128)
-    downs = jnp.pad(downs, ((0, 12), (0, 0), (0, 0))).reshape(16, 34, 16, 128)
-    grads = jnp.concatenate([grads, downs], axis=1).reshape(4, 4, UNIT, 16, 128)
-
-    hidden_gain_part = jnp.sum(grad_two * middle * second_scale, axis=0)
-    weighted_two = grad_two * second_gain
-    grad_middle = (
-        grad_out
-        + second_scale * weighted_two
-        - middle
-        * (second_scale * second_scale * second_scale)
-        * jnp.mean(weighted_two * middle, axis=-1, keepdims=True)
-    )
-    grad_attn = grad_middle.astype(BF)
-    grad_attended = by_head(dot_nt(grad_attn, out_weight).astype(BF))
-    grad_attended = jnp.concatenate([jnp.zeros_like(grad_attended), grad_attended], axis=-1)
-    dkv, dq, total = back(q, grad_attended, ot, lse, kv, extra, kpos, qpos, grads)
+    (
+        output,
+        grad_middle,
+        grad_attn,
+        hidden_gain_part,
+        grad_attended,
+        grads,
+        down_a,
+        down_b,
+    ) = middle_call(
+        attended, tokens[0], small_all, wo_all, cot_all, gate_all, up_all, down_weight
+    )
+    dkv, dq, total = back(
+        q, grad_attended, ot, lse, kv, extra, kpos, qpos, down_a, down_b, grads
+    )
     token_grad, late, thin, whole = last_call(
         total,
         dq,
@@ -1078,48 +1558,10 @@
         wk_all,
         wv_all,
         small_all,
-        jnp.broadcast_to(hidden_gain_part[None], (8, WIDTH)),
-    )
-    late = late.reshape(16, SHARD, 128).transpose(1, 0, 2).reshape(SHARD, 2048).astype(F32)
-    whole = whole.reshape(16, UNIT, 16, 128)
-    down_out = whole[:, 72:].reshape(544, 16, 128)[:532].reshape(76, 7, 16, 128)
-    down_out = down_out.transpose(0, 2, 1, 3).reshape(UNITS, WIDTH).astype(F32)
-    both = []
-    for n in range(4):
-        block = whole[:, 18 * n : 18 * n + 18].reshape(288, 16, 128)[:280].reshape(14, 20, 16, 128)
-        block = block.transpose(0, 2, 1, 3).reshape(SHARD, 2 * WINDOW)
-        start = 128 * ((19 * n) // 2)
-        both.append(
-            [
-                jnp.pad(half, ((0, 0), (start, 4 * UNITS - WINDOW - start)))
-                for half in (block[:, :WINDOW], block[:, WINDOW:])
-            ]
-        )
-    gate_out, up_out = (
-        ((both[0][n] + both[1][n]) + (both[2][n] + both[3][n])).astype(F32) for n in range(2)
-    )
-    wide, narrow = WIDTH, 128
-
-    def share(row, start, count):
-        part = count // 4
-        return lax.dynamic_slice_in_dim(thin[row], start + f * part, part)
-
-    return (
-        output.astype(BF)[None],
-        token_grad[None],
-        late[:, :wide],
-        late[:, wide : wide + narrow],
-        late[:, wide + narrow : wide + 2 * narrow],
-        late[:, wide + 2 * narrow :],
-        gate_out,
-        up_out,
-        down_out,
-        share(0, 0, wide),
-        share(3, 0, narrow),
-        share(3, narrow, narrow),
-        share(1, 0, wide),
-        share(2, 0, wide),
-    )
+        hidden_gain_part,
+    )
+    ends = finish(late, thin, whole)
+    return (output[None], token_grad[None], *ends[:7], *(end.reshape(-1) for end in ends[7:]))
 
 
 def solution(mesh):

time: 496 us -> 313 us (0.63)
  waiting for transfers between devices: 57.7 us -> 0 us
  local copies, waits for them, and re-layouts: 53.3 us -> 4.5 us
  matrix products: 40.6 us -> 0 us
  other arithmetic: 23.4 us -> 6.9 us
  between operations: 14.7 us -> 1.26 us
    pallas_call x0 -> x2, Pallas kernels: none -> 62.3 us  [the longest x1 52.6 us: middle_call(): pl.pallas_call(middle_kernel, out_shape=[shape((ROWS, WIDTH), BF), shape(...]
    pallas_call x1, Pallas kernels: 116 us -> 72.4 us  [back(): pl.pallas_call(back_kernel, out_shape=[shape((KVH, ROWS, 128), F32), shap...]
    dot_general x10 -> x0, matrix products: 40.6 us -> none  [the longest x4 17.5 us: dot(): return jnp.dot(left, right, preferred_element_type=F32)]
    all_gather x2 -> x0, waiting for transfers between devices: 33.2 us -> none  [the longest x1 19.9 us: body(): normed_all = lax.all_gather(normed_two, 'fsdp', axis=0, tiled=True)]
    reduce_scatter x2 -> x0, waiting for transfers between devices: 23.7 us -> none  [the longest x1 23.7 us: body(): lax.psum_scatter(out_part.astype(BF), 'fsdp', scatter_dimension=0, tiled=...]
    pallas_call x1, Pallas kernels: 87.6 us -> 73.2 us  [front(): pl.pallas_call(front_kernel, out_shape=[shape((ROWS, WIDTH), BF), shape((...]
    reshape x2 -> x0, local copies, waits for them, and re-layouts: 13.3 us -> none  [the longest x1 8.75 us: body(): gate_up_grad.reshape(4, 14, 16, 20, 128).transpose(0, 1, 3, 2, 4)]
    convert_element_type x6 -> x0, other arithmetic: 9.81 us -> none  [the longest x2 4.7 us: body(): (both[0][n] + both[1][n] + (both[2][n] + both[3][n])).astype(F32)]
  transfers between devices with their start and end apart: 4 -> 0, of which waited for: 3 -> 0; matrix products, arithmetic and copies ran while one was open for 12% -> 0% of each run, Pallas kernels for 0% -> 0%
where the time goes in v2:
time: 313 us; the launch traced here: 307 us
  Pallas kernels  294 us (94%)
  other arithmetic  6.9 us (2%)
  local copies, waits for them, and re-layouts  4.5 us (1%)
    pallas_call x1, Pallas kernels, last_call(): pl.pallas_call(last_kernel, out_shape=[shape((ROWS, WIDTH), F32), shape((...  86.4 us
    pallas_call x1, Pallas kernels, front(): pl.pallas_call(front_kernel, out_shape=[shape((ROWS, WIDTH), BF), shape((...  73.2 us
    pallas_call x1, Pallas kernels, back(): pl.pallas_call(back_kernel, out_shape=[shape((KVH, ROWS, 128), F32), shap...  72.4 us
    pallas_call x1, Pallas kernels, middle_call(): pl.pallas_call(middle_kernel, out_shape=[shape((ROWS, WIDTH), BF), shape(...  52.6 us
    pallas_call x1, Pallas kernels, finish(): pl.pallas_call(finish_kernel, out_shape=[shape(size, F32) for size in lar...  9.72 us

profile of v2, /device:TPU:8, one launch (start us, length us, event | category | flops | bytes accessed | tf_op | source)
XLA Modules:
  0.0 307.0 jit_solution(1218656230640462838)
XLA Ops:
  0.7 0.7 broadcast_multiply_fusion
  1.6 0.7 and_select_fusion
  2.3 0.7 pad_convert_fusion.4
  3.0 0.7 pad_convert_fusion.1
  3.7 0.7 pad_convert_fusion
  4.3 0.7 pad_convert_fusion.3
  5.0 0.7 pad_convert_fusion.2
  5.7 0.6 stack.50.small_ref
  6.5 0.1 broadcast_in_dim.122
  6.6 0.1 broadcast_in_dim.124
  6.8 0.1 broadcast_in_dim.131
  6.9 0.1 broadcast_in_dim.119
  7.1 0.6 broadcast_in_dim.134.qpos_ref
  7.9 0.6 pad_maximum_fusion.2.extra_ref
  8.5 0.8 broadcast_in_dim.133.kpos_ref
  9.2 0.4 fusion
  9.7 0.9 pad_maximum_fusion
  10.6 73.2 %front.1 = (bf16[192,896]{1,0:T(8,128)(2,1)}, f32[2,64,1408]{2,1,0:T(8,128)}, f32[2,8,1408]{2,1,0:T(8,128)}, bf16[2,1408,256]{2,1,0:T(8,128)(2,1)}, bf16[2,4,153...) custom-call(bf16[192,896]{1,0:T(8,128)(2,1)} %bitcast.18, ...), custom_call_target="tpu_custom_call" | custom-call | tf_op jit(solution)/shard_map/front/pallas_call | solution.py:442
  83.8 52.6 %middle.1 = (bf16[192,896]{1,0:T(8,128)(2,1)}, f32[192,896]{1,0:T(8,128)}, bf16[192,896]{1,0:T(8,128)(2,1)}, f32[8,896]{1,0:T(8,128)}, bf16[2,1408,128]{2,1,0:T(...) custom-call(bf16[192,896]{1,0:T(8,128)(2,1)} %get-tuple-element.55.a, ...), custom_call_target="tpu_custom_call" | custom-call | tf_op jit(solution)/shard_map/middle/pallas_call | solution.py:711
  136.4 72.4 %back.1 = (f32[2,192,128]{2,1,0:T(8,128)}, f32[2,64,1408]{2,1,0:T(8,128)}, bf16[106,16,128]{2,1,0:T(8,128)(2,1)}) custom-call(bf16[2,1408,256]{2,1,0:T(8,128)(2,1)} %get-tuple-element.62.q_ref, bf16[2,1408,128]{2,1,0:T(8,128)(2,1)} %get-tuple-element.63.do_ref, f32[2,64,1408]{2,1,0:T(8,128)} %get-tuple-element.64.ot_ref, ...), custom_call_target="tpu_custom_call" | custom-call | tf_op jit(solution)/shard_map/back/pallas_call | solution.py:1025
  208.8 86.4 %last.1 = (f32[192,896]{1,0:T(8,128)}, bf16[4,4,224,128]{3,2,1,0:T(8,128)(2,1)}, f32[8,896]{1,0:T(8,128)}, bf16[4,4,106,16,128]{4,3,2,1,0:T(8,128)(2,1)}) custom-call(bf16[106,16,128]{2,1,0:T(8,128)(2,1)} %get-tuple-element.70.sum_ref, f32[2,64,1408]{2,1,0:T(8,128)} %get-tuple-element.71.dq_ref, f32[2,192,128]{2,1,0:T(8,128)} %get-tuple-element.72.dkv_ref, ...), custom_call_target="tpu_custom_call" | custom-call | tf_op jit(solution)/shard_map/last/pallas_call | solution.py:1308
  295.2 9.7 %finish.1 = (f32[224,896]{1,0:T(8,128)}, f32[224,128]{1,0:T(8,128)}, f32[224,128]{1,0:T(8,128)}, f32[224,896]{1,0:T(8,128)}, f32[224,4864]{1,0:T(8,128)}, /*inde...) custom-call(bf16[4,4,224,128]{3,2,1,0:T(8,128)(2,1)} %get-tuple-elem, ...), custom_call_target="tpu_custom_call" | custom-call | tf_op jit(solution)/shard_map/finish/pallas_call | solution.py:1433
  305.0 0.7 copy.39
  305.7 0.8 copy.40
  (24 shorter events, 0.7 us)
Async XLA Ops:
  295.2 9.8 %copy-start.1 = (bf16[192,896]{1,0:T(8,128)(2,1)S(1)}, bf16[192,896]{1,0:T(8,128)(2,1)}, u32[]{:S(2)}) copy-start(bf16[192,896]{1,0:T(8,128)(2,1)} %get-tuple-element.61) | copy-start | bytes 1032196
  295.2 10.5 %copy-start = (f32[192,896]{1,0:T(8,128)S(1)}, f32[192,896]{1,0:T(8,128)}, u32[]{:S(2)}) copy-start(f32[192,896]{1,0:T(8,128)} %get-tuple-element.80) | copy-start | bytes 2064388

commit v3 on v2

--- a/solution.py
+++ b/solution.py
@@ -1,8 +1,8 @@
-import functools
 import math
 
 import jax
 import jax.numpy as jnp
+import numpy as np
 from jax import lax
 from jax.experimental import pallas as pl
 from jax.experimental.pallas import tpu as pltpu
@@ -175,17 +175,60 @@
     return pl.multiple_of(lax.div(19 * f, 2) * 128, 128)
 
 
+def tables(order_ref, token_angle, block_angle, cos_ref, sin_ref, extra_ref, kpos_ref, qpos_ref):
+    ctx = lax.axis_index("ctx")
+    mine = [order_ref[2 * ctx], order_ref[2 * ctx + 1]]
+    lane = lax.broadcasted_iota(jnp.int32, (BLK, 128), 1)
+    sign = jnp.where(lax.rem(lane, 64) < 32, -1.0, 1.0)
+    for n in range(2):
+        rows = slice(n * BLK, (n + 1) * BLK)
+        cosine, sine = block_angle[0, pl.ds(mine[n], 1), :], block_angle[1, pl.ds(mine[n], 1), :]
+        cos_ref[rows] = token_angle[0] * cosine - token_angle[1] * sine
+        sin_ref[rows] = (token_angle[1] * cosine + token_angle[0] * sine) * sign
+    lane = lax.broadcasted_iota(jnp.int32, (1, 128), 1)
+    ones = jnp.where((lane >= 2) & (lane < 5), 1.0, 0.0)
+    for slot in range(64):
+        block = order_ref[slot]
+        other = slot // 2 != ctx
+        row = ones
+        for n in range(2):
+            shown = jnp.where((block < mine[n]) & other, 0.0, MASKED)
+            row = jnp.where(lane == n, shown, row)
+        yl, x, z, n = slot // 32, slot // 8 % 4, slot // 2 % 4, slot % 2
+        for g, spot in enumerate((((x * 4 + z) * 2 + yl) * 2 + n, ((z * 4 + x) * 2 + yl) * 2 + n)):
+            extra_ref[g, spot : spot + 1, :] = row
+
+    def position(index):
+        block = jnp.where(index < BLK, mine[0], mine[1])
+        return (block * BLK + lax.rem(index, BLK)).astype(F32)
+
+    row = lax.broadcasted_iota(jnp.int32, (OWN, 128), 0)
+    kpos_ref[...] = jnp.where(row < ROWS, position(row), 1e9)
+    lane = lax.broadcasted_iota(jnp.int32, (8, LANES), 1)
+    qpos_ref[...] = jnp.where(lane < GROUP * ROWS, position(lax.rem(lane, ROWS)), 5e8)
+
+
+def angle_tables():
+    lane = np.arange(128) % 32
+    frequency = np.exp(lane * (-2.0 * math.log(THETA) / HD))
+    token = np.arange(BLK)[:, None] * frequency
+    block = np.arange(64)[:, None] * BLK * frequency
+    return [np.stack([np.cos(a), np.sin(a)]).astype(np.float32) for a in (token, block)]
+
+
 def front_kernel(
     tokens_ref,
     wq_ref,
     wk_ref,
     wv_ref,
-    small_ref,
-    cos_ref,
-    sin_ref,
-    extra_ref,
-    kpos_ref,
-    qpos_ref,
+    qb_ref,
+    ag_ref,
+    hg_ref,
+    kb_ref,
+    vb_ref,
+    order_ref,
+    token_angle_ref,
+    block_angle_ref,
     wo_ref,
     gate_ref,
     up_ref,
@@ -200,6 +243,11 @@
     wk_all,
     wv_all,
     small_all,
+    cos_ref,
+    sin_ref,
+    extra_ref,
+    kpos_ref,
+    qpos_ref,
     wo_all,
     gate_all,
     up_all,
@@ -246,24 +294,25 @@
         for relay in relays:
             relay.wait()
 
-    first = gather_start(
-        [(wq_ref, wq_all), (wk_ref, wk_all), (wv_ref, wv_all), (small_ref, small_all)]
+    first = gather_start([(wq_ref, wq_all), (wk_ref, wk_all), (wv_ref, wv_all)])
+    small_all[f] = jnp.zeros((8, 256), F32)
+    for row, (ref, count) in enumerate(
+        ((qb_ref, SHARD), (ag_ref, SHARD), (hg_ref, SHARD), (kb_ref, 32), (vb_ref, 32))
+    ):
+        small_all[f, row : row + 1, 0:count] = ref[...].astype(F32)
+    first += gather_start([(small_all.at[f], small_all)])
+    keep = [
+        pltpu.make_async_copy(mine, whole.at[f], local.at[n])
+        for n, (mine, whole) in enumerate(((wo_ref, wo_all), (cot_ref, cot_all)))
+    ]
+    for copy in keep:
+        copy.start()
+    tables(
+        order_ref, token_angle_ref, block_angle_ref, cos_ref, sin_ref, extra_ref, kpos_ref, qpos_ref
     )
-    keep = []
-    for n, (mine, whole) in enumerate(
-        [(wo_ref, wo_all.at[f]), (cot_ref, cot_all.at[f])]
-        + [
-            (ref.at[:, pl.ds(window_start(f), WINDOW)], whole.at[f])
-            for ref, whole in ((gate_ref, gate_all), (up_ref, up_all))
-        ]
-    ):
-        copy = pltpu.make_async_copy(mine, whole, local.at[n])
-        copy.start()
-        keep.append(copy)
     wq_all[f] = wq_ref[...]
     wk_all[f] = wk_ref[...]
     wv_all[f] = wv_ref[...]
-    small_all[f] = small_ref[...]
     inputs = tokens_ref[...].astype(F32)
     scale = lax.rsqrt(jnp.mean(inputs * inputs, axis=-1, keepdims=True) + EPSILON)
     relays = gather_relay(first)
@@ -361,9 +410,9 @@
         )
         return links.copy(kv_ref.at[g, slab], kv_ref.at[g, slab], device, base + g * 3 + d - 1)
 
-    slabs = [slab_copy(g, d, slab_of[g]) for d in (1, 3, 2) for g in range(KVH)]
-    for copy in slabs:
-        copy.start()
+    for d in (1, 3):
+        for g in range(KVH):
+            slab_copy(g, d, slab_of[g]).start()
     again = links.reserve(12)
 
     def quarters():
@@ -387,6 +436,10 @@
                 copies.append(links.copy(mine, whole.at[f], device, second + len(copies)))
         return copies
 
+    def slabs_on():
+        for g in range(KVH):
+            slab_copy(g, 2, slab_of[g]).start()
+
     def spread_on():
         for copy in spread[0:4]:
             copy.wait_recv()
@@ -405,12 +458,14 @@
         rows = extra_ref[g, pl.ds(pl.multiple_of(slab * 16, 16), 16), :]
         keys = jnp.concatenate([kv_ref[g, slab], key_extra(rows)], axis=1)
         mix(g, keys, dot_nt(keys, q_ref[g]))
-        pl.when(i == 0)(spread_on)
+        pl.when(i == 1)(slabs_on)
+        pl.when(i == 3)(spread_on)
         return 0
 
     lax.fori_loop(0, 8, step, 0)
-    for copy in slabs:
-        copy.wait_send()
+    for d in (1, 2, 3):
+        for g in range(KVH):
+            slab_copy(g, d, slab_of[g]).wait_send()
     outers = outer()
     second = list(zip(outers[0::2], outers[1::2], (wo_all, cot_all)))
     relays = gather_relay(second)
@@ -437,8 +492,9 @@
         copy.wait()
 
 
-def front(tokens, wq, wk, wv, small, cosine, sine, extra, kpos, qpos, wo, gate, up, cot):
+def front(*operands):
     shape = jax.ShapeDtypeStruct
+    scalars = pl.BlockSpec(memory_space=pltpu.SMEM)
     return pl.pallas_call(
         front_kernel,
         out_shape=[
@@ -452,13 +508,18 @@
             shape((4, SHARD, 128), BF),
             shape((4, SHARD, 128), BF),
             shape((4, 8, 256), F32),
+            shape((ROWS, 128), F32),
+            shape((ROWS, 128), F32),
+            shape((KVH, 64, 128), F32),
+            shape((OWN, 128), F32),
+            shape((8, LANES), F32),
             shape((4, SHARD, WIDTH), BF),
             shape((4, SHARD, WINDOW), BF),
             shape((4, SHARD, WINDOW), BF),
             shape((4, ROWS, WIDTH), BF),
         ],
-        in_specs=[VMEM] * 10 + [ANY] * 4,
-        out_specs=[VMEM] * 10 + [ANY] * 4,
+        in_specs=[VMEM] * 9 + [scalars] + [VMEM] * 2 + [ANY] * 4,
+        out_specs=[VMEM] * 15 + [ANY] * 4,
         scratch_shapes=[
             pltpu.VMEM((KVH, OWN, 128), BF),
             pltpu.VMEM((KVH, 72, LANES), F32),
@@ -472,7 +533,7 @@
             vmem_limit_bytes=58 * MIB, collective_id=0, has_side_effects=True
         ),
         name="front",
-    )(tokens, wq, wk, wv, small, cosine, sine, extra, kpos, qpos, wo, gate, up, cot)
+    )(*operands)
 
 
 def tile_stores(ref, value, first_row, first_lane, place_of):
@@ -500,6 +561,8 @@
     cot_all,
     gate_hbm,
     up_hbm,
+    gate_own,
+    up_own,
     down_hbm,
     output_ref,
     grad_middle_ref,
@@ -536,13 +599,19 @@
     sib = at(yl, x, z, yh, 1 - c)
     cross = at(1 - yl, x, z, 1 - yh, c)
     links = Links(send, recv)
+    window = pl.ds(window_start(f), WINDOW)
     loads = [
-        pltpu.make_async_copy(gate_hbm, gate_ref, local.at[0]),
-        pltpu.make_async_copy(up_hbm, up_ref, local.at[1]),
         pltpu.make_async_copy(
-            down_hbm, down_ref.at[pl.ds(pl.multiple_of(64 * c, 64), UNITS)], local.at[2]
+            down_hbm, down_ref.at[pl.ds(pl.multiple_of(64 * c, 64), UNITS)], local.at[0]
         ),
+        pltpu.make_async_copy(gate_own.at[:, window], gate_ref.at[f], local.at[1]),
+        pltpu.make_async_copy(up_own.at[:, window], up_ref.at[f], local.at[2]),
     ]
+    for n, index in enumerate((f_sib, f_cross, f_far)):
+        loads += [
+            pltpu.make_async_copy(gate_hbm.at[index], gate_ref.at[index], local.at[3 + 2 * n]),
+            pltpu.make_async_copy(up_hbm.at[index], up_ref.at[index], local.at[4 + 2 * n]),
+        ]
     for copy in loads:
         copy.start()
     down_ref[pl.ds(pl.multiple_of((1 - c) * UNITS, 64), 64), :] = jnp.zeros((64, WIDTH), BF)
@@ -720,7 +789,7 @@
             shape((4, 17, 16, 128), BF),
             shape((4, 17, 16, 128), BF),
         ],
-        in_specs=[VMEM] * 5 + [ANY] * 3,
+        in_specs=[VMEM] * 5 + [ANY] * 5,
         out_specs=[VMEM] * 8,
         scratch_shapes=[
             pltpu.VMEM((4, SHARD, WINDOW), BF),
@@ -740,7 +809,7 @@
             pltpu.VMEM((2, 2, 2, 17, 16, 128), BF),
             pltpu.SemaphoreType.DMA((24,)),
             pltpu.SemaphoreType.DMA((24,)),
-            pltpu.SemaphoreType.DMA((3,)),
+            pltpu.SemaphoreType.DMA((9,)),
         ],
         compiler_params=pltpu.CompilerParams(
             vmem_limit_bytes=60 * MIB, collective_id=3, has_side_effects=True
@@ -749,9 +818,9 @@
     )(*operands)
 
 
-UNIT = 106
-HALF = 53
-UPPER = 36
+UNIT = 72
+HALF = 36
+DOWN = 17
 CHUNK = 768
 
 
@@ -770,302 +839,6 @@
     qpos_ref,
     down_a_ref,
     down_b_ref,
-    grads_ref,
-    dkv_ref,
-    dq_ref,
-    sum_ref,
-    qx,
-    dox,
-    own,
-    own_grad,
-    parts,
-    parts_in,
-    pairs,
-    pairs_in,
-    single,
-    single_in,
-    side_a,
-    side_b,
-    relay,
-    landing,
-    staged,
-    late_a,
-    late_b,
-    whole,
-    whole_in,
-    send,
-    recv,
-    local,
-):
-    yl, x, z, yh, c = place()
-    f = yh * 2 + c
-    mate = at(1 - yl, x, z, yh, c)
-    on_x = [at(yl, turn(x, d), z, yh, c) for d in (1, 2, 3)]
-    on_z = [at(yl, x, turn(z, d), yh, c) for d in (1, 2, 3)]
-    links = Links(send, recv)
-    greet([mate] + on_x + on_z)
-
-    rings = (
-        RingSum(
-            links,
-            x,
-            on_x,
-            lambda n, half: grads_ref.at[n, 2 * half : 2 * half + 2, 0:UPPER],
-            relay.at[0],
-            landing.at[0],
-            staged.at[0],
-        ),
-        RingSum(
-            links,
-            z,
-            on_z,
-            lambda n, half: grads_ref.at[2 * half : 2 * half + 2, n, UPPER : 2 * UPPER],
-            relay.at[1],
-            landing.at[1],
-            staged.at[1],
-        ),
-    )
-    for ring in rings:
-        ring.start()
-
-    def keep():
-        moves = (
-            (grads_ref.at[turn(x, 1), 0:2, 0:UPPER], staged.at[0, 0]),
-            (grads_ref.at[turn(x, 3), 2:4, 0:UPPER], staged.at[0, 1]),
-            (grads_ref.at[0:2, turn(z, 1), UPPER : 2 * UPPER], staged.at[1, 0]),
-            (grads_ref.at[2:4, turn(z, 3), UPPER : 2 * UPPER], staged.at[1, 1]),
-            (grads_ref.at[x, :, 0:UPPER], side_a.at[:, 0:UPPER]),
-            (grads_ref.at[:, z, UPPER : 2 * UPPER], side_b.at[:, 0:UPPER]),
-        )
-        return [pltpu.make_async_copy(*move, local.at[n]) for n, move in enumerate(moves)]
-
-    for copy in keep():
-        copy.start()
-    side_a[:, UPPER:HALF] = down_a_ref[...]
-    side_b[:, UPPER:HALF] = down_b_ref[...]
-
-    row = lax.broadcasted_iota(jnp.int32, (128, LANES), 0)
-    for g in range(KVH):
-        lse = thirds(lse_ref[g, 0:1])
-        inner = jnp.sum(do_ref[g].astype(F32).T[64:128] * ot_ref[g], axis=0, keepdims=True)
-        inner = thirds(inner)
-        extra_q = jnp.zeros((128, LANES), F32)
-        extra_d = jnp.zeros((128, LANES), F32)
-        for n in range(3):
-            extra_q = jnp.where(row == 2 + n, -lse[n], extra_q)
-            extra_d = jnp.where(row == 2 + n, -inner[n], extra_d)
-        qx[g, :, 0:128] = q_ref[g, :, 0:128]
-        qx[g, :, 128:256] = (q_ref[g, :, 128:256].astype(F32) + extra_q.T).astype(BF)
-        dox[g, :, 0:128] = do_ref[g]
-        dox[g, :, 128:256] = extra_d.T.astype(BF)
-
-    def piece(g, keys, mask):
-        scores = dot_nt(keys, qx[g])
-        if mask is not None:
-            scores = scores + mask
-        probs = jnp.exp(scores)
-        grad = (probs * dot_nt(keys, dox[g])).astype(BF)
-        both = dot(grad, qx[g, :, 0:128]) + dot(probs.astype(BF), dox[g, :, 0:128])
-        return both, dot(keys[:, 0:128].T[0:64], grad)
-
-    mask = jnp.where(kpos_ref[:, 0:1] <= qpos_ref[0:1], 0.0, MASKED)
-    spots = (
-        pl.ds(pl.multiple_of((z * 2 + yl) * ROWS, ROWS), ROWS),
-        pl.ds(pl.multiple_of((x * 2 + yl) * ROWS, ROWS), ROWS),
-    )
-    slab_of = (x, z)
-    for g in range(KVH):
-        own[...] = jnp.zeros(own.shape, BF)
-        own[0:ROWS] = kv_ref[g, slab_of[g], spots[g], :]
-        both, dq = piece(g, jnp.concatenate([own[...], own_extra()], axis=1), mask)
-        own_grad[g] = both[0:ROWS]
-        dq_ref[g] = dq
-    count = SLAB // CHUNK
-    base = links.reserve(6)
-
-    def part_copy(g, d, slab):
-        device = (
-            ((yl * 4 + jnp.where(g == 0, slab, x)) * 4 + jnp.where(g == 0, z, slab)),
-            f,
-        )
-        n = g * 3 + d - 1
-        return links.copy(parts.at[g, slab], parts_in.at[g, d - 1], device, base + n)
-
-    def step(i, _):
-        n, part = lax.div(i, count), lax.rem(i, count)
-        g = lax.rem(n, 2)
-        d = lax.rem(lax.div(n, 2) + 1, 4)
-        slab = turn(jnp.where(g == 0, x, z), d)
-        start = pl.multiple_of(part * CHUNK, CHUNK)
-        rows = extra_ref[g, pl.ds(pl.multiple_of(slab * 16 + part * 8, 8), 8), :]
-        keys = jnp.concatenate([kv_ref[g, slab, pl.ds(start, CHUNK), :], key_extra(rows)], axis=1)
-        both, dq = piece(g, keys, None)
-        parts[g, slab, pl.ds(start, CHUNK), :] = both.astype(BF)
-        dq_ref[g] += dq
-
-        @pl.when((part == count - 1) & (d > 0))
-        def _():
-            part_copy(g, d, slab).start()
-
-        for at_step, event in events:
-            pl.when(i == at_step)(event)
-        return 0
-
-    pair_base, single_base, second_base, third_slot = (
-        links.reserve(6),
-        links.reserve(2),
-        links.reserve(6),
-        links.reserve(1),
-    )
-
-    def pair_copies(g):
-        other, devices = (z, x)[g], (on_z, on_x)[g]
-        return [
-            links.copy(
-                pairs.at[g, turn(other, n + 1)],
-                pairs_in.at[g, n],
-                devices[n],
-                pair_base + 3 * g + n,
-            )
-            for n in range(3)
-        ]
-
-    def pair_start(g):
-        slab = slab_of[g]
-        for d in (1, 2, 3):
-            part_copy(g, d, turn(slab, d)).wait()
-        for n in range(4):
-            rows = slice(n * 2 * ROWS, (n + 1) * 2 * ROWS)
-            total = parts[g, slab, rows, :].astype(F32)
-            for m in range(3):
-                total = total + parts_in[g, m, rows, :].astype(F32)
-            pairs[g, n] = total.astype(BF)
-        for copy in pair_copies(g):
-            copy.start()
-
-    def single_copy(g):
-        return links.copy(single_in.at[g, 0], single_in.at[g, 1], mate, single_base + g)
-
-    def single_start(g):
-        for copy in pair_copies(g):
-            copy.wait()
-        total = pairs[g, (z, x)[g]].astype(F32)
-        for m in range(3):
-            total = total + pairs_in[g, m].astype(F32)
-        single[g, 0] = total[0:ROWS]
-        single[g, 1] = total[ROWS:]
-        single_in[g, 0] = jnp.where(yl == 0, total[ROWS:], total[0:ROWS]).astype(BF)
-        single_copy(g).start()
-
-    def single_end(g):
-        single_copy(g).wait()
-        dkv_ref[g] = single[g, yl] + single_in[g, 1].astype(F32) + own_grad[g]
-
-    def merge():
-        for copy in keep():
-            copy.wait()
-        for ring in rings:
-            ring.merge()
-
-    def second_copies():
-        copies = []
-        for n in range(3):
-            for source, target, index, device in (
-                (side_a, late_a, turn(z, n + 1), on_z[n]),
-                (side_b, late_b, turn(x, n + 1), on_x[n]),
-            ):
-                copies.append(
-                    links.copy(source.at[index], target.at[n], device, second_base + len(copies))
-                )
-        return copies
-
-    def second_start():
-        for side, ring in zip((side_a, side_b), rings):
-            ring.finish()
-            for half in range(2):
-                rows = slice(2 * half, 2 * half + 2)
-                total = side[rows, 0:UPPER].astype(F32) + ring.arrived(half)
-                side[rows, 0:UPPER] = total.astype(BF)
-        for copy in second_copies():
-            copy.start()
-
-    def third():
-        return links.copy(whole, whole_in, mate, third_slot)
-
-    def third_start():
-        for copy in second_copies():
-            copy.wait()
-        a = side_a[z].astype(F32)
-        b = side_b[x].astype(F32)
-        for m in range(3):
-            a = a + late_a[m].astype(F32)
-            b = b + late_b[m].astype(F32)
-        whole[0:HALF] = a.astype(BF)
-        whole[HALF:UNIT] = b.astype(BF)
-        third().start()
-
-    events = (
-        (3, merge),
-        (9, second_start),
-        (13, lambda: pair_start(0)),
-        (14, third_start),
-    )
-    lax.fori_loop(0, KVH * SLABS * count, step, 0)
-    pair_start(1)
-    single_start(0)
-    single_end(0)
-    single_start(1)
-    single_end(1)
-    third().wait()
-    sum_ref[...] = (whole[...].astype(F32) + whole_in[...].astype(F32)).astype(BF)
-
-
-def back(q, do, ot, lse, kv, extra, kpos, qpos, down_a, down_b, grads):
-    shape = jax.ShapeDtypeStruct
-    return pl.pallas_call(
-        back_kernel,
-        out_shape=[
-            shape((KVH, ROWS, 128), F32),
-            shape((KVH, HD, LANES), F32),
-            shape((UNIT, 16, 128), BF),
-        ],
-        in_specs=[VMEM] * 10 + [ANY],
-        out_specs=[VMEM] * 3,
-        scratch_shapes=[
-            pltpu.VMEM((KVH, LANES, 256), BF),
-            pltpu.VMEM((KVH, LANES, 256), BF),
-            pltpu.VMEM((OWN, 128), BF),
-            pltpu.VMEM((KVH, ROWS, 128), F32),
-            pltpu.VMEM((KVH, SLABS, SLAB, 128), BF),
-            pltpu.VMEM((KVH, 3, SLAB, 128), BF),
-            pltpu.VMEM((KVH, 4, 2 * ROWS, 128), BF),
-            pltpu.VMEM((KVH, 3, 2 * ROWS, 128), BF),
-            pltpu.VMEM((KVH, 2, ROWS, 128), F32),
-            pltpu.VMEM((KVH, 2, ROWS, 128), BF),
-            pltpu.VMEM((4, HALF, 16, 128), BF),
-            pltpu.VMEM((4, HALF, 16, 128), BF),
-            pltpu.VMEM((2, 2, 2, UPPER, 16, 128), BF),
-            pltpu.VMEM((2, 2, 2, 2, UPPER, 16, 128), BF),
-            pltpu.VMEM((2, 2, 2, UPPER, 16, 128), BF),
-            pltpu.VMEM((3, HALF, 16, 128), BF),
-            pltpu.VMEM((3, HALF, 16, 128), BF),
-            pltpu.VMEM((UNIT, 16, 128), BF),
-            pltpu.VMEM((UNIT, 16, 128), BF),
-            pltpu.SemaphoreType.DMA((48,)),
-            pltpu.SemaphoreType.DMA((48,)),
-            pltpu.SemaphoreType.DMA((6,)),
-        ],
-        compiler_params=pltpu.CompilerParams(
-            vmem_limit_bytes=62 * MIB, collective_id=1, has_side_effects=True
-        ),
-        name="back",
-    )(q, do, ot, lse, kv, extra, kpos, qpos, down_a, down_b, grads)
-
-
-def last_kernel(
-    sum_ref,
-    dq_ref,
-    dkv_ref,
     cos_ref,
     sin_ref,
     normed_ref,
@@ -1078,10 +851,36 @@
     wv_all,
     small_all,
     hidden_gain_ref,
+    grads_ref,
     token_grad_ref,
     late_ref,
     thin_ref,
     whole_ref,
+    downs_ref,
+    dq_ref,
+    dkv_ref,
+    sum_ref,
+    qx,
+    dox,
+    own,
+    own_grad,
+    parts,
+    parts_in,
+    pairs,
+    pairs_in,
+    across,
+    side_a,
+    side_b,
+    relay,
+    landing,
+    staged,
+    late_a,
+    late_b,
+    whole,
+    whole_in,
+    down_late,
+    down_whole,
+    down_in,
     natural,
     table,
     table_in,
@@ -1110,21 +909,321 @@
     links = Links(send, recv)
     greet([sib, cross, far, mate] + on_x + on_z)
 
-    shared = []
-
-    def spot(index):
-        return pl.ds(18 * index + 17 * lax.div(index, 2), 18)
-
-    for device, index in ((sib, f_sib), (cross, f_cross), (far, f_far)):
-        shared.append(
-            links.push(sum_ref.at[spot(index)], whole_ref.at[x, z, spot(f)], device)
+    rings = (
+        RingSum(
+            links,
+            x,
+            on_x,
+            lambda n, half: grads_ref.at[n, 2 * half : 2 * half + 2, 0:HALF],
+            relay.at[0],
+            landing.at[0],
+            staged.at[0],
+        ),
+        RingSum(
+            links,
+            z,
+            on_z,
+            lambda n, half: grads_ref.at[2 * half : 2 * half + 2, n, HALF:UNIT],
+            relay.at[1],
+            landing.at[1],
+            staged.at[1],
+        ),
+    )
+    def keep():
+        moves = (
+            (grads_ref.at[turn(x, 1), 0:2, 0:HALF], staged.at[0, 0]),
+            (grads_ref.at[turn(x, 3), 2:4, 0:HALF], staged.at[0, 1]),
+            (grads_ref.at[0:2, turn(z, 1), HALF:UNIT], staged.at[1, 0]),
+            (grads_ref.at[2:4, turn(z, 3), HALF:UNIT], staged.at[1, 1]),
+            (grads_ref.at[x, :, 0:HALF], side_a),
+            (grads_ref.at[:, z, HALF:UNIT], side_b),
         )
-    keep = [
-        pltpu.make_async_copy(sum_ref.at[part], whole_ref.at[x, z, part], local.at[n])
-        for n, part in enumerate((spot(f), slice(UPPER, HALF), slice(HALF + UPPER, UNIT)))
-    ]
-    for copy in keep:
+        return [pltpu.make_async_copy(*move, local.at[n]) for n, move in enumerate(moves)]
+
+    for copy in keep():
         copy.start()
+
+    down_second, down_third, down_fourth, down_fifth, down_sixth = (
+        links.reserve(6),
+        links.reserve(1),
+        links.reserve(6),
+        links.reserve(4),
+        links.reserve(4),
+    )
+
+    def down_copies():
+        copies = []
+        for n in range(3):
+            for source, half, index, device in (
+                (down_a_ref, 0, turn(z, n + 1), on_z[n]),
+                (down_b_ref, 1, turn(x, n + 1), on_x[n]),
+            ):
+                copies.append(
+                    links.copy(
+                        source.at[index],
+                        down_late.at[half, n],
+                        device,
+                        down_second + len(copies),
+                    )
+                )
+        return copies
+
+    def down_mate():
+        return links.copy(down_whole, down_in, mate, down_third)
+
+    def down_third_start():
+        for copy in down_copies():
+            copy.wait()
+        for half, own_part in ((0, down_a_ref[z]), (1, down_b_ref[x])):
+            total = own_part.astype(F32)
+            for m in range(3):
+                total = total + down_late[half, m].astype(F32)
+            down_whole[half] = total.astype(BF)
+        down_mate().start()
+
+    def down_spread():
+        copies = []
+        for n in range(3):
+            for half, device in ((0, on_z[n]), (1, on_x[n])):
+                part = downs_ref.at[half, x, z]
+                copies.append(links.copy(part, part, device, down_fourth + len(copies)))
+        return copies
+
+    def down_spread_start():
+        down_mate().wait()
+        downs_ref[:, x, z] = (
+            down_whole[...].astype(F32) + down_in[...].astype(F32)
+        ).astype(BF)
+        for copy in down_spread():
+            copy.start()
+
+    def down_rounds():
+        copies = []
+        for n in (0, 2):
+            for part, device in (
+                (downs_ref.at[0, x], on_x[n]),
+                (downs_ref.at[1, :, z], on_z[n]),
+            ):
+                copies.append(links.copy(part, part, device, down_fifth + len(copies)))
+        return copies
+
+    def down_rounds_start():
+        for copy in down_spread():
+            copy.wait()
+        for copy in down_rounds():
+            copy.start()
+
+    def down_last():
+        copies = []
+        for half, came, n in ((0, 3, 0), (1, 1, 2)):
+            rows = slice(2 * half, 2 * half + 2)
+            for part, device in (
+                (downs_ref.at[0, turn(x, came), rows], on_x[n]),
+                (downs_ref.at[1, rows, turn(z, came)], on_z[n]),
+            ):
+                copies.append(links.copy(part, part, device, down_sixth + len(copies)))
+        return copies
+
+    def down_last_start():
+        for copy in down_rounds():
+            copy.wait()
+        for copy in down_last():
+            copy.start()
+
+
+    for copy in down_copies():
+        copy.start()
+    for ring in rings:
+        ring.start()
+
+    row = lax.broadcasted_iota(jnp.int32, (128, LANES), 0)
+    for g in range(KVH):
+        lse = thirds(lse_ref[g, 0:1])
+        inner = jnp.sum(do_ref[g].astype(F32).T[64:128] * ot_ref[g], axis=0, keepdims=True)
+        inner = thirds(inner)
+        extra_q = jnp.zeros((128, LANES), F32)
+        extra_d = jnp.zeros((128, LANES), F32)
+        for n in range(3):
+            extra_q = jnp.where(row == 2 + n, -lse[n], extra_q)
+            extra_d = jnp.where(row == 2 + n, -inner[n], extra_d)
+        qx[g, :, 0:128] = q_ref[g, :, 0:128]
+        qx[g, :, 128:256] = (q_ref[g, :, 128:256].astype(F32) + extra_q.T).astype(BF)
+        dox[g, :, 0:128] = do_ref[g]
+        dox[g, :, 128:256] = extra_d.T.astype(BF)
+
+    def piece(g, keys, mask):
+        scores = dot_nt(keys, qx[g])
+        if mask is not None:
+            scores = scores + mask
+        probs = jnp.exp(scores)
+        grad = (probs * dot_nt(keys, dox[g])).astype(BF)
+        both = dot(grad, qx[g, :, 0:128]) + dot(probs.astype(BF), dox[g, :, 0:128])
+        return both, dot(keys[:, 0:128].T[0:64], grad)
+
+    mask = jnp.where(kpos_ref[:, 0:1] <= qpos_ref[0:1], 0.0, MASKED)
+    spots = (
+        pl.ds(pl.multiple_of((z * 2 + yl) * ROWS, ROWS), ROWS),
+        pl.ds(pl.multiple_of((x * 2 + yl) * ROWS, ROWS), ROWS),
+    )
+    slab_of = (x, z)
+    for g in range(KVH):
+        own[...] = jnp.zeros(own.shape, BF)
+        own[0:ROWS] = kv_ref[g, slab_of[g], spots[g], :]
+        both, dq = piece(g, jnp.concatenate([own[...], own_extra()], axis=1), mask)
+        own_grad[g] = both[0:ROWS]
+        dq_ref[g] = dq
+    count = SLAB // CHUNK
+    base = links.reserve(6)
+
+    across_base = links.reserve(16)
+
+    def across_copy(g, d, slab, part):
+        rows = pl.ds(2 * part, 2)
+        return links.copy(
+            parts.at[g, slab, rows, 1 - yl],
+            across.at[g, d, rows],
+            mate,
+            across_base + (g * 4 + d) * 2 + part,
+        )
+
+    def part_copy(g, d, slab):
+        device = (
+            ((yl * 4 + jnp.where(g == 0, slab, x)) * 4 + jnp.where(g == 0, z, slab)),
+            f,
+        )
+        return links.copy(
+            across.at[g, d], parts_in.at[g, d - 1], device, base + g * 3 + d - 1
+        )
+
+    def combine(g, d, slab):
+        for part in range(count):
+            across_copy(g, d, slab, part).wait()
+        total = parts[g, slab, :, yl].astype(F32) + across[g, d].astype(F32)
+        across[g, d] = total.astype(BF)
+
+    def slab_at(n):
+        g, d = lax.rem(n, 2), lax.rem(lax.div(n, 2) + 1, 4)
+        return g, d, turn(jnp.where(g == 0, x, z), d)
+
+    def step(i, _):
+        n, part = lax.div(i, count), lax.rem(i, count)
+        g, d, slab = slab_at(n)
+        start = pl.multiple_of(part * CHUNK, CHUNK)
+        rows = extra_ref[g, pl.ds(pl.multiple_of(slab * 16 + part * 8, 8), 8), :]
+        keys = jnp.concatenate([kv_ref[g, slab, pl.ds(start, CHUNK), :], key_extra(rows)], axis=1)
+        both, dq = piece(g, keys, None)
+        parts[g, slab, pl.ds(2 * part, 2)] = both.astype(BF).reshape(2, 2, ROWS, 128)
+        dq_ref[g] += dq
+
+        across_copy(g, d, slab, part).start()
+
+        @pl.when((part == count - 1) & (n > 0))
+        def _():
+            before = slab_at(n - 1)
+            combine(*before)
+
+            @pl.when(n < 7)
+            def _():
+                part_copy(*before).start()
+
+        for at_step, event in events:
+            pl.when(i == at_step)(event)
+        return 0
+
+    pair_base, second_base, third_slot = (
+        links.reserve(6),
+        links.reserve(6),
+        links.reserve(1),
+    )
+
+    def pair_copies(g):
+        other, devices = (z, x)[g], (on_z, on_x)[g]
+        return [
+            links.copy(
+                pairs.at[g, turn(other, n + 1)],
+                pairs_in.at[g, n],
+                devices[n],
+                pair_base + 3 * g + n,
+            )
+            for n in range(3)
+        ]
+
+    def pair_start(g):
+        slab = slab_of[g]
+        for d in (1, 2, 3):
+            part_copy(g, d, turn(slab, d)).wait()
+        for n in range(4):
+            total = across[g, 0, n].astype(F32)
+            for m in range(3):
+                total = total + parts_in[g, m, n].astype(F32)
+            pairs[g, n] = total.astype(BF)
+        for copy in pair_copies(g):
+            copy.start()
+
+    def pair_end(g):
+        for copy in pair_copies(g):
+            copy.wait()
+        total = pairs[g, (z, x)[g]].astype(F32) + own_grad[g]
+        for m in range(3):
+            total = total + pairs_in[g, m].astype(F32)
+        dkv_ref[g] = total
+
+    def merge():
+        for copy in keep():
+            copy.wait()
+        for ring in rings:
+            ring.merge()
+
+    def second_copies():
+        copies = []
+        for n in range(3):
+            for source, target, index, device in (
+                (side_a, late_a, turn(z, n + 1), on_z[n]),
+                (side_b, late_b, turn(x, n + 1), on_x[n]),
+            ):
+                copies.append(
+                    links.copy(source.at[index], target.at[n], device, second_base + len(copies))
+                )
+        return copies
+
+    def second_start():
+        for side, ring in zip((side_a, side_b), rings):
+            ring.finish()
+            for half in range(2):
+                rows = slice(2 * half, 2 * half + 2)
+                side[rows] = (side[rows].astype(F32) + ring.arrived(half)).astype(BF)
+        for copy in second_copies():
+            copy.start()
+
+    def third():
+        return links.copy(whole, whole_in, mate, third_slot)
+
+    def third_start():
+        for copy in second_copies():
+            copy.wait()
+        a = side_a[z].astype(F32)
+        b = side_b[x].astype(F32)
+        for m in range(3):
+            a = a + late_a[m].astype(F32)
+            b = b + late_b[m].astype(F32)
+        whole[0:HALF] = a.astype(BF)
+        whole[HALF:UNIT] = b.astype(BF)
+        third().start()
+
+    events = (
+        (1, down_third_start),
+        (6, down_spread_start),
+        (5, merge),
+        (10, second_start),
+        (11, down_rounds_start),
+        (13, third_start),
+        (15, down_last_start),
+    )
+    lax.fori_loop(0, KVH * SLABS * count, step, 0)
+    pair_start(0)
+
+    low = lanes_below((ROWS, 128), 64)
+    cosine, sine = cos_ref[...], -sin_ref[...]
 
     def assemble(tile):
         even, odd = tile * 2, tile * 2 + 1
@@ -1132,8 +1231,6 @@
         right = natural[odd // GROUP, (odd % GROUP) * ROWS : (odd % GROUP + 1) * ROWS]
         return jnp.where(low, left, swap64(right))
 
-    low = lanes_below((ROWS, 128), 64)
-    cosine, sine = cos_ref[...], -sin_ref[...]
     for g in range(KVH):
         natural[g] = jnp.concatenate([dq_ref[g], jnp.zeros((64, LANES), F32)], axis=0).T
     grad_queries = jnp.concatenate(
@@ -1143,10 +1240,69 @@
         ],
         axis=1,
     ).astype(BF)
+
+    combine(1, 0, slab_of[1])
+    pair_start(1)
+
+    normed = normed_ref[...]
+
+    def table_columns(first, left, right):
+        product = dot_tn(left, right).astype(BF)
+        for n in range(right.shape[1] // 128):
+            table[first + n] = product[:, n * 128 : n * 128 + 128].reshape(4, SHARD, 128)
+
+    def beside(slot, start, stop):
+        return [
+            links.copy(
+                table.at[start:stop, 2 * n + 1 - c], table_in.at[n, start:stop], sib, slot + n
+            )
+            for n in range(2)
+        ]
+
+    def add_beside(n, _):
+        for m in range(2):
+            total = table[n, 2 * m + c].astype(F32) + table_in[m, n].astype(F32)
+            lines[m, n] = total.astype(BF)
+        return 0
+
+    beside_slots = links.reserve(6)
+    table_columns(0, normed, grad_queries)
+    for copy in beside(beside_slots, 0, 7):
+        copy.start()
+    table_columns(9, attended_ref[...], grad_attn_ref[...])
+    for copy in beside(beside_slots + 2, 9, 16):
+        copy.start()
+    pair_end(0)
+
+    third().wait()
+    sum_ref[...] = (whole[...].astype(F32) + whole_in[...].astype(F32)).astype(BF)
+
+    def spot(index):
+        return pl.ds(18 * index, 18)
+
+    shared = [
+        links.push(sum_ref.at[spot(index)], whole_ref.at[x, z, spot(f)], device)
+        for device, index in ((cross, f_cross), (far, f_far), (sib, f_sib))
+    ]
+    keep_own = [
+        pltpu.make_async_copy(sum_ref.at[spot(f)], whole_ref.at[x, z, spot(f)], local.at[0])
+    ]
+    for copy in keep_own:
+        copy.start()
+    for copy in beside(beside_slots, 0, 7) + beside(beside_slots + 2, 9, 16):
+        copy.wait()
+    lax.fori_loop(0, 7, add_beside, 0)
+    lax.fori_loop(9, 16, add_beside, 0)
+
+    pair_end(1)
     grad_keys = turn_pairs(jnp.where(low, dkv_ref[0], swap64(dkv_ref[1])), cosine, sine).astype(BF)
     grad_values = jnp.where(low, swap64(dkv_ref[0]), dkv_ref[1]).astype(BF)
-
-    for copy in keep + shared:
+    table_columns(7, normed, grad_keys)
+    table_columns(8, normed, grad_values)
+    for copy in beside(beside_slots + 4, 7, 9):
+        copy.start()
+
+    for copy in keep_own + shared:
         copy.wait()
     spread = []
     for n in range(3):
@@ -1156,22 +1312,18 @@
         spread.append(
             links.push(whole_ref.at[x, z, HALF:UNIT], whole_ref.at[x, z, HALF:UNIT], on_x[n])
         )
-
-    normed, attended = normed_ref[...], attended_ref[...]
-    column = 0
-    for left, right in (
-        (normed, grad_queries),
-        (normed, grad_keys),
-        (normed, grad_values),
-        (attended, grad_attn_ref[...]),
-    ):
-        product = dot_tn(left, right).astype(BF)
-        for n in range(right.shape[1] // 128):
-            table[column] = product[:, n * 128 : n * 128 + 128].reshape(4, SHARD, 128)
-            column += 1
-    beside = [
-        links.push(table.at[:, 2 * n + 1 - c], table_in.at[n], sib) for n in range(2)
-    ]
+    for copy in beside(beside_slots + 4, 7, 9):
+        copy.wait()
+    lax.fori_loop(7, 9, add_beside, 0)
+
+    along = []
+    for n in range(3):
+        xt, zt = turn(x, n + 1), turn(z, n + 1)
+        along.append(links.push(lines.at[0, pl.ds(xt * 4, 4)], lines_in.at[0, n], on_x[n]))
+        for m in range(4):
+            along.append(
+                links.push(lines.at[1, m * 4 + zt], lines_in.at[1, n, m], on_z[n])
+            )
 
     inputs = tokens_ref[...].astype(F32)
     scale = lax.rsqrt(jnp.mean(inputs * inputs, axis=-1, keepdims=True) + EPSILON)
@@ -1211,7 +1363,11 @@
     def thin_push(level, index, device):
         return links.push(thin.at[level, index], thin.at[level, index], device)
 
-    thin_copies = [thin_push(0, c, sib)]
+    thin_copy = thin_push(0, c, sib)
+    thin_copy.wait()
+    thin[1, x] = thin[0, 0] + thin[0, 1]
+    for n in range(3):
+        along.append(thin_push(1, x, on_x[n]))
 
     for copy in spread:
         copy.wait()
@@ -1223,26 +1379,6 @@
         rounds.append(
             links.push(whole_ref.at[:, z, HALF:UNIT], whole_ref.at[:, z, HALF:UNIT], on_z[n])
         )
-    for copy in beside + thin_copies:
-        copy.wait()
-
-    def add_beside(n, _):
-        for m in range(2):
-            total = table[n, 2 * m + c].astype(F32) + table_in[m, n].astype(F32)
-            lines[m, n] = total.astype(BF)
-        return 0
-
-    lax.fori_loop(0, 16, add_beside, 0)
-    thin[1, x] = thin[0, 0] + thin[0, 1]
-    along = []
-    for n in range(3):
-        xt, zt = turn(x, n + 1), turn(z, n + 1)
-        along.append(links.push(lines.at[0, pl.ds(xt * 4, 4)], lines_in.at[0, n], on_x[n]))
-        for m in range(4):
-            along.append(
-                links.push(lines.at[1, m * 4 + zt], lines_in.at[1, n, m], on_z[n])
-            )
-        along.append(thin_push(1, x, on_x[n]))
     for copy in along:
         copy.wait()
     for m in range(4):
@@ -1299,23 +1435,48 @@
     for n in range(3):
         along.append(links.push(late_ref.at[x, :, 0:cut], late_ref.at[x, :, 0:cut], on_x[n]))
         along.append(links.push(late_ref.at[:, z, cut:], late_ref.at[:, z, cut:], on_z[n]))
-    for copy in along + rounds:
-        copy.wait()
-
-
-def last_call(*operands):
+    for copy in along + rounds + down_last():
+        copy.wait()
+
+
+def back(*operands):
     shape = jax.ShapeDtypeStruct
     return pl.pallas_call(
-        last_kernel,
+        back_kernel,
         out_shape=[
             shape((ROWS, WIDTH), F32),
             shape((4, 4, SHARD, 128), BF),
             shape((8, WIDTH), F32),
             shape((4, 4, UNIT, 16, 128), BF),
+            shape((2, 4, 4, DOWN, 16, 128), BF),
         ],
-        in_specs=[VMEM] * 15,
-        out_specs=[VMEM] * 3 + [ANY],
+        in_specs=[VMEM] * 22 + [ANY],
+        out_specs=[VMEM] * 3 + [ANY, VMEM],
         scratch_shapes=[
+            pltpu.VMEM((KVH, HD, LANES), F32),
+            pltpu.VMEM((KVH, ROWS, 128), F32),
+            pltpu.VMEM((UNIT, 16, 128), BF),
+            pltpu.VMEM((KVH, LANES, 256), BF),
+            pltpu.VMEM((KVH, LANES, 256), BF),
+            pltpu.VMEM((OWN, 128), BF),
+            pltpu.VMEM((KVH, ROWS, 128), F32),
+            pltpu.VMEM((KVH, SLABS, 4, 2, ROWS, 128), BF),
+            pltpu.VMEM((KVH, 3, 4, ROWS, 128), BF),
+            pltpu.VMEM((KVH, 4, ROWS, 128), BF),
+            pltpu.VMEM((KVH, 3, ROWS, 128), BF),
+            pltpu.VMEM((KVH, 4, 4, ROWS, 128), BF),
+            pltpu.VMEM((4, HALF, 16, 128), BF),
+            pltpu.VMEM((4, HALF, 16, 128), BF),
+            pltpu.VMEM((2, 2, 2, HALF, 16, 128), BF),
+            pltpu.VMEM((2, 2, 2, 2, HALF, 16, 128), BF),
+            pltpu.VMEM((2, 2, 2, HALF, 16, 128), BF),
+            pltpu.VMEM((3, HALF, 16, 128), BF),
+            pltpu.VMEM((3, HALF, 16, 128), BF),
+            pltpu.VMEM((UNIT, 16, 128), BF),
+            pltpu.VMEM((UNIT, 16, 128), BF),
+            pltpu.VMEM((2, 3, DOWN, 16, 128), BF),
+            pltpu.VMEM((2, DOWN, 16, 128), BF),
+            pltpu.VMEM((2, DOWN, 16, 128), BF),
             pltpu.VMEM((KVH, LANES, 128), F32),
             pltpu.VMEM((16, 4, SHARD, 128), BF),
             pltpu.VMEM((2, 16, SHARD, 128), BF),
@@ -1326,14 +1487,14 @@
             pltpu.VMEM((3, SHARD, 128), BF),
             pltpu.VMEM((2, SHARD, 128), BF),
             pltpu.VMEM((5, 4, 8, WIDTH), F32),
-            pltpu.SemaphoreType.DMA((72,)),
-            pltpu.SemaphoreType.DMA((72,)),
-            pltpu.SemaphoreType.DMA((3,)),
+            pltpu.SemaphoreType.DMA((144,)),
+            pltpu.SemaphoreType.DMA((144,)),
+            pltpu.SemaphoreType.DMA((6,)),
         ],
         compiler_params=pltpu.CompilerParams(
-            vmem_limit_bytes=58 * MIB, collective_id=2, has_side_effects=True
+            vmem_limit_bytes=63 * MIB, collective_id=1, has_side_effects=True
         ),
-        name="last",
+        name="back",
     )(*operands)
 
 
@@ -1341,6 +1502,7 @@
     late_ref,
     thin_ref,
     whole_ref,
+    downs_ref,
     q_out,
     k_out,
     v_out,
@@ -1371,7 +1533,7 @@
 
     def gate_tile(n, r, lane):
         t = r * 20 + lane
-        p, k = t // 18, 18 * n + 17 * (n // 2) + t % 18
+        p, k = t // 18, 18 * n + t % 18
         return whole_ref[p // 4, p % 4, k].astype(F32)
 
     for value, out, first in ((gate_val, gate_out, 0), (up_val, up_out, 10)):
@@ -1389,9 +1551,8 @@
         for tile in range(7):
             t = r * 7 + tile
             p, k = t // 34, t % 34
-            k = UPPER + k if k < 17 else HALF + UPPER + k - 17
-            down_val[r * 16 : r * 16 + 16, tile * 128 : tile * 128 + 128] = whole_ref[
-                p // 4, p % 4, k
+            down_val[r * 16 : r * 16 + 16, tile * 128 : tile * 128 + 128] = downs_ref[
+                k // DOWN, p // 4, p % 4, k % DOWN
             ].astype(F32)
     leave(down_val, down_out)
     column = 0
@@ -1418,7 +1579,7 @@
         copy.wait()
 
 
-def finish(late, thin, whole):
+def finish(late, thin, whole, downs):
     shape = jax.ShapeDtypeStruct
     large = [
         (SHARD, WIDTH),
@@ -1433,42 +1594,13 @@
     return pl.pallas_call(
         finish_kernel,
         out_shape=[shape(size, F32) for size in large + tiny],
-        in_specs=[VMEM] * 3,
+        in_specs=[VMEM] * 4,
         out_specs=[ANY] * 7 + [VMEM] * 5,
         scratch_shapes=[pltpu.VMEM(size, F32) for size in large]
         + [pltpu.SemaphoreType.DMA((7,))],
         compiler_params=pltpu.CompilerParams(vmem_limit_bytes=58 * MIB),
         name="finish",
-    )(late, thin, whole)
-
-
-def tables(block_order, ctx):
-    own_blocks = lax.dynamic_slice_in_dim(block_order, ctx * 2, 2)
-    own_pos = (own_blocks[:, None] * BLK + jnp.arange(BLK, dtype=jnp.int32)[None, :]).reshape(ROWS)
-    own_pos = own_pos.astype(F32)
-    frequency = jnp.exp(jnp.arange(HD // 2, dtype=F32) * (-2.0 * math.log(THETA) / HD))
-    angles = own_pos[:, None] * frequency[None, :]
-    cosine, sine = jnp.cos(angles), jnp.sin(angles)
-    cosine = jnp.concatenate([cosine] * 4, axis=1)
-    sine = jnp.concatenate([-sine, sine] * 2, axis=1)
-    slots = jnp.arange(64, dtype=jnp.int32)
-    shown = (block_order[:, None] < own_blocks[None, :]) & (slots // 2 != ctx)[:, None]
-    lane = jnp.arange(128)[None, :]
-    bias = jnp.where(shown, 0.0, MASKED)
-    extra = jnp.where(lane == 0, bias[:, 0:1], jnp.where(lane == 1, bias[:, 1:2], 0.0))
-    extra = jnp.where((lane >= 2) & (lane < 5), 1.0, extra).astype(F32).reshape(2, 4, 4, 2, 128)
-    extra = jnp.stack(
-        [
-            extra.transpose(1, 2, 0, 3, 4).reshape(64, 128),
-            extra.transpose(2, 1, 0, 3, 4).reshape(64, 128),
-        ]
-    )
-    kpos = jnp.pad(own_pos, (0, OWN - ROWS), constant_values=1e9)
-    kpos = jnp.broadcast_to(kpos[:, None], (OWN, 128))
-    qpos = jnp.pad(jnp.tile(own_pos, GROUP), (0, LANES - GROUP * ROWS), constant_values=5e8)
-    qpos = jnp.broadcast_to(qpos[None, :], (8, LANES))
-    return cosine, sine, extra, kpos, qpos
-
+    )(late, thin, whole, downs)
 
 def body(
     tokens,
@@ -1487,16 +1619,9 @@
     hidden_gain,
     cotangent,
 ):
-    ctx = lax.axis_index("ctx")
-    cosine, sine, extra, kpos, qpos = tables(block_order, ctx)
-
-    def line(vector):
-        return jnp.pad(vector.astype(F32), (0, 256 - vector.shape[0]))
-
-    small = jnp.stack(
-        [line(v) for v in (query_bias, attention_gain, hidden_gain, key_bias, value_bias)]
-        + [jnp.zeros((256,), F32)] * 3
-    )
+    def row(vector):
+        return vector.reshape(1, -1)
+
     (
         attended,
         ot,
@@ -1508,6 +1633,11 @@
         wk_all,
         wv_all,
         small_all,
+        cosine,
+        sine,
+        extra,
+        kpos,
+        qpos,
         wo_all,
         gate_all,
         up_all,
@@ -1517,12 +1647,13 @@
         query_weight,
         key_weight,
         value_weight,
-        small,
-        cosine,
-        sine,
-        extra,
-        kpos,
-        qpos,
+        row(query_bias),
+        row(attention_gain),
+        row(hidden_gain),
+        row(key_bias),
+        row(value_bias),
+        block_order,
+        *angle_tables(),
         output_weight,
         gate_weight,
         up_weight,
@@ -1538,15 +1669,28 @@
         down_a,
         down_b,
     ) = middle_call(
-        attended, tokens[0], small_all, wo_all, cot_all, gate_all, up_all, down_weight
+        attended,
+        tokens[0],
+        small_all,
+        wo_all,
+        cot_all,
+        gate_all,
+        up_all,
+        gate_weight,
+        up_weight,
+        down_weight,
     )
-    dkv, dq, total = back(
-        q, grad_attended, ot, lse, kv, extra, kpos, qpos, down_a, down_b, grads
-    )
-    token_grad, late, thin, whole = last_call(
-        total,
-        dq,
-        dkv,
+    token_grad, late, thin, whole, downs = back(
+        q,
+        grad_attended,
+        ot,
+        lse,
+        kv,
+        extra,
+        kpos,
+        qpos,
+        down_a,
+        down_b,
         cosine,
         sine,
         normed,
@@ -1559,8 +1703,9 @@
         wv_all,
         small_all,
         hidden_gain_part,
+        grads,
     )
-    ends = finish(late, thin, whole)
+    ends = finish(late, thin, whole, downs)
     return (output[None], token_grad[None], *ends[:7], *(end.reshape(-1) for end in ends[7:]))
 
 

time: 313 us -> 281 us (0.90)
  Pallas kernels: 294 us -> 269 us
  other arithmetic: 6.9 us -> 0 us
    pallas_call x2 -> x1, Pallas kernels: 159 us -> 137 us  [back(): pl.pallas_call(back_kernel, out_shape=[shape((ROWS, WIDTH), F32), shape((...]
    another operation x6 -> x0, other arithmetic: 3.92 us -> none  [the longest x5 3.29 us: body(): jnp.stack([line(v) for v in (query_bias, attention_gain, hidden_gain, key...]
    reshape x0 -> x3, local copies, waits for them, and re-layouts: none -> 3.66 us  [row(): return vector.reshape(1, -1)]
where the time goes in v3:
time: 281 us; the launch traced here: 276 us
  Pallas kernels  269 us (96%)
  local copies, waits for them, and re-layouts  5.25 us (2%)
    pallas_call x1, Pallas kernels, back(): pl.pallas_call(back_kernel, out_shape=[shape((ROWS, WIDTH), F32), shape((...  137 us
    pallas_call x1, Pallas kernels, front(): pl.pallas_call(front_kernel, out_shape=[shape((ROWS, WIDTH), BF), shape((...  72.2 us
    pallas_call x1, Pallas kernels, middle_call(): pl.pallas_call(middle_kernel, out_shape=[shape((ROWS, WIDTH), BF), shape(...  50.8 us
    pallas_call x1, Pallas kernels, finish(): pl.pallas_call(finish_kernel, out_shape=[shape(size, F32) for size in lar...  9.76 us

profile of v3, /device:TPU:8, one launch (start us, length us, event | category | flops | bytes accessed | tf_op | source)
XLA Modules:
  0.0 275.7 jit_solution(12672357483225038216)
XLA Ops:
  0.6 1.2 reshape.58.qb_ref
  1.9 1.2 reshape.59.ag_ref
  3.1 1.2 reshape.60.hg_ref
  4.3 72.2 %front.1 = (bf16[192,896]{1,0:T(8,128)(2,1)}, f32[2,64,1408]{2,1,0:T(8,128)}, f32[2,8,1408]{2,1,0:T(8,128)}, bf16[2,1408,256]{2,1,0:T(8,128)(2,1)}, bf16[2,4,153...) custom-call(bf16[192,896]{1,0:T(8,128)(2,1)} %bitcast.11, ...), custom_call_target="tpu_custom_call" | custom-call | tf_op jit(solution)/shard_map/front/pallas_call | solution.py:498
  76.6 50.8 %middle.1 = (bf16[192,896]{1,0:T(8,128)(2,1)}, f32[192,896]{1,0:T(8,128)}, bf16[192,896]{1,0:T(8,128)(2,1)}, f32[8,896]{1,0:T(8,128)}, bf16[2,1408,128]{2,1,0:T(...) custom-call(bf16[192,896]{1,0:T(8,128)(2,1)} %get-tuple-element.58.a, ...), custom_call_target="tpu_custom_call" | custom-call | tf_op jit(solution)/shard_map/middle/pallas_call | solution.py:780
  127.4 136.5 %back.1 = (f32[192,896]{1,0:T(8,128)}, bf16[4,4,224,128]{3,2,1,0:T(8,128)(2,1)}, f32[8,896]{1,0:T(8,128)}, bf16[4,4,72,16,128]{4,3,2,1,0:T(8,128)(2,1)}, bf16[2,4,4,17,16,128]{5,4,3,2,1,0:T(8,128)(2,1)}) custom-call(bf16[2,1408,256]{2,1,0:T(8,128)(2,1)} %get-tuple-element.65.q_ref, bf16[2,1408,128]{2,1,0:T(8,128)(2,1)} %get-tuple-element.66.do_ref, ...), custom_call_target="tpu_custom_call" | custom-call | tf_op jit(solution)/shard_map/back/pallas_call | solution.py:1444
  263.9 0.0 copy-start.1
  263.9 0.0 copy-start
  263.9 9.8 %finish.1 = (f32[224,896]{1,0:T(8,128)}, f32[224,128]{1,0:T(8,128)}, f32[224,128]{1,0:T(8,128)}, f32[224,896]{1,0:T(8,128)}, f32[224,4864]{1,0:T(8,128)}, /*inde...) custom-call(bf16[4,4,224,128]{3,2,1,0:T(8,128)(2,1)} %get-tuple-elem, ...), custom_call_target="tpu_custom_call" | custom-call | tf_op jit(solution)/shard_map/finish/pallas_call | solution.py:1594
  273.7 0.0 copy-done.1
  273.7 0.7 copy.33
  274.4 0.0 copy-done
  274.4 0.8 copy.34
Async XLA Ops:
  263.9 9.8 %copy-start.1 = (bf16[192,896]{1,0:T(8,128)(2,1)S(1)}, bf16[192,896]{1,0:T(8,128)(2,1)}, u32[]{:S(2)}) copy-start(bf16[192,896]{1,0:T(8,128)(2,1)} %get-tuple-element.64) | copy-start | bytes 1032196
  263.9 10.5 %copy-start = (f32[192,896]{1,0:T(8,128)S(1)}, f32[192,896]{1,0:T(8,128)}, u32[]{:S(2)}) copy-start(f32[192,896]{1,0:T(8,128)} %get-tuple-element.85) | copy-start | bytes 2064388

commit v4 on v3

--- a/solution.py
+++ b/solution.py
@@ -299,7 +299,7 @@
     for row, (ref, count) in enumerate(
         ((qb_ref, SHARD), (ag_ref, SHARD), (hg_ref, SHARD), (kb_ref, 32), (vb_ref, 32))
     ):
-        small_all[f, row : row + 1, 0:count] = ref[...].astype(F32)
+        small_all[f, row : row + 1, 0:count] = ref[...].astype(F32).reshape(1, count)
     first += gather_start([(small_all.at[f], small_all)])
     keep = [
         pltpu.make_async_copy(mine, whole.at[f], local.at[n])
@@ -1501,8 +1501,8 @@
 def finish_kernel(
     late_ref,
     thin_ref,
-    whole_ref,
-    downs_ref,
+    whole_hbm,
+    downs_hbm,
     q_out,
     k_out,
     v_out,
@@ -1522,8 +1522,16 @@
     gate_val,
     up_val,
     down_val,
+    whole_ref,
+    downs_ref,
+    loads,
     sems,
 ):
+    parts = [
+        pltpu.make_async_copy(whole_hbm.at[n], whole_ref.at[n], loads.at[n]) for n in range(4)
+    ] + [pltpu.make_async_copy(downs_hbm, downs_ref, loads.at[4])]
+    for part in parts:
+        part.start()
     copies = []
 
     def leave(value, out):
@@ -1536,17 +1544,25 @@
         p, k = t // 18, 18 * n + t % 18
         return whole_ref[p // 4, p % 4, k].astype(F32)
 
-    for value, out, first in ((gate_val, gate_out, 0), (up_val, up_out, 10)):
-        for r in range(14):
+    arrived = 0
+    for r in range(14):
+        while arrived <= (r * 20 + 19) // 18 // 4:
+            parts[arrived].wait()
+            arrived += 1
+        for value, first in ((gate_val, 0), (up_val, 10)):
             for tile in range(38):
-                parts = []
+                pieces = []
                 for n in range(4):
                     lane = tile - (19 * n) // 2
                     if 0 <= lane < 10:
-                        parts.append(gate_tile(n, r, first + lane))
-                total = parts[0] if len(parts) == 1 else parts[0] + parts[1]
+                        pieces.append(gate_tile(n, r, first + lane))
+                total = pieces[0] if len(pieces) == 1 else pieces[0] + pieces[1]
                 value[r * 16 : r * 16 + 16, tile * 128 : tile * 128 + 128] = total
-        leave(value, out)
+        if r % 7 == 6:
+            rows = pl.ds((r // 7) * 112, 112)
+            leave(gate_val.at[rows], gate_out.at[rows])
+            leave(up_val.at[rows], up_out.at[rows])
+    parts[4].wait()
     for r in range(76):
         for tile in range(7):
             t = r * 7 + tile
@@ -1594,10 +1610,15 @@
     return pl.pallas_call(
         finish_kernel,
         out_shape=[shape(size, F32) for size in large + tiny],
-        in_specs=[VMEM] * 4,
+        in_specs=[VMEM] * 2 + [ANY] * 2,
         out_specs=[ANY] * 7 + [VMEM] * 5,
         scratch_shapes=[pltpu.VMEM(size, F32) for size in large]
-        + [pltpu.SemaphoreType.DMA((7,))],
+        + [
+            pltpu.VMEM((4, 4, UNIT, 16, 128), BF),
+            pltpu.VMEM((2, 4, 4, DOWN, 16, 128), BF),
+            pltpu.SemaphoreType.DMA((5,)),
+            pltpu.SemaphoreType.DMA((9,)),
+        ],
         compiler_params=pltpu.CompilerParams(vmem_limit_bytes=58 * MIB),
         name="finish",
     )(late, thin, whole, downs)
@@ -1619,8 +1640,6 @@
     hidden_gain,
     cotangent,
 ):
-    def row(vector):
-        return vector.reshape(1, -1)
 
     (
         attended,
@@ -1647,11 +1666,11 @@
         query_weight,
         key_weight,
         value_weight,
-        row(query_bias),
-        row(attention_gain),
-        row(hidden_gain),
-        row(key_bias),
-        row(value_bias),
+        query_bias,
+        attention_gain,
+        hidden_gain,
+        key_bias,
+        value_bias,
         block_order,
         *angle_tables(),
         output_weight,

time: 281 us -> 277 us (0.986)
  local copies, waits for them, and re-layouts: 5.25 us -> 1.59 us
    reshape x3 -> x0, local copies, waits for them, and re-layouts: 3.66 us -> none  [row(): return vector.reshape(1, -1)]
where the time goes in v4:
time: 277 us; the launch traced here: 271 us
  Pallas kernels  269 us (97%)
    pallas_call x1, Pallas kernels, back(): pl.pallas_call(back_kernel, out_shape=[shape((ROWS, WIDTH), F32), shape((...  136 us
    pallas_call x1, Pallas kernels, front(): pl.pallas_call(front_kernel, out_shape=[shape((ROWS, WIDTH), BF), shape((...  72.4 us
    pallas_call x1, Pallas kernels, middle_call(): pl.pallas_call(middle_kernel, out_shape=[shape((ROWS, WIDTH), BF), shape(...  50.8 us
    pallas_call x1, Pallas kernels, finish(): pl.pallas_call(finish_kernel, out_shape=[shape(size, F32) for size in lar...  8.92 us

profile of v4, /device:TPU:8, one launch (start us, length us, event | category | flops | bytes accessed | tf_op | source)
XLA Modules:
  0.0 271.3 jit_solution(17449673953337725159)
XLA Ops:
  0.6 72.4 %front.1 = (bf16[192,896]{1,0:T(8,128)(2,1)}, f32[2,64,1408]{2,1,0:T(8,128)}, f32[2,8,1408]{2,1,0:T(8,128)}, bf16[2,1408,256]{2,1,0:T(8,128)(2,1)}, bf16[2,4,153...) custom-call(bf16[192,896]{1,0:T(8,128)(2,1)} %bitcast.9, ...), custom_call_target="tpu_custom_call" | custom-call | tf_op jit(solution)/shard_map/front/pallas_call | solution.py:498
  73.0 50.8 %middle.1 = (bf16[192,896]{1,0:T(8,128)(2,1)}, f32[192,896]{1,0:T(8,128)}, bf16[192,896]{1,0:T(8,128)(2,1)}, f32[8,896]{1,0:T(8,128)}, bf16[2,1408,128]{2,1,0:T(...) custom-call(bf16[192,896]{1,0:T(8,128)(2,1)} %get-tuple-element.58.a, ...), custom_call_target="tpu_custom_call" | custom-call | tf_op jit(solution)/shard_map/middle/pallas_call | solution.py:780
  123.8 136.5 %back.1 = (f32[192,896]{1,0:T(8,128)}, bf16[4,4,224,128]{3,2,1,0:T(8,128)(2,1)}, f32[8,896]{1,0:T(8,128)}, bf16[4,4,72,16,128]{4,3,2,1,0:T(8,128)(2,1)}, bf16[2,4,4,17,16,128]{5,4,3,2,1,0:T(8,128)(2,1)}) custom-call(bf16[2,1408,256]{2,1,0:T(8,128)(2,1)} %get-tuple-element.65.q_ref, bf16[2,1408,128]{2,1,0:T(8,128)(2,1)} %get-tuple-element.66.do_ref, ...), custom_call_target="tpu_custom_call" | custom-call | tf_op jit(solution)/shard_map/back/pallas_call | solution.py:1444
  260.3 0.0 copy-start.1
  260.3 0.0 copy-start
  260.4 8.9 %finish.1 = (f32[224,896]{1,0:T(8,128)}, f32[224,128]{1,0:T(8,128)}, f32[224,128]{1,0:T(8,128)}, f32[224,896]{1,0:T(8,128)}, f32[224,4864]{1,0:T(8,128)}, /*inde...) custom-call(bf16[4,4,224,128]{3,2,1,0:T(8,128)(2,1)} %get-tuple-elem, ...), custom_call_target="tpu_custom_call" | custom-call | tf_op jit(solution)/shard_map/finish/pallas_call | solution.py:1610
  269.3 0.0 copy-done.1
  269.3 0.7 copy.33
  270.0 0.0 copy-done
  270.0 0.8 copy.34
Async XLA Ops:
  260.3 9.0 %copy-start.1 = (bf16[192,896]{1,0:T(8,128)(2,1)S(1)}, bf16[192,896]{1,0:T(8,128)(2,1)}, u32[]{:S(2)}) copy-start(bf16[192,896]{1,0:T(8,128)(2,1)} %get-tuple-element.64) | copy-start | bytes 1032196
  260.3 9.7 %copy-start = (f32[192,896]{1,0:T(8,128)S(1)}, f32[192,896]{1,0:T(8,128)}, u32[]{:S(2)}) copy-start(f32[192,896]{1,0:T(8,128)} %get-tuple-element.85) | copy-start | bytes 2064388
